TPU v7x, 32 devices: a whole 2x2x4 slice. The times are simulated.
32 devices in a mesh: depth: 4 (over x, core), height: 4 (over z), filt: 2 (over y).
Axes of the slice: x: 2, y: 2, z: 4, core: 2. Of those that a mesh axis runs over, the one named last changes fastest.
Arguments:
- volume: bfloat16 [16, 16, 64, 256], P('depth', 'height', None, 'filt'), may hold values from -6 to 6
- kernel_one: bfloat16 [3, 3, 3, 256, 256], replicated, may hold values from -0.078125 to 0.078125
- bias_one: float32 [256], replicated, may hold values from -3 to 3
- kernel_two: bfloat16 [3, 3, 3, 256, 256], replicated, may hold values from -0.078125 to 0.078125
- bias_two: float32 [256], replicated, may hold values from -3 to 3
Outputs:
- features: bfloat16 [16, 16, 64, 256], P('depth', 'height', None, 'filt')
All inputs are finite; a program needn't handle non-finite values.
Results may differ from a plain program's by a relative error of at most 0.0044.
Values may be sent and summed in bfloat16 or wider, within the bound.
No kernel may reach another device: no remote copies, remote signals or barrier semaphores. Data moves between devices by JAX's collectives and lax.ppermute only.
A program may use at most 64 MiB of HBM per device.

v0:
```python
import jax
import jax.numpy as jnp
from jax import lax
from jax.sharding import PartitionSpec as P


def extended(x, sides, width):
    for axis, dim in sides:
        peers, length = (lax.axis_size(axis), x.shape[dim])
        up = [(i, (i + 1) % peers) for i in range(peers - 1)]
        down = [(j, i) for i, j in up]
        last = lax.slice_in_dim(x, length - width, length, axis=dim)
        initial = lax.slice_in_dim(x, 0, width, axis=dim)
        before = lax.ppermute(last, axis, up)
        after = lax.ppermute(initial, axis, down)
        x = jnp.concatenate([before, x, after], axis=dim)
    return x


def leaky(value):
    return jnp.where(value > 0, value, 0.3 * value)


def convolve(padded, kernel, width_pad):
    out = lax.conv_general_dilated(
        padded[None],
        kernel,
        (1, 1, 1),
        [(0, 0), (0, 0), (width_pad, width_pad)],
        dimension_numbers=("NDHWC", "DHWIO", "NDHWC"),
        preferred_element_type=jnp.float32,
    )
    return out[0]


def body(volume, kernel_one, bias_one, kernel_two, bias_two):
    shard = volume.shape[3]
    offset = lax.axis_index("filt") * shard
    whole = lax.all_gather(volume, "filt", axis=3, tiled=True)
    padded = extended(whole, (("depth", 0), ("height", 1)), 1)
    kernel_own = lax.dynamic_slice_in_dim(kernel_one, offset, shard, 4)
    bias_own = lax.dynamic_slice_in_dim(bias_one, offset, shard, 0)
    hidden = leaky(convolve(padded, kernel_own, 1) + bias_own).astype(jnp.bfloat16)
    bias_last = lax.dynamic_slice_in_dim(bias_two, offset, shard, 0)
    hidden_whole = lax.all_gather(hidden, "filt", axis=3, tiled=True)
    hidden_padded = extended(hidden_whole, (("depth", 0), ("height", 1)), 1)
    kernel_last = lax.dynamic_slice_in_dim(kernel_two, offset, shard, 4)
    summed = convolve(hidden_padded, kernel_last, 1)
    return leaky(summed + bias_last).astype(jnp.bfloat16)


def solution(mesh):
    in_specs = (P("depth", "height", None, "filt"), P(), P(), P(), P())
    out_specs = P("depth", "height", None, "filt")
    return jax.shard_map(body, mesh=mesh, in_specs=in_specs, out_specs=out_specs, check_vma=False)
```

profile of v0, /device:TPU:1, one launch (start us, length us, event | category | flops | bytes accessed | tf_op | source)
XLA Modules:
  0.0 79.6 jit_solution(6441605663436722148)
XLA Ops:
  0.0 0.0 copy-start
  0.0 9.1 %all_gather.6 = bf16[4,4,64,256]{3,2,1,0:T(8,128)(2,1)S(1)} all-gather(bf16[4,4,64,128]{3,2,1,0:T(8,128)(2,1)} %param.5), channel_id=1, replica_groups=mesh['depth'=4,'height'=4,'filt'=2] {'filt'}, dimensions={3}, use_global_device_ids=true | all-gather | bytes 786432 | tf_op jit(solution)/shard_map/all_gather | solution.py:39
  9.1 0.0 copy-start.3
  9.2 4.4 %collective-permute-start = (bf16[1,4,64,256]{3,2,1,0:T(8,128)(2,1)S(1)}, bf16[1,4,64,256]{3,2,1,0:T(8,128)(2,1)S(1)}, u32[]{:S(2)}, u32[]{:S(2)}) collective-permute-start(bf16[1,4,64,256]{3,2,1,0:T(8,128)(2,1)S(1)} %get-tuple-element.12), channel_id=1, source_target_pairs={{0,8},{8,16},{16,24},{1,9},{9,17},{17,25},{2,10},{10,18},{18,26},{... | collective-permute-start | bytes 393224 | tf_op jit(solution)/shard_map/ppermute | solution.py:14
  13.6 1.9 %collective-permute-start.1 = (bf16[1,4,64,256]{3,2,1,0:T(8,128)(2,1)S(1)}, bf16[1,4,64,256]{3,2,1,0:T(8,128)(2,1)S(1)}, u32[]{:S(2)}, u32[]{:S(2)}) collective-permute-start(bf16[1,4,64,256]{3,2,1,0:T(8,128)(2,1)S(1)} %get-tuple-element.11), channel_id=1, source_target_pairs={{8,0},{16,8},{24,16},{9,1},{17,9},{25,17},{10,2},{18,10},{26,18},{... | collective-permute-start | bytes 393224 | tf_op jit(solution)/shard_map/ppermute | solution.py:15
  15.5 0.0 collective-permute-done
  15.6 4.3 %collective-permute-done.1 = bf16[1,4,64,256]{3,2,1,0:T(8,128)(2,1)S(1)} collective-permute-done((bf16[1,4,64,256]{3,2,1,0:T(8,128)(2,1)S(1)}, bf16[1,4,64,256]{3,2,1,0:T(8,128)(2,1)S(1)}, u32[]{:S(2)}, u32[]{:S(2)}) %collective-permute-start.1) | collective-permute-done | bytes 131104 | tf_op jit(solution)/shard_map/ppermute | solution.py:15
  19.9 0.0 copy-start.1
  19.9 0.9 %copy-done.1 = bf16[6,4,64,256]{3,2,1,0:T(8,128)(2,1)} copy-done((bf16[6,4,64,256]{3,2,1,0:T(8,128)(2,1)}, bf16[6,4,64,256]{3,2,1,0:T(8,128)(2,1)S(1)}, u32[]{:S(2)}) %copy-start.1) | copy-done | bytes 786456
  20.8 0.8 fusion.43
  21.6 3.9 %collective-permute-start.2 = (bf16[6,1,64,256]{3,2,1,0:T(8,128)(2,1)}, bf16[6,1,64,256]{3,2,1,0:T(8,128)(2,1)}, u32[]{:S(2)}, u32[]{:S(2)}) collective-permute-start(bf16[6,1,64,256]{3,2,1,0:T(8,128)(2,1)} %get-tuple-element.7), channel_id=1, source_target_pairs={{0,2},{2,4},{4,6},{1,3},{3,5},{5,7},{8,10},{10,12},{12,14},{9,11},... | collective-permute-start | bytes 589832 | tf_op jit(solution)/shard_map/ppermute | solution.py:14
  25.4 1.3 %collective-permute-start.3 = (bf16[6,1,64,256]{3,2,1,0:T(8,128)(2,1)}, bf16[6,1,64,256]{3,2,1,0:T(8,128)(2,1)}, u32[]{:S(2)}, u32[]{:S(2)}) collective-permute-start(bf16[6,1,64,256]{3,2,1,0:T(8,128)(2,1)} %get-tuple-element.8), channel_id=1, source_target_pairs={{2,0},{4,2},{6,4},{3,1},{5,3},{7,5},{10,8},{12,10},{14,12},{11,9},... | collective-permute-start | bytes 589832 | tf_op jit(solution)/shard_map/ppermute | solution.py:15
  26.7 0.0 copy-done.3
  26.8 0.1 dynamic_slice.13
  26.8 0.9 %collective-permute-done.2 = bf16[6,1,64,256]{3,2,1,0:T(8,128)(2,1)} collective-permute-done((bf16[6,1,64,256]{3,2,1,0:T(8,128)(2,1)}, bf16[6,1,64,256]{3,2,1,0:T(8,128)(2,1)}, u32[]{:S(2)}, u32[]{:S(2)}) %collective-permute-start.2) | collective-permute-done | bytes 196640 | tf_op jit(solution)/shard_map/ppermute | solution.py:14
  27.7 4.5 %collective-permute-done.3 = bf16[6,1,64,256]{3,2,1,0:T(8,128)(2,1)} collective-permute-done((bf16[6,1,64,256]{3,2,1,0:T(8,128)(2,1)}, bf16[6,1,64,256]{3,2,1,0:T(8,128)(2,1)}, u32[]{:S(2)}, u32[]{:S(2)}) %collective-permute-start.3) | collective-permute-done | bytes 196640 | tf_op jit(solution)/shard_map/ppermute | solution.py:15
  32.2 1.4 %maximum_bitcast_fusion.1 = bf16[6,6,1,64,256]{4,3,1,0,2:T(8,128)(2,1)S(1)} fusion(bf16[6,1,64,256]{3,2,1,0:T(8,128)(2,1)} %collective-permute-done.3, bf16[6,4,64,256]{3,2,1,0:T(8,128)(2,1)} %copy-done.1, bf16[6,1,64,256]{3,2,1,0:T(8,128)(2,1)} %collective-permute-done.2), kind=kLoop, calls=%fused_computation.22 | loop fusion | flops 1179648 | bytes 2359296 | tf_op jit(solution)/shard_map/broadcast_in_dim | solution.py:26
  33.6 0.8 copy.14
  34.3 0.3 pad.clone
  34.7 0.0 copy-start.5
  34.7 0.3 copy.8
  35.0 0.1 slice.40
  35.0 0.0 copy-done
  35.0 0.3 copy-done.5
  35.4 4.3 %fusion.18 = f32[4,4,8,9,128]{4,2,3,1,0:T(8,128)S(1)} fusion(bf16[3,3,3,256,256]{4,3,2,1,0:T(8,128)(2,1)S(1)} %copy-done, s32[]{:T(128)S(6)} %select_n.13, bf16[6,6,1,7,2,256]{5,3,4,1,0,2:T(8,128)(2,1)S(1)} %slice.40, bf16[6,6,1,8,9,256]{5,3,4,1,0,2:T(8,128)(2,1)S(1)} %copy.8, pred[8,9]{0,1:T(8,128)(4,1)S(1)} %copy-done.5), kind=kOutput, calls=%fused_computation.20 | convolution fusion | flops 2043445248 | bytes 3983364 | tf_op jit(solution)/shard_map/conv_general_dilated | solution.py:25
  39.7 0.2 copy.9
  39.9 0.2 fusion.30
  40.1 7.6 %all_gather.7 = bf16[4,4,64,256]{3,1,2,0:T(4,128)(2,1)S(1)} all-gather(bf16[4,4,64,128]{3,1,2,0:T(4,128)(2,1)S(1)} %fusion.30), channel_id=1, replica_groups=mesh['depth'=4,'height'=4,'filt'=2] {'filt'}, dimensions={3}, use_global_device_ids=true | all-gather | bytes 786432 | tf_op jit(solution)/shard_map/all_gather | solution.py:45
  47.6 0.1 fusion.44
  47.7 0.0 copy-start.4
  47.7 2.7 %collective-permute-start.4 = (bf16[1,4,64,256]{3,1,2,0:T(4,128)(2,1)S(1)}, bf16[1,4,64,256]{3,1,2,0:T(4,128)(2,1)S(1)}, u32[]{:S(2)}, u32[]{:S(2)}) collective-permute-start(bf16[1,4,64,256]{3,1,2,0:T(4,128)(2,1)S(1)} %get-tuple-element.10), channel_id=1, source_target_pairs={{0,8},{8,16},{16,24},{1,9},{9,17},{17,25},{2,10},{10,18},{18,26},{... | collective-permute-start | bytes 393224 | tf_op jit(solution)/shard_map/ppermute | solution.py:14
  50.4 1.9 %collective-permute-start.5 = (bf16[1,4,64,256]{3,1,2,0:T(4,128)(2,1)S(1)}, bf16[1,4,64,256]{3,1,2,0:T(4,128)(2,1)S(1)}, u32[]{:S(2)}, u32[]{:S(2)}) collective-permute-start(bf16[1,4,64,256]{3,1,2,0:T(4,128)(2,1)S(1)} %get-tuple-element.9), channel_id=1, source_target_pairs={{8,0},{16,8},{24,16},{9,1},{17,9},{25,17},{10,2},{18,10},{26,18},{... | collective-permute-start | bytes 393224 | tf_op jit(solution)/shard_map/ppermute | solution.py:15
  52.4 0.0 collective-permute-done.4
  52.4 0.2 constant_dynamic-update-slice_fusion.4
  52.7 4.1 %collective-permute-done.5 = bf16[1,4,64,256]{3,1,2,0:T(4,128)(2,1)S(1)} collective-permute-done((bf16[1,4,64,256]{3,1,2,0:T(4,128)(2,1)S(1)}, bf16[1,4,64,256]{3,1,2,0:T(4,128)(2,1)S(1)}, u32[]{:S(2)}, u32[]{:S(2)}) %collective-permute-start.5) | collective-permute-done | bytes 131104 | tf_op jit(solution)/shard_map/ppermute | solution.py:15
  56.7 0.1 constant_dynamic-update-slice_fusion.3
  56.8 0.6 fusion.42
  57.4 2.6 %collective-permute-start.6 = (bf16[6,1,64,256]{3,1,2,0:T(2,128)(2,1)S(1)}, bf16[6,1,64,256]{3,1,2,0:T(2,128)(2,1)S(1)}, u32[]{:S(2)}, u32[]{:S(2)}) collective-permute-start(bf16[6,1,64,256]{3,1,2,0:T(2,128)(2,1)S(1)} %get-tuple-element.5), channel_id=1, source_target_pairs={{0,2},{2,4},{4,6},{1,3},{3,5},{5,7},{8,10},{10,12},{12,14},{9,11},... | collective-permute-start | bytes 589832 | tf_op jit(solution)/shard_map/ppermute | solution.py:14
  60.0 1.5 %collective-permute-start.7 = (bf16[6,1,64,256]{3,1,2,0:T(2,128)(2,1)S(1)}, bf16[6,1,64,256]{3,1,2,0:T(2,128)(2,1)S(1)}, u32[]{:S(2)}, u32[]{:S(2)}) collective-permute-start(bf16[6,1,64,256]{3,1,2,0:T(2,128)(2,1)S(1)} %get-tuple-element.6), channel_id=1, source_target_pairs={{2,0},{4,2},{6,4},{3,1},{5,3},{7,5},{10,8},{12,10},{14,12},{11,9},... | collective-permute-start | bytes 589832 | tf_op jit(solution)/shard_map/ppermute | solution.py:15
  61.5 0.0 copy-done.4
  61.5 0.1 dynamic_slice.15
  61.6 4.8 %collective-permute-done.6 = bf16[6,1,64,256]{3,1,2,0:T(2,128)(2,1)S(1)} collective-permute-done((bf16[6,1,64,256]{3,1,2,0:T(2,128)(2,1)S(1)}, bf16[6,1,64,256]{3,1,2,0:T(2,128)(2,1)S(1)}, u32[]{:S(2)}, u32[]{:S(2)}) %collective-permute-start.6) | collective-permute-done | bytes 196640 | tf_op jit(solution)/shard_map/ppermute | solution.py:14
  66.3 4.1 %collective-permute-done.7 = bf16[6,1,64,256]{3,1,2,0:T(2,128)(2,1)S(1)} collective-permute-done((bf16[6,1,64,256]{3,1,2,0:T(2,128)(2,1)S(1)}, bf16[6,1,64,256]{3,1,2,0:T(2,128)(2,1)S(1)}, u32[]{:S(2)}, u32[]{:S(2)}) %collective-permute-start.7) | collective-permute-done | bytes 196640 | tf_op jit(solution)/shard_map/ppermute | solution.py:15
  70.4 1.3 %maximum_bitcast_fusion = bf16[6,6,1,64,256]{4,1,3,0,2:T(8,128)(2,1)S(1)} fusion(bf16[6,1,64,256]{3,1,2,0:T(2,128)(2,1)S(1)} %collective-permute-done.7, bf16[6,4,64,256]{3,1,2,0:T(4,128)(2,1)S(1)} %constant_dynamic-update-slice_fusion.3, bf16[6,1,64,256]{3,1,2,0:T(2,128)(2,1)S(1)} %collective-permute-done.6), kind=kLoop, calls=%fused_computation.17 | loop fusion | flops 3538944 | bytes 2359296 | tf_op jit(solution)/shard_map/broadcast_in_dim | solution.py:26
  71.7 0.3 pad.2
  72.1 0.0 copy-start.2
  72.1 0.3 copy.11
  72.4 0.1 slice.46
  72.4 1.6 %copy-done.2 = bf16[3,3,3,256,256]{4,3,2,1,0:T(8,128)(2,1)S(1)} copy-done((bf16[3,3,3,256,256]{4,3,2,1,0:T(8,128)(2,1)S(1)}, bf16[3,3,3,256,256]{4,3,2,1,0:T(8,128)(2,1)}, u32[]{:S(2)}) %copy-start.2) | copy-done | bytes 3538968
  74.1 4.4 %fusion.23 = f32[4,4,8,9,128]{4,2,3,1,0:T(8,128)S(1)} fusion(bf16[3,3,3,256,256]{4,3,2,1,0:T(8,128)(2,1)S(1)} %copy-done.2, s32[]{:T(128)S(6)} %select_n.13, bf16[6,6,1,7,2,256]{5,3,4,1,0,2:T(8,128)(2,1)S(1)} %slice.46, bf16[6,6,1,8,9,256]{5,3,4,1,0,2:T(8,128)(2,1)S(1)} %copy.11, pred[8,9]{0,1:T(8,128)(4,1)S(1)} %copy-done.5), kind=kOutput, calls=%fused_computation.21 | convolution fusion | flops 2043445248 | bytes 3983364 | tf_op jit(solution)/shard_map/conv_general_dilated | solution.py:25
  78.5 0.2 copy.12
  78.6 0.2 fusion.31
  78.8 0.8 copy.13
  (5 shorter events, 0.1 us)
Async XLA Ops:
  0.0 35.0 %copy-start = (bf16[3,3,3,256,256]{4,3,2,1,0:T(8,128)(2,1)S(1)}, bf16[3,3,3,256,256]{4,3,2,1,0:T(8,128)(2,1)}, u32[]{:S(2)}) copy-start(bf16[3,3,3,256,256]{4,3,2,1,0:T(8,128)(2,1)} %param.6) | copy-start | bytes 10616836
  9.1 17.6 %copy-start.3 = (f32[256]{0:T(256)S(1)}, f32[256]{0:T(256)}, u32[]{:S(2)}) copy-start(f32[256]{0:T(256)} %param.7) | copy-start | bytes 3076
  9.2 6.4 %collective-permute-start = (bf16[1,4,64,256]{3,2,1,0:T(8,128)(2,1)S(1)}, bf16[1,4,64,256]{3,2,1,0:T(8,128)(2,1)S(1)}, u32[]{:S(2)}, u32[]{:S(2)}) collective-permute-start(bf16[1,4,64,256]{3,2,1,0:T(8,128)(2,1)S(1)} %get-tuple-element.12), channel_id=1, source_target_pairs={{0,8},{8,16},{16,24},{1,9},{9,17},{17,25},{2,10},{10,18},{18,26},{... | collective-permute-start | bytes 393224 | tf_op jit(solution)/shard_map/ppermute | solution.py:14
  13.6 6.3 %collective-permute-start.1 = (bf16[1,4,64,256]{3,2,1,0:T(8,128)(2,1)S(1)}, bf16[1,4,64,256]{3,2,1,0:T(8,128)(2,1)S(1)}, u32[]{:S(2)}, u32[]{:S(2)}) collective-permute-start(bf16[1,4,64,256]{3,2,1,0:T(8,128)(2,1)S(1)} %get-tuple-element.11), channel_id=1, source_target_pairs={{8,0},{16,8},{24,16},{9,1},{17,9},{25,17},{10,2},{18,10},{26,18},{... | collective-permute-start | bytes 393224 | tf_op jit(solution)/shard_map/ppermute | solution.py:15
  19.9 0.9 %copy-start.1 = (bf16[6,4,64,256]{3,2,1,0:T(8,128)(2,1)}, bf16[6,4,64,256]{3,2,1,0:T(8,128)(2,1)S(1)}, u32[]{:S(2)}) copy-start(bf16[6,4,64,256]{3,2,1,0:T(8,128)(2,1)S(1)} %constant_dynamic-update-slice_fusion) | copy-start | bytes 2359300
  21.6 6.1 %collective-permute-start.2 = (bf16[6,1,64,256]{3,2,1,0:T(8,128)(2,1)}, bf16[6,1,64,256]{3,2,1,0:T(8,128)(2,1)}, u32[]{:S(2)}, u32[]{:S(2)}) collective-permute-start(bf16[6,1,64,256]{3,2,1,0:T(8,128)(2,1)} %get-tuple-element.7), channel_id=1, source_target_pairs={{0,2},{2,4},{4,6},{1,3},{3,5},{5,7},{8,10},{10,12},{12,14},{9,11},... | collective-permute-start | bytes 589832 | tf_op jit(solution)/shard_map/ppermute | solution.py:14
  25.4 6.7 %collective-permute-start.3 = (bf16[6,1,64,256]{3,2,1,0:T(8,128)(2,1)}, bf16[6,1,64,256]{3,2,1,0:T(8,128)(2,1)}, u32[]{:S(2)}, u32[]{:S(2)}) collective-permute-start(bf16[6,1,64,256]{3,2,1,0:T(8,128)(2,1)} %get-tuple-element.8), channel_id=1, source_target_pairs={{2,0},{4,2},{6,4},{3,1},{5,3},{7,5},{10,8},{12,10},{14,12},{11,9},... | collective-permute-start | bytes 589832 | tf_op jit(solution)/shard_map/ppermute | solution.py:15
  34.7 0.7 copy-start.5
  47.7 13.8 %copy-start.4 = (f32[256]{0:T(256)S(1)}, f32[256]{0:T(256)}, u32[]{:S(2)}) copy-start(f32[256]{0:T(256)} %param.9) | copy-start | bytes 3076
  47.7 4.6 %collective-permute-start.4 = (bf16[1,4,64,256]{3,1,2,0:T(4,128)(2,1)S(1)}, bf16[1,4,64,256]{3,1,2,0:T(4,128)(2,1)S(1)}, u32[]{:S(2)}, u32[]{:S(2)}) collective-permute-start(bf16[1,4,64,256]{3,1,2,0:T(4,128)(2,1)S(1)} %get-tuple-element.10), channel_id=1, source_target_pairs={{0,8},{8,16},{16,24},{1,9},{9,17},{17,25},{2,10},{10,18},{18,26},{... | collective-permute-start | bytes 393224 | tf_op jit(solution)/shard_map/ppermute | solution.py:14
  50.4 6.3 %collective-permute-start.5 = (bf16[1,4,64,256]{3,1,2,0:T(4,128)(2,1)S(1)}, bf16[1,4,64,256]{3,1,2,0:T(4,128)(2,1)S(1)}, u32[]{:S(2)}, u32[]{:S(2)}) collective-permute-start(bf16[1,4,64,256]{3,1,2,0:T(4,128)(2,1)S(1)} %get-tuple-element.9), channel_id=1, source_target_pairs={{8,0},{16,8},{24,16},{9,1},{17,9},{25,17},{10,2},{18,10},{26,18},{... | collective-permute-start | bytes 393224 | tf_op jit(solution)/shard_map/ppermute | solution.py:15
  57.4 8.9 %collective-permute-start.6 = (bf16[6,1,64,256]{3,1,2,0:T(2,128)(2,1)S(1)}, bf16[6,1,64,256]{3,1,2,0:T(2,128)(2,1)S(1)}, u32[]{:S(2)}, u32[]{:S(2)}) collective-permute-start(bf16[6,1,64,256]{3,1,2,0:T(2,128)(2,1)S(1)} %get-tuple-element.5), channel_id=1, source_target_pairs={{0,2},{2,4},{4,6},{1,3},{3,5},{5,7},{8,10},{10,12},{12,14},{9,11},... | collective-permute-start | bytes 589832 | tf_op jit(solution)/shard_map/ppermute | solution.py:14
  60.0 10.4 %collective-permute-start.7 = (bf16[6,1,64,256]{3,1,2,0:T(2,128)(2,1)S(1)}, bf16[6,1,64,256]{3,1,2,0:T(2,128)(2,1)S(1)}, u32[]{:S(2)}, u32[]{:S(2)}) collective-permute-start(bf16[6,1,64,256]{3,1,2,0:T(2,128)(2,1)S(1)} %get-tuple-element.6), channel_id=1, source_target_pairs={{2,0},{4,2},{6,4},{3,1},{5,3},{7,5},{10,8},{12,10},{14,12},{11,9},... | collective-permute-start | bytes 589832 | tf_op jit(solution)/shard_map/ppermute | solution.py:15
  72.1 2.0 %copy-start.2 = (bf16[3,3,3,256,256]{4,3,2,1,0:T(8,128)(2,1)S(1)}, bf16[3,3,3,256,256]{4,3,2,1,0:T(8,128)(2,1)}, u32[]{:S(2)}) copy-start(bf16[3,3,3,256,256]{4,3,2,1,0:T(8,128)(2,1)} %param.8) | copy-start | bytes 10616836
where the time goes:
time: 79.9 us; the launch traced here: 79.6 us
  waiting for transfers between devices  22.6 us (28%)
  starting transfers between devices  20.2 us (25%)
  blocking collectives  16.7 us (21%)
  matrix products  8.71 us (11%)
  local copies, waits for them, and re-layouts  8.09 us (10%)
  other arithmetic  3.06 us (4%)
    ppermute x4, waiting for transfers between devices, extended(): after = lax.ppermute(initial, axis, down)  17 us
    ppermute x4, starting transfers between devices, extended(): before = lax.ppermute(last, axis, up)  13.6 us
    all_gather x1, blocking collectives, body(): whole = lax.all_gather(volume, 'filt', axis=3, tiled=True)  9.14 us
    conv_general_dilated x2, matrix products, convolve(): lax.conv_general_dilated(padded[None], kernel, (1, 1, 1), [(0, 0), (0, 0)...  8.71 us
    all_gather x1, blocking collectives, body(): hidden_whole = lax.all_gather(hidden, 'filt', axis=3, tiled=True)  7.56 us
    ppermute x4, starting transfers between devices, extended(): after = lax.ppermute(initial, axis, down)  6.59 us
    ppermute x4, waiting for transfers between devices, extended(): before = lax.ppermute(last, axis, up)  5.61 us
    unnamed x17, local copies, waits for them, and re-layouts  3.95 us
  transfers between devices with their start and end apart: 8, of which 6 were waited for; matrix products, arithmetic and copies ran while one was open for 1% of the time, Pallas kernels for 0%

commit v1 on v0

v1 whole, which is shorter than its diff:
```python
import functools

import jax
import jax.numpy as jnp
from jax import lax
from jax.experimental import pallas as pl
from jax.experimental.pallas import tpu as pltpu
from jax.sharding import PartitionSpec as P


def leaky(value):
    return jnp.where(value > 0, value, 0.3 * value)


def exchange(first, last, axis):
    peers, index = lax.axis_size(axis), lax.axis_index(axis)
    odd = index % 2 == 1
    pairs = [(i, i + 1) for i in range(0, peers - 1, 2)]
    evens = [(i, i) for i in range(peers) if peers % 2 == 1 and i == peers - 1]
    gaps = [(i, i + 1) for i in range(1, peers - 1, 2)]
    rest = [(i, i) for i in range(peers) if i == 0 or (peers % 2 == 0 and i == peers - 1)]
    both = lambda p, own: p + [(j, i) for i, j in p] + own
    one = lax.ppermute(jnp.where(odd, first, last), axis, both(pairs, evens))
    two = lax.ppermute(jnp.where(odd, last, first), axis, both(gaps, rest))
    before = jnp.where(odd, one, two)
    after = jnp.where(odd, two, one)
    before = jnp.where(index == 0, jnp.zeros_like(before), before)
    after = jnp.where(index == peers - 1, jnp.zeros_like(after), after)
    return before, after


def to_columns(x, axis):
    peers, index = lax.axis_size(axis), lax.axis_index(axis)
    own = x.shape[2] // peers
    padded = jnp.pad(x, ((0, 0), (0, 0), (2, 2), (0, 0)))
    parts = [lax.dynamic_slice_in_dim(padded, index * own, own + 4, 2)]
    for s in range(1, peers):
        dest = (index + s) % peers
        part = lax.dynamic_slice_in_dim(padded, dest * own, own + 4, 2)
        parts.append(lax.ppermute(part, axis, [(i, (i + s) % peers) for i in range(peers)]))
    if peers == 2:
        return jnp.where(index == 0, jnp.concatenate(parts, 3), jnp.concatenate(parts[::-1], 3))
    stacked = jnp.stack(parts)
    order = (index - jnp.arange(peers)) % peers
    return jnp.concatenate([stacked[order[c]] for c in range(peers)], 3)


def to_channels(y, axis):
    peers, index = lax.axis_size(axis), lax.axis_index(axis)
    shard, own = y.shape[3] // peers, y.shape[2]
    parts = [lax.dynamic_slice_in_dim(y, index * shard, shard, 3)]
    for s in range(1, peers):
        dest = (index + s) % peers
        part = lax.dynamic_slice_in_dim(y, dest * shard, shard, 3)
        parts.append(lax.ppermute(part, axis, [(i, (i + s) % peers) for i in range(peers)]))
    if peers == 2:
        return jnp.where(index == 0, jnp.concatenate(parts, 2), jnp.concatenate(parts[::-1], 2))
    stacked = jnp.stack(parts)
    order = (index - jnp.arange(peers)) % peers
    return jnp.concatenate([stacked[order[c]] for c in range(peers)], 2)


def conv_kernel(sides, edges, xb, xc, xa, k1, b1, k2, b2, o_ref, x3, ef, e3, eb, h3):
    C = xc.shape[3]
    D, H, Wp = xc.shape[0], xc.shape[1], xc.shape[2]
    own = Wp - 4
    D2, H2, D1, H1, H0 = D + 4, H, D + 2, H - 2, H - 4
    index, peers = edges[4], edges[5]
    rows = [xb.at[d] for d in range(2)] + [xc.at[d] for d in range(D)] + [xa.at[d] for d in range(2)]
    for d in range(D2):
        x = rows[d][...]
        for c in range(3):
            x3[d, :, :, c * C:(c + 1) * C] = x[:, 1 + c:1 + c + own, :]
        for s in range(sides):
            low, high = x[:, 0:3, :], x[:, Wp - 3:Wp, :]
            if sides == 1:
                pick = jnp.where(index == 0, high, low)
            else:
                pick = low if s == 0 else high
            pick = pick.astype(jnp.float32)
            for l in range(0, C, 128):
                for h in range(H2):
                    ef[s, l // 128, pl.ds((d * H2 + h) * 8, 3), :] = pick[h, :, l:l + 128]
                for c in range(3):
                    e3[s, d, 0:H2, c * C + l:c * C + l + 128] = ef[s, l // 128, pl.ds(d * H2 * 8 + c, H2, stride=8), :]
            for b in range(3):
                eb[s, b, d] = e3[s, d, b:b + H2, :].astype(jnp.bfloat16)

    bias1 = b1[...]
    for d in range(0, D1, 2):
        main = 2 * H1 * own
        acc = jnp.zeros((main + sides * 2 * H2, C), jnp.float32)
        for a in range(3):
            for b in range(3):
                lhs = [x3[d + a:d + a + 2, b:b + H1].reshape(main, 3 * C)]
                lhs += [eb[s, b, d + a:d + a + 2].reshape(2 * H2, 3 * C) for s in range(sides)]
                acc += jnp.dot(jnp.concatenate(lhs, 0), k1[a, b].reshape(3 * C, C), preferred_element_type=jnp.float32)
        acc = leaky(acc + bias1)
        for q in range(2):
            hid = acc[q * H1 * own:(q + 1) * H1 * own].reshape(H1, own, C)
            ends = [acc[main + (s * 2 + q) * H2:main + (s * 2 + q + 1) * H2] for s in range(sides)]
            inside = True
            if d + q == 0:
                inside = edges[0] == 0
            if d + q == D1 - 1:
                inside = edges[1] == 0
            for h in range(H1):
                row = hid[h]
                ok = inside
                if h == 0:
                    ok = jnp.logical_and(ok, edges[2] == 0)
                if h == H1 - 1:
                    ok = jnp.logical_and(ok, edges[3] == 0)
                if ok is not True:
                    row = jnp.where(ok, row, 0.0)
                none = jnp.zeros((1, C), jnp.float32)
                if sides == 1:
                    end = ends[0][h:h + 1]
                    left = jnp.where(index == 0, none, end)
                    right = jnp.where(index == 0, end, none)
                else:
                    left = jnp.where(index == 0, none, ends[0][h:h + 1])
                    right = jnp.where(index == peers - 1, none, ends[1][h:h + 1])
                if ok is not True:
                    left, right = jnp.where(ok, left, 0.0), jnp.where(ok, right, 0.0)
                column = lax.broadcasted_iota(jnp.int32, (own, C), 0)
                h3[d + q, h, :, 0:C] = jnp.where(column == 0, left, pltpu.roll(row, 1, 0)).astype(jnp.bfloat16)
                h3[d + q, h, :, C:2 * C] = row.astype(jnp.bfloat16)
                h3[d + q, h, :, 2 * C:] = jnp.where(column == own - 1, right, pltpu.roll(row, own - 1, 0)).astype(jnp.bfloat16)

    bias2 = b2[...]
    for d in range(0, D, 2):
        acc = jnp.zeros((2 * H0 * own, C), jnp.float32)
        for a in range(3):
            for b in range(3):
                acc += jnp.dot(h3[d + a:d + a + 2, b:b + H0].reshape(2 * H0 * own, 3 * C), k2[a, b].reshape(3 * C, C), preferred_element_type=jnp.float32)
        o_ref[d:d + 2] = leaky(acc + bias2).astype(jnp.bfloat16).reshape(2, H0, own, C)


def convolutions(xb, xc, xa, k1, b1, k2, b2):
    D, H, Wp, C = xc.shape
    own = Wp - 4
    d, h, f = (lax.axis_index(a) for a in ("depth", "height", "filt"))
    nd, nh, nf = (lax.axis_size(a) for a in ("depth", "height", "filt"))
    edges = jnp.stack([d == 0, d == nd - 1, h == 0, h == nh - 1, f, jnp.int32(nf)]).astype(jnp.int32)
    sides = 1 if nf == 2 else 2
    vmem = pl.BlockSpec(memory_space=pltpu.VMEM)
    return pl.pallas_call(
        functools.partial(conv_kernel, sides),
        out_shape=jax.ShapeDtypeStruct((D, H - 4, own, C), jnp.bfloat16),
        in_specs=[pl.BlockSpec(memory_space=pltpu.SMEM)] + [vmem] * 7,
        out_specs=vmem,
        scratch_shapes=[
            pltpu.VMEM((D + 4, H, own, 3 * C), jnp.bfloat16),
            pltpu.VMEM((sides, C // 128, (D + 4) * H * 8, 128), jnp.float32),
            pltpu.VMEM((sides, D + 4, 2 * H, 3 * C), jnp.float32),
            pltpu.VMEM((sides, 3, D + 4, H, 3 * C), jnp.bfloat16),
            pltpu.VMEM((D + 2, H - 2, own, 3 * C), jnp.bfloat16),
        ],
        compiler_params=pltpu.CompilerParams(vmem_limit_bytes=40 * 2**20),
        cost_estimate=pl.CostEstimate(flops=2 * 27 * C * C * own * ((D + 2) * (H - 2) + D * (H - 4)), bytes_accessed=8 * 2**20, transcendentals=0),
    )(edges, xb, xc, xa, k1, b1, k2, b2)


def body(volume, kernel_one, bias_one, kernel_two, bias_two):
    whole = to_columns(volume, "filt")
    before, after = exchange(whole[:, :2], whole[:, -2:], "height")
    tall = jnp.concatenate([before, whole, after], 1)
    front, back = exchange(tall[:2], tall[-2:], "depth")
    out = convolutions(front, tall, back, kernel_one, bias_one.reshape(1, -1), kernel_two, bias_two.reshape(1, -1))
    return to_channels(out, "filt")


def solution(mesh):
    in_specs = (P("depth", "height", None, "filt"), P(), P(), P(), P())
    out_specs = P("depth", "height", None, "filt")
    return jax.shard_map(body, mesh=mesh, in_specs=in_specs, out_specs=out_specs, check_vma=False)
```

time: 79.9 us -> 43.4 us (0.54)
  the two profiles are of different devices: /device:TPU:1 before, /device:TPU:18 now
where the time goes in v1:
time: 43.4 us; the launch traced here: 43.2 us
  waiting for transfers between devices  19.4 us (45%)
  starting transfers between devices  8.7 us (20%)
  Pallas kernels  8.45 us (19%)
  local copies, waits for them, and re-layouts  5.31 us (12%)
  other arithmetic  1.16 us (3%)
    ppermute x2, waiting for transfers between devices, exchange(): two = lax.ppermute(jnp.where(odd, last, first), axis, both(gaps, rest))  9.73 us
    pallas_call x1, Pallas kernels, convolutions(): pl.pallas_call(functools.partial(conv_kernel, sides), out_shape=jax.Shape...  8.45 us
    ppermute x1, waiting for transfers between devices, to_columns(): lax.ppermute(part, axis, [(i, (i + s) % peers) for i in range(peers)])  4.43 us
    unnamed x8, local copies, waits for them, and re-layouts  4 us
    ppermute x2, starting transfers between devices, exchange(): two = lax.ppermute(jnp.where(odd, last, first), axis, both(gaps, rest))  3.83 us
    ppermute x1, waiting for transfers between devices, to_channels(): lax.ppermute(part, axis, [(i, (i + s) % peers) for i in range(peers)])  3.45 us
    ppermute x2, waiting for transfers between devices, exchange(): one = lax.ppermute(jnp.where(odd, first, last), axis, both(pairs, evens))  1.81 us
    ppermute x2, starting transfers between devices, exchange(): one = lax.ppermute(jnp.where(odd, first, last), axis, both(pairs, evens))  1.71 us
  transfers between devices with their start and end apart: 6, of which 5 were waited for; matrix products, arithmetic and copies ran while one was open for 0% of the time, Pallas kernels for 0%

profile of v1, /device:TPU:18, one launch (start us, length us, event | category | flops | bytes accessed | tf_op | source)
XLA Modules:
  0.0 43.2 jit_solution(3255764661103103715)
XLA Ops:
  0.0 0.0 copy-start.3
  0.0 0.0 copy-start.2
  0.0 1.2 %pad_dynamic-slice_fusion.1 = (bf16[4,4,36,128]{3,2,1,0:T(8,128)(2,1)S(1)}, bf16[4,4,36,128]{3,2,1,0:T(8,128)(2,1)S(1)}) fusion(s32[]{:T(128)S(6)} %select_n.117, bf16[4,4,64,128]{3,2,1,0:T(8,128)(2,1)} %param.5, s32[]{:T(128)S(6)} %select_n.119), kind=kLoop, calls=%fused_computation.7 | loop fusion | bytes 557064 | tf_op jit(solution)/shard_map/dynamic_slice | solution.py:36
  1.2 1.6 %collective-permute-start = (bf16[4,4,36,128]{3,2,1,0:T(8,128)(2,1)S(1)}, bf16[4,4,36,128]{3,2,1,0:T(8,128)(2,1)S(1)}, u32[]{:S(2)}, u32[]{:S(2)}) collective-permute-start(bf16[4,4,36,128]{3,2,1,0:T(8,128)(2,1)S(1)} %get-tuple-element.16), channel_id=1, source_target_pairs={{0,1},{1,0},{2,3},{3,2},{4,5},{5,4},{6,7},{7,6},{8,9},{9,8},{10,11... | collective-permute-start | bytes 442376 | tf_op jit(solution)/shard_map/ppermute | solution.py:40
  2.7 4.4 %collective-permute-done = bf16[4,4,36,128]{3,2,1,0:T(8,128)(2,1)S(1)} collective-permute-done((bf16[4,4,36,128]{3,2,1,0:T(8,128)(2,1)S(1)}, bf16[4,4,36,128]{3,2,1,0:T(8,128)(2,1)S(1)}, u32[]{:S(2)}, u32[]{:S(2)}) %collective-permute-start) | collective-permute-done | bytes 147488 | tf_op jit(solution)/shard_map/ppermute | solution.py:40
  7.2 0.1 maximum_select_fusion
  7.3 1.6 %collective-permute-start.1 = (bf16[4,2,36,256]{3,2,1,0:T(8,128)(2,1)S(1)}, bf16[4,2,36,256]{3,2,1,0:T(8,128)(2,1)S(1)}, u32[]{:S(2)}, u32[]{:S(2)}) collective-permute-start(bf16[4,2,36,256]{3,2,1,0:T(8,128)(2,1)S(1)} %get-tuple-element.11), channel_id=1, source_target_pairs={{0,2},{4,6},{2,0},{6,4},{1,3},{5,7},{3,1},{7,5},{8,10},{12,14},{10... | collective-permute-start | bytes 442376 | tf_op jit(solution)/shard_map/ppermute | solution.py:23
  9.0 1.9 %collective-permute-start.2 = (bf16[4,2,36,256]{3,2,1,0:T(8,128)(2,1)S(1)}, bf16[4,2,36,256]{3,2,1,0:T(8,128)(2,1)S(1)}, u32[]{:S(2)}, u32[]{:S(2)}) collective-permute-start(bf16[4,2,36,256]{3,2,1,0:T(8,128)(2,1)S(1)} %get-tuple-element.12), channel_id=1, source_target_pairs={{2,4},{4,2},{0,0},{6,6},{3,5},{5,3},{1,1},{7,7},{10,12},{12,10},{8... | collective-permute-start | bytes 442376 | tf_op jit(solution)/shard_map/ppermute | solution.py:24
  10.9 1.8 %collective-permute-done.1 = bf16[4,2,36,256]{3,2,1,0:T(8,128)(2,1)S(1)} collective-permute-done((bf16[4,2,36,256]{3,2,1,0:T(8,128)(2,1)S(1)}, bf16[4,2,36,256]{3,2,1,0:T(8,128)(2,1)S(1)}, u32[]{:S(2)}, u32[]{:S(2)}) %collective-permute-start.1) | collective-permute-done | bytes 147488 | tf_op jit(solution)/shard_map/ppermute | solution.py:23
  12.7 3.5 %collective-permute-done.2 = bf16[4,2,36,256]{3,2,1,0:T(8,128)(2,1)S(1)} collective-permute-done((bf16[4,2,36,256]{3,2,1,0:T(8,128)(2,1)S(1)}, bf16[4,2,36,256]{3,2,1,0:T(8,128)(2,1)S(1)}, u32[]{:S(2)}, u32[]{:S(2)}) %collective-permute-start.2) | collective-permute-done | bytes 147488 | tf_op jit(solution)/shard_map/ppermute | solution.py:24
  16.2 0.1 pad_maximum_fusion.xc
  16.3 1.9 %collective-permute-start.4 = (bf16[2,8,36,256]{3,2,1,0:T(8,128)(2,1)S(1)}, bf16[2,8,36,256]{3,2,1,0:T(8,128)(2,1)S(1)}, u32[]{:S(2)}, u32[]{:S(2)}) collective-permute-start(bf16[2,8,36,256]{3,2,1,0:T(8,128)(2,1)S(1)} %get-tuple-element.7), channel_id=1, source_target_pairs={{8,16},{16,8},{0,0},{24,24},{9,17},{17,9},{1,1},{25,25},{10,18},{1... | collective-permute-start | bytes 884744 | tf_op jit(solution)/shard_map/ppermute | solution.py:24
  18.3 0.1 collective-permute-start.3
  18.4 0.1 stack.39.edges
  18.5 6.3 %collective-permute-done.4 = bf16[2,8,36,256]{3,2,1,0:T(8,128)(2,1)S(1)} collective-permute-done((bf16[2,8,36,256]{3,2,1,0:T(8,128)(2,1)S(1)}, bf16[2,8,36,256]{3,2,1,0:T(8,128)(2,1)S(1)}, u32[]{:S(2)}, u32[]{:S(2)}) %collective-permute-start.4) | collective-permute-done | bytes 294944 | tf_op jit(solution)/shard_map/ppermute | solution.py:24
  24.7 0.0 collective-permute-done.3
  24.8 0.0 copy-done.3
  24.8 0.0 copy-done.2
  24.8 0.0 copy-start
  24.8 2.0 %copy-done = bf16[3,3,3,256,256]{4,3,2,1,0:T(8,128)(2,1)S(1)} copy-done((bf16[3,3,3,256,256]{4,3,2,1,0:T(8,128)(2,1)S(1)}, bf16[3,3,3,256,256]{4,3,2,1,0:T(8,128)(2,1)}, u32[]{:S(2)}) %copy-start) | copy-done | bytes 3538968
  26.8 0.0 copy-start.1
  26.8 2.0 %copy-done.1 = bf16[3,3,3,256,256]{4,3,2,1,0:T(8,128)(2,1)S(1)} copy-done((bf16[3,3,3,256,256]{4,3,2,1,0:T(8,128)(2,1)S(1)}, bf16[3,3,3,256,256]{4,3,2,1,0:T(8,128)(2,1)}, u32[]{:S(2)}) %copy-start.1) | copy-done | bytes 3538968
  28.8 8.4 %shard_map.55 = bf16[4,4,32,256]{3,2,1,0:T(8,128)(2,1)S(1)} custom-call(s32[6]{0:T(128)S(1)} %stack.39.edges, bf16[2,8,36,256]{3,2,1,0:T(8,128)(2,1)S(1)} %get-tuple-element.6.xb, bf16[4,8,36,256]{3,2,1,0:T(8,128)(2,1)S(1)} %pad_maximum_fusion.xc, bf16[2,8,36,256]{3,2,1,0:T(8,128)(2,1)S(1)} %get-tuple-element.5.xa, bf16[3,3,3,256,256]{4,3,2,1,0:T(8,128)(2,1)S(1)} %copy-done, ...), custom_call_target="tpu_custom_call" | custom-call | flops 5888802816 | bytes 8388608 | tf_op jit(solution)/shard_map/pallas_call | solution.py:148
  37.3 0.1 constant_dynamic-slice_fusion.1
  37.3 1.6 %collective-permute-start.5 = (bf16[4,4,32,128]{3,2,1,0:T(8,128)(2,1)S(1)}, bf16[4,4,32,128]{3,2,1,0:T(8,128)(2,1)S(1)}, u32[]{:S(2)}, u32[]{:S(2)}) collective-permute-start(bf16[4,4,32,128]{3,2,1,0:T(8,128)(2,1)S(1)} %get-tuple-element.14), channel_id=1, source_target_pairs={{0,1},{1,0},{2,3},{3,2},{4,5},{5,4},{6,7},{7,6},{8,9},{9,8},{10,11... | collective-permute-start | bytes 393224 | tf_op jit(solution)/shard_map/ppermute | solution.py:55
  38.9 3.5 %collective-permute-done.5 = bf16[4,4,32,128]{3,2,1,0:T(8,128)(2,1)S(1)} collective-permute-done((bf16[4,4,32,128]{3,2,1,0:T(8,128)(2,1)S(1)}, bf16[4,4,32,128]{3,2,1,0:T(8,128)(2,1)S(1)}, u32[]{:S(2)}, u32[]{:S(2)}) %collective-permute-start.5) | collective-permute-done | bytes 131104 | tf_op jit(solution)/shard_map/ppermute | solution.py:55
  42.4 0.8 %maximum_select_fusion.1 = bf16[4,4,64,128]{3,2,1,0:T(8,128)(2,1)} fusion(bf16[4,4,32,128]{3,2,1,0:T(8,128)(2,1)S(1)} %collective-permute-done.5, bf16[4,4,32,128]{3,2,1,0:T(8,128)(2,1)S(1)} %get-tuple-element.13, pred[]{:T(512)S(6)} %eq.31), kind=kLoop, calls=%fused_computation.8 | loop fusion | flops 1179648 | bytes 524289 | tf_op jit(solution)/shard_map/jit(_where)/select_n | solution.py:57
  (4 shorter events, 0.2 us)
Async XLA Ops:
  0.0 24.8 %copy-start.3 = (f32[256]{0:T(256)S(1)}, f32[256]{0:T(256)}, u32[]{:S(2)}) copy-start(f32[256]{0:T(256)} %param.9) | copy-start | bytes 3076
  0.0 24.8 %copy-start.2 = (f32[256]{0:T(256)S(1)}, f32[256]{0:T(256)}, u32[]{:S(2)}) copy-start(f32[256]{0:T(256)} %param.7) | copy-start | bytes 3076
  1.2 6.0 %collective-permute-start = (bf16[4,4,36,128]{3,2,1,0:T(8,128)(2,1)S(1)}, bf16[4,4,36,128]{3,2,1,0:T(8,128)(2,1)S(1)}, u32[]{:S(2)}, u32[]{:S(2)}) collective-permute-start(bf16[4,4,36,128]{3,2,1,0:T(8,128)(2,1)S(1)} %get-tuple-element.16), channel_id=1, source_target_pairs={{0,1},{1,0},{2,3},{3,2},{4,5},{5,4},{6,7},{7,6},{8,9},{9,8},{10,11... | collective-permute-start | bytes 442376 | tf_op jit(solution)/shard_map/ppermute | solution.py:40
  7.3 5.4 %collective-permute-start.1 = (bf16[4,2,36,256]{3,2,1,0:T(8,128)(2,1)S(1)}, bf16[4,2,36,256]{3,2,1,0:T(8,128)(2,1)S(1)}, u32[]{:S(2)}, u32[]{:S(2)}) collective-permute-start(bf16[4,2,36,256]{3,2,1,0:T(8,128)(2,1)S(1)} %get-tuple-element.11), channel_id=1, source_target_pairs={{0,2},{4,6},{2,0},{6,4},{1,3},{5,7},{3,1},{7,5},{8,10},{12,14},{10... | collective-permute-start | bytes 442376 | tf_op jit(solution)/shard_map/ppermute | solution.py:23
  9.0 7.2 %collective-permute-start.2 = (bf16[4,2,36,256]{3,2,1,0:T(8,128)(2,1)S(1)}, bf16[4,2,36,256]{3,2,1,0:T(8,128)(2,1)S(1)}, u32[]{:S(2)}, u32[]{:S(2)}) collective-permute-start(bf16[4,2,36,256]{3,2,1,0:T(8,128)(2,1)S(1)} %get-tuple-element.12), channel_id=1, source_target_pairs={{2,4},{4,2},{0,0},{6,6},{3,5},{5,3},{1,1},{7,7},{10,12},{12,10},{8... | collective-permute-start | bytes 442376 | tf_op jit(solution)/shard_map/ppermute | solution.py:24
  16.3 8.4 %collective-permute-start.4 = (bf16[2,8,36,256]{3,2,1,0:T(8,128)(2,1)S(1)}, bf16[2,8,36,256]{3,2,1,0:T(8,128)(2,1)S(1)}, u32[]{:S(2)}, u32[]{:S(2)}) collective-permute-start(bf16[2,8,36,256]{3,2,1,0:T(8,128)(2,1)S(1)} %get-tuple-element.7), channel_id=1, source_target_pairs={{8,16},{16,8},{0,0},{24,24},{9,17},{17,9},{1,1},{25,25},{10,18},{1... | collective-permute-start | bytes 884744 | tf_op jit(solution)/shard_map/ppermute | solution.py:24
  18.3 6.5 %collective-permute-start.3 = (bf16[2,8,36,256]{3,2,1,0:T(8,128)(2,1)S(1)}, bf16[2,8,36,256]{3,2,1,0:T(8,128)(2,1)S(1)}, u32[]{:S(2)}, u32[]{:S(2)}) collective-permute-start(bf16[2,8,36,256]{3,2,1,0:T(8,128)(2,1)S(1)} %get-tuple-element.8), channel_id=1, source_target_pairs={{0,8},{16,24},{8,0},{24,16},{1,9},{17,25},{9,1},{25,17},{2,10},{18... | collective-permute-start | bytes 884744 | tf_op jit(solution)/shard_map/ppermute | solution.py:23
  24.8 2.0 %copy-start = (bf16[3,3,3,256,256]{4,3,2,1,0:T(8,128)(2,1)S(1)}, bf16[3,3,3,256,256]{4,3,2,1,0:T(8,128)(2,1)}, u32[]{:S(2)}) copy-start(bf16[3,3,3,256,256]{4,3,2,1,0:T(8,128)(2,1)} %k1.1) | copy-start | bytes 10616836
  26.8 2.0 %copy-start.1 = (bf16[3,3,3,256,256]{4,3,2,1,0:T(8,128)(2,1)S(1)}, bf16[3,3,3,256,256]{4,3,2,1,0:T(8,128)(2,1)}, u32[]{:S(2)}) copy-start(bf16[3,3,3,256,256]{4,3,2,1,0:T(8,128)(2,1)} %k2.1) | copy-start | bytes 10616836
  37.3 5.0 %collective-permute-start.5 = (bf16[4,4,32,128]{3,2,1,0:T(8,128)(2,1)S(1)}, bf16[4,4,32,128]{3,2,1,0:T(8,128)(2,1)S(1)}, u32[]{:S(2)}, u32[]{:S(2)}) collective-permute-start(bf16[4,4,32,128]{3,2,1,0:T(8,128)(2,1)S(1)} %get-tuple-element.14), channel_id=1, source_target_pairs={{0,1},{1,0},{2,3},{3,2},{4,5},{5,4},{6,7},{7,6},{8,9},{9,8},{10,11... | collective-permute-start | bytes 393224 | tf_op jit(solution)/shard_map/ppermute | solution.py:55

commit v2 on v0

v2 whole, which is shorter than its diff:
```python
import functools

import jax
import jax.numpy as jnp
from jax import lax
from jax.experimental import pallas as pl
from jax.experimental.pallas import tpu as pltpu
from jax.sharding import PartitionSpec as P

VMEM = pl.BlockSpec(memory_space=pltpu.VMEM)
SMEM = pl.BlockSpec(memory_space=pltpu.SMEM)
ANY = pl.BlockSpec(memory_space=pl.ANY)


def leaky(value):
    return jnp.where(value > 0, value, 0.3 * value)


def pairings(peers):
    rounds = []
    for start in (0, 1):
        pairs = [(i, i + 1) for i in range(start, peers - 1, 2)]
        busy = {i for pair in pairs for i in pair}
        rounds.append(pairs + [(j, i) for i, j in pairs] + [(i, i) for i in range(peers) if i not in busy])
    return rounds


def exchange(first, last, axis):
    odd = lax.axis_index(axis) % 2 == 1
    near, far = pairings(lax.axis_size(axis))
    one = lax.ppermute(jnp.where(odd, first, last), axis, near)
    two = lax.ppermute(jnp.where(odd, last, first), axis, far)
    return one, two


def beside(one, two, axis):
    peers, index = lax.axis_size(axis), lax.axis_index(axis)
    odd = index % 2 == 1
    before = jnp.where(odd, one, two)
    after = jnp.where(odd, two, one)
    before = jnp.where(index == 0, jnp.zeros_like(before), before)
    after = jnp.where(index == peers - 1, jnp.zeros_like(after), after)
    return before, after


def by_origin(parts, axis, dim):
    peers, index = lax.axis_size(axis), lax.axis_index(axis)
    if peers == 2:
        return jnp.where(index == 0, jnp.concatenate(parts, dim), jnp.concatenate(parts[::-1], dim))
    stacked = jnp.stack(parts)
    order = (index - jnp.arange(peers)) % peers
    return jnp.concatenate([stacked[order[c]] for c in range(peers)], dim)


def swapped(piece, axis):
    peers, index = lax.axis_size(axis), lax.axis_index(axis)
    parts = [piece(index)]
    for s in range(1, peers):
        parts.append(lax.ppermute(piece((index + s) % peers), axis, [(i, (i + s) % peers) for i in range(peers)]))
    return parts


def to_columns(x, axis):
    own = x.shape[2] // lax.axis_size(axis)
    padded = jnp.pad(x, ((0, 0), (0, 0), (2, 2), (0, 0)))
    return by_origin(swapped(lambda i: lax.dynamic_slice_in_dim(padded, i * own, own + 4, 2), axis), axis, 3)


def stage_kernel(k1, k2, o1, o2, sems):
    copies = [pltpu.make_async_copy(k1, o1, sems.at[0]), pltpu.make_async_copy(k2, o2, sems.at[1])]
    for copy in copies:
        copy.start()
    for copy in copies:
        copy.wait()


def staged(k1, k2):
    return pl.pallas_call(
        stage_kernel,
        out_shape=[jax.ShapeDtypeStruct(k1.shape, k1.dtype), jax.ShapeDtypeStruct(k2.shape, k2.dtype)],
        in_specs=[ANY, ANY],
        out_specs=[VMEM, VMEM],
        scratch_shapes=[pltpu.SemaphoreType.DMA((2,))],
        cost_estimate=pl.CostEstimate(flops=0, bytes_accessed=2 * (k1.size + k2.size) * 2, transcendentals=0),
        compiler_params=pltpu.CompilerParams(vmem_limit_bytes=24 * 2**20),
        name="weights",
    )(k1, k2)


def spread(x, row, sides, info, x3, ef, e3, eb):
    H, Wp, C = x.shape
    own = Wp - 4
    for c in range(3):
        x3[row, :, :, c * C:(c + 1) * C] = x[:, 1 + c:1 + c + own, :]
    for s in range(sides):
        low, high = x[:, 0:3, :], x[:, Wp - 3:Wp, :]
        pick = jnp.where(info[4] == 0, high, low) if sides == 1 else (low, high)[s]
        pick = pick.astype(jnp.float32)
        for l in range(0, C, 128):
            for h in range(H):
                ef[s, l // 128, pl.ds(pl.multiple_of((row * H + h) * 8, 8), 3), :] = pick[h, :, l:l + 128]
            for c in range(3):
                e3[s, row, 0:H, c * C + l:c * C + l + 128] = ef[s, l // 128, pl.ds(row * H * 8 + c, H, stride=8), :]
        for b in range(3):
            eb[s, b, row] = e3[s, row, b:b + H, :].astype(jnp.bfloat16)


def hidden_rows(d, sides, info, global_row, x3, eb, k1, bias, store):
    H, own, C = x3.shape[1], x3.shape[2], x3.shape[3] // 3
    H1 = H - 2
    main = 2 * H1 * own
    acc = jnp.zeros((main + sides * 2 * H, C), jnp.float32)
    for a in range(3):
        for b in range(3):
            lhs = [x3[d + a:d + a + 2, b:b + H1].reshape(main, 3 * C)]
            lhs += [eb[s, b, d + a:d + a + 2].reshape(2 * H, 3 * C) for s in range(sides)]
            acc += jnp.dot(jnp.concatenate(lhs, 0), k1[a, b].reshape(3 * C, C), preferred_element_type=jnp.float32)
    acc = leaky(acc + bias)
    column = lax.broadcasted_iota(jnp.int32, (own, C), 0)
    none = jnp.zeros((1, C), jnp.float32)
    for q in range(2):
        rows = acc[q * H1 * own:(q + 1) * H1 * own].reshape(H1, own, C)
        ends = [acc[main + (s * 2 + q) * H:main + (s * 2 + q + 1) * H] for s in range(sides)]
        depth = global_row + q
        inside = jnp.logical_and(depth >= 0, depth < info[1])
        for h in range(H1):
            ok = inside
            if h == 0:
                ok = jnp.logical_and(ok, info[2] == 0)
            if h == H1 - 1:
                ok = jnp.logical_and(ok, info[3] == 0)
            row = jnp.where(ok, rows[h], 0.0)
            left, right = ends[0][h:h + 1], ends[sides - 1][h:h + 1]
            left = jnp.where(jnp.logical_and(ok, info[4] > 0), left, none)
            right = jnp.where(jnp.logical_and(ok, info[4] < info[5] - 1), right, none)
            store(q, h, 0, jnp.where(column == 0, left, pltpu.roll(row, 1, 0)).astype(jnp.bfloat16))
            store(q, h, 1, row.astype(jnp.bfloat16))
            store(q, h, 2, jnp.where(column == own - 1, right, pltpu.roll(row, own - 1, 0)).astype(jnp.bfloat16))


def feature_rows(d, h3, k2, bias, o_ref):
    H1, own, C = h3.shape[1], h3.shape[2], h3.shape[3] // 3
    H0 = H1 - 2
    acc = jnp.zeros((2 * H0 * own, C), jnp.float32)
    for a in range(3):
        for b in range(3):
            lhs = h3[d + a:d + a + 2, b:b + H0].reshape(2 * H0 * own, 3 * C)
            acc += jnp.dot(lhs, k2[a, b].reshape(3 * C, C), preferred_element_type=jnp.float32)
    o_ref[...] = leaky(acc + bias).astype(jnp.bfloat16).reshape(2, H0, own, C)


def near_kernel(sides, info, xc, xn, k1, b1, k2, b2, o_ref, keep, x3, ef, e3, eb, h3):
    D = xc.shape[0]
    C = xc.shape[3]
    odd = info[6]
    for d in range(D):
        spread(xc[d], 2 * odd + d, sides, info, x3, ef, e3, eb)
    for d in range(2):
        x = xn[d]
        x = jnp.where(info[7] == 0, x, jnp.zeros_like(x))
        spread(x, D * (1 - odd) + d, sides, info, x3, ef, e3, eb)
    first = info[0] - 1 + 2 * (1 - odd)

    for d in range(0, D, 2):
        def store(q, h, c, value, d=d):
            h3[d + q, h, :, c * C:(c + 1) * C] = value
        hidden_rows(d, sides, info, first + d, x3, eb, k1, b1[...], store)
    keep[...] = h3[pl.ds((D - 2) * odd, 2)]
    for d in range(0, D - 2, 2):
        feature_rows(d, h3, k2, b2[...], o_ref)


def far_kernel(sides, info, xc, xf, keep, k1, b1, k2, b2, o_ref, x3, ef, e3, eb, h3):
    D = xc.shape[0]
    C = xc.shape[3]
    odd = info[6]
    for d in range(2):
        spread(xc[(D - 2) * odd + d], 2 * (1 - odd) + d, sides, info, x3, ef, e3, eb)
    for d in range(2):
        x = xf[d]
        x = jnp.where(info[8] == 0, x, jnp.zeros_like(x))
        spread(x, 2 * odd + d, sides, info, x3, ef, e3, eb)
    first = info[0] - 1 + D * odd
    h3[pl.ds(2 * (1 - odd), 2)] = keep[...]

    def store(q, h, c, value):
        h3[2 * odd + q, h, :, c * C:(c + 1) * C] = value
    hidden_rows(0, sides, info, first, x3, eb, k1, b1[...], store)
    feature_rows(0, h3, k2, b2[...], o_ref)


def kernel_call(kernel, name, rows, sides, xc, keeps, operands):
    D, H, Wp, C = xc.shape
    own = Wp - 4
    out = [jax.ShapeDtypeStruct((2, H - 4, own, C), jnp.bfloat16)]
    if keeps:
        out.append(jax.ShapeDtypeStruct((2, H - 2, own, 3 * C), jnp.bfloat16))
    hid = (rows - 2) * (H - 2) * own
    return pl.pallas_call(
        functools.partial(kernel, sides),
        out_shape=out,
        in_specs=[SMEM] + [VMEM] * (len(operands) - 1),
        out_specs=[VMEM] * len(out),
        scratch_shapes=[
            pltpu.VMEM((rows, H, own, 3 * C), jnp.bfloat16),
            pltpu.VMEM((sides, C // 128, rows * H * 8, 128), jnp.float32),
            pltpu.VMEM((sides, rows, 2 * H, 3 * C), jnp.float32),
            pltpu.VMEM((sides, 3, rows, H, 3 * C), jnp.bfloat16),
            pltpu.VMEM((4, H - 2, own, 3 * C), jnp.bfloat16),
        ],
        compiler_params=pltpu.CompilerParams(vmem_limit_bytes=24 * 2**20),
        cost_estimate=pl.CostEstimate(flops=2 * 27 * C * C * (hid + 2 * (H - 4) * own), bytes_accessed=2**20, transcendentals=0),
        name=name,
    )(*operands)


def body(volume, kernel_one, bias_one, kernel_two, bias_two):
    k1, k2 = staged(kernel_one, kernel_two)
    b1, b2 = bias_one.reshape(1, -1), bias_two.reshape(1, -1)
    d, h, f = (lax.axis_index(a) for a in ("depth", "height", "filt"))
    nd, nh, nf = (lax.axis_size(a) for a in ("depth", "height", "filt"))
    rows = volume.shape[0]
    odd = d % 2
    info = jnp.stack([
        d * rows, jnp.int32(nd * rows), (h == 0).astype(jnp.int32), (h == nh - 1).astype(jnp.int32), f, jnp.int32(nf), odd,
        jnp.logical_and(odd == 0, d == nd - 1).astype(jnp.int32),
        jnp.where(odd == 1, d == nd - 1, d == 0).astype(jnp.int32),
    ])
    sides = 1 if nf == 2 else 2

    whole = to_columns(volume, "filt")
    before, after = beside(*exchange(whole[:, :2], whole[:, -2:], "height"), "height")
    tall = jnp.concatenate([before, whole, after], 1)
    near, far = exchange(tall[:2], tall[-2:], "depth")
    out_near, keep = kernel_call(near_kernel, "near", rows + 2, sides, tall, True, (info, tall, near, k1, b1, k2, b2))
    shard = volume.shape[3]
    near_parts = swapped(lambda i: lax.dynamic_slice_in_dim(out_near, i * shard, shard, 3), "filt")
    out_far, = kernel_call(far_kernel, "far", 4, sides, tall, False, (info, tall, far, keep, k1, b1, k2, b2))
    far_parts = swapped(lambda i: lax.dynamic_slice_in_dim(out_far, i * shard, shard, 3), "filt")
    out_near, out_far = by_origin(near_parts, "filt", 2), by_origin(far_parts, "filt", 2)
    return jnp.where(odd == 1, jnp.concatenate([out_near, out_far], 0), jnp.concatenate([out_far, out_near], 0))


def solution(mesh):
    in_specs = (P("depth", "height", None, "filt"), P(), P(), P(), P())
    out_specs = P("depth", "height", None, "filt")
    return jax.shard_map(body, mesh=mesh, in_specs=in_specs, out_specs=out_specs, check_vma=False)
```

time: 79.9 us -> 50.4 us (0.63)
  the two profiles are of different devices: /device:TPU:1 before, /device:TPU:18 now
where the time goes in v2:
time: 50.4 us; the launch traced here: 50.1 us
  waiting for transfers between devices  13.4 us (27%)
  local copies, waits for them, and re-layouts  12.8 us (25%)
  Pallas kernels  12.7 us (25%)
  starting transfers between devices  9.79 us (19%)
  other arithmetic  1.1 us (2%)
    pallas_call x2, Pallas kernels, kernel_call(): pl.pallas_call(functools.partial(kernel, sides), out_shape=out, in_specs=...  11.9 us
    unnamed x16, local copies, waits for them, and re-layouts  11.6 us
    ppermute x3, waiting for transfers between devices, swapped(): lax.ppermute(piece((index + s) % peers), axis, [(i, (i + s) % peers) for...  8.14 us
    ppermute x2, starting transfers between devices, exchange(): two = lax.ppermute(jnp.where(odd, last, first), axis, far)  4.41 us
    ppermute x3, starting transfers between devices, swapped(): lax.ppermute(piece((index + s) % peers), axis, [(i, (i + s) % peers) for...  3.67 us
    ppermute x2, waiting for transfers between devices, exchange(): two = lax.ppermute(jnp.where(odd, last, first), axis, far)  3.46 us
    ppermute x2, waiting for transfers between devices, exchange(): one = lax.ppermute(jnp.where(odd, first, last), axis, near)  1.81 us
    ppermute x2, starting transfers between devices, exchange(): one = lax.ppermute(jnp.where(odd, first, last), axis, near)  1.71 us
  transfers between devices with their start and end apart: 7, of which 5 were waited for; matrix products, arithmetic and copies ran while one was open for 0% of the time, Pallas kernels for 14%

profile of v2, /device:TPU:18, one launch (start us, length us, event | category | flops | bytes accessed | tf_op | source)
XLA Modules:
  0.0 50.1 jit_solution(6009987277432422956)
XLA Ops:
  0.0 1.1 %pad_dynamic-slice_fusion.1 = (bf16[4,4,36,128]{3,2,1,0:T(8,128)(2,1)S(1)}, bf16[4,4,36,128]{3,2,1,0:T(8,128)(2,1)S(1)}) fusion(s32[]{:T(128)S(6)} %select_n.121, bf16[4,4,64,128]{3,2,1,0:T(8,128)(2,1)} %param.5, s32[]{:T(128)S(6)} %select_n.123), kind=kLoop, calls=%fused_computation.5 | loop fusion | bytes 557064 | tf_op jit(solution)/shard_map/dynamic_slice | solution.py:66
  1.1 1.6 %collective-permute-start = (bf16[4,4,36,128]{3,2,1,0:T(8,128)(2,1)S(1)}, bf16[4,4,36,128]{3,2,1,0:T(8,128)(2,1)S(1)}, u32[]{:S(2)}, u32[]{:S(2)}) collective-permute-start(bf16[4,4,36,128]{3,2,1,0:T(8,128)(2,1)S(1)} %get-tuple-element.20), channel_id=1, source_target_pairs={{0,1},{1,0},{2,3},{3,2},{4,5},{5,4},{6,7},{7,6},{8,9},{9,8},{10,11... | collective-permute-start | bytes 442376 | tf_op jit(solution)/shard_map/ppermute | solution.py:59
  2.7 4.4 %collective-permute-done = bf16[4,4,36,128]{3,2,1,0:T(8,128)(2,1)S(1)} collective-permute-done((bf16[4,4,36,128]{3,2,1,0:T(8,128)(2,1)S(1)}, bf16[4,4,36,128]{3,2,1,0:T(8,128)(2,1)S(1)}, u32[]{:S(2)}, u32[]{:S(2)}) %collective-permute-start) | collective-permute-done | bytes 147488 | tf_op jit(solution)/shard_map/ppermute | solution.py:59
  7.1 0.1 maximum_select_fusion
  7.3 1.6 %collective-permute-start.1 = (bf16[4,2,36,256]{3,2,1,0:T(8,128)(2,1)S(1)}, bf16[4,2,36,256]{3,2,1,0:T(8,128)(2,1)S(1)}, u32[]{:S(2)}, u32[]{:S(2)}) collective-permute-start(bf16[4,2,36,256]{3,2,1,0:T(8,128)(2,1)S(1)} %get-tuple-element.17), channel_id=1, source_target_pairs={{0,2},{4,6},{2,0},{6,4},{1,3},{5,7},{3,1},{7,5},{8,10},{12,14},{10... | collective-permute-start | bytes 442376 | tf_op jit(solution)/shard_map/ppermute | solution.py:31
  8.9 1.9 %collective-permute-start.2 = (bf16[4,2,36,256]{3,2,1,0:T(8,128)(2,1)S(1)}, bf16[4,2,36,256]{3,2,1,0:T(8,128)(2,1)S(1)}, u32[]{:S(2)}, u32[]{:S(2)}) collective-permute-start(bf16[4,2,36,256]{3,2,1,0:T(8,128)(2,1)S(1)} %get-tuple-element.18), channel_id=1, source_target_pairs={{2,4},{4,2},{0,0},{6,6},{3,5},{5,3},{1,1},{7,7},{10,12},{12,10},{8... | collective-permute-start | bytes 442376 | tf_op jit(solution)/shard_map/ppermute | solution.py:32
  10.9 1.8 %collective-permute-done.1 = bf16[4,2,36,256]{3,2,1,0:T(8,128)(2,1)S(1)} collective-permute-done((bf16[4,2,36,256]{3,2,1,0:T(8,128)(2,1)S(1)}, bf16[4,2,36,256]{3,2,1,0:T(8,128)(2,1)S(1)}, u32[]{:S(2)}, u32[]{:S(2)}) %collective-permute-start.1) | collective-permute-done | bytes 147488 | tf_op jit(solution)/shard_map/ppermute | solution.py:31
  12.7 3.5 %collective-permute-done.2 = bf16[4,2,36,256]{3,2,1,0:T(8,128)(2,1)S(1)} collective-permute-done((bf16[4,2,36,256]{3,2,1,0:T(8,128)(2,1)S(1)}, bf16[4,2,36,256]{3,2,1,0:T(8,128)(2,1)S(1)}, u32[]{:S(2)}, u32[]{:S(2)}) %collective-permute-start.2) | collective-permute-done | bytes 147488 | tf_op jit(solution)/shard_map/ppermute | solution.py:32
  16.2 0.1 pad_maximum_fusion.xc
  16.3 0.1 collective-permute-start.3
  16.4 0.0 copy-start
  16.4 2.0 %copy-done = bf16[3,3,3,256,256]{4,3,2,1,0:T(8,128)(2,1)S(1)} copy-done((bf16[3,3,3,256,256]{4,3,2,1,0:T(8,128)(2,1)S(1)}, bf16[3,3,3,256,256]{4,3,2,1,0:T(8,128)(2,1)}, u32[]{:S(2)}) %copy-start) | copy-done | bytes 3538968
  18.4 0.0 copy-start.1
  18.4 2.0 %copy-done.1 = bf16[3,3,3,256,256]{4,3,2,1,0:T(8,128)(2,1)S(1)} copy-done((bf16[3,3,3,256,256]{4,3,2,1,0:T(8,128)(2,1)S(1)}, bf16[3,3,3,256,256]{4,3,2,1,0:T(8,128)(2,1)}, u32[]{:S(2)}) %copy-start.1) | copy-done | bytes 3538968
  20.4 0.0 copy-start.6
  20.4 0.0 copy-start.7
  20.4 0.8 %weights.1 = (bf16[3,3,3,256,256]{4,3,2,1,0:T(8,128)(2,1)S(1)}, bf16[3,3,3,256,256]{4,3,2,1,0:T(8,128)(2,1)S(1)}) custom-call(bf16[3,3,3,256,256]{4,3,2,1,0:T(8,128)(2,1)S(1)} %copy-done, bf16[3,3,3,256,256]{4,3,2,1,0:T(8,128)(2,1)S(1)} %copy-done.1), custom_call_target="tpu_custom_call" | custom-call | bytes 14155776 | tf_op jit(solution)/shard_map/weights/pallas_call | solution.py:78
  21.3 0.0 copy-start.2
  21.3 1.8 %copy-done.2 = bf16[3,3,3,256,256]{4,3,2,1,0:T(8,128)(2,1)} copy-done((bf16[3,3,3,256,256]{4,3,2,1,0:T(8,128)(2,1)}, bf16[3,3,3,256,256]{4,3,2,1,0:T(8,128)(2,1)S(1)}, u32[]{:S(2)}) %copy-start.2) | copy-done | bytes 3538968
  23.0 0.0 copy-start.4
  23.0 1.8 %copy-done.4 = bf16[3,3,3,256,256]{4,3,2,1,0:T(8,128)(2,1)} copy-done((bf16[3,3,3,256,256]{4,3,2,1,0:T(8,128)(2,1)}, bf16[3,3,3,256,256]{4,3,2,1,0:T(8,128)(2,1)S(1)}, u32[]{:S(2)}) %copy-start.4) | copy-done | bytes 3538968
  24.8 0.1 stack.47.info
  24.9 2.5 %collective-permute-start.5 = (bf16[2,8,36,256]{3,2,1,0:T(8,128)(2,1)S(1)}, bf16[2,8,36,256]{3,2,1,0:T(8,128)(2,1)S(1)}, u32[]{:S(2)}, u32[]{:S(2)}) collective-permute-start(bf16[2,8,36,256]{3,2,1,0:T(8,128)(2,1)S(1)} %get-tuple-element.14), channel_id=1, source_target_pairs={{8,16},{16,8},{0,0},{24,24},{9,17},{17,9},{1,1},{25,25},{10,18},{1... | collective-permute-start | bytes 884744 | tf_op jit(solution)/shard_map/ppermute | solution.py:32
  27.4 0.0 collective-permute-done.3.xn
  27.4 0.0 copy-done.6
  27.4 0.0 copy-done.7
  27.5 0.0 copy-start.3
  27.5 2.0 %copy-done.3 = bf16[3,3,3,256,256]{4,3,2,1,0:T(8,128)(2,1)S(1)} copy-done((bf16[3,3,3,256,256]{4,3,2,1,0:T(8,128)(2,1)S(1)}, bf16[3,3,3,256,256]{4,3,2,1,0:T(8,128)(2,1)}, u32[]{:S(2)}) %copy-start.3) | copy-done | bytes 3538968
  29.5 0.0 copy-start.5
  29.5 2.0 %copy-done.5 = bf16[3,3,3,256,256]{4,3,2,1,0:T(8,128)(2,1)S(1)} copy-done((bf16[3,3,3,256,256]{4,3,2,1,0:T(8,128)(2,1)S(1)}, bf16[3,3,3,256,256]{4,3,2,1,0:T(8,128)(2,1)}, u32[]{:S(2)}) %copy-start.5) | copy-done | bytes 3538968
  31.5 6.4 %near.1 = (bf16[2,4,32,256]{3,2,1,0:T(8,128)(2,1)S(1)}, bf16[2,6,32,768]{3,2,1,0:T(8,128)(2,1)S(1)}) custom-call(s32[9]{0:T(128)S(1)} %stack.47.info, bf16[4,8,36,256]{3,2,1,0:T(8,128)(2,1)S(1)} %pad_maximum_fusion.xc, bf16[2,8,36,256]{3,2,1,0:T(8,128)(2,1)S(1)} %collective-permute-done.3.xn, bf16[3,3,3,256,256]{4,3,2,1,0:T(8,128)(2,1)S(1)} %copy-done.3, ...), custom_call_target="tpu_custom_call" | custom-call | flops 3623878656 | bytes 1048576 | tf_op jit(solution)/shard_map/near/pallas_call | solution.py:199
  37.9 0.0 collective-permute-done.5.xf
  37.9 5.5 %far.1 = bf16[2,4,32,256]{3,2,1,0:T(8,128)(2,1)S(1)} custom-call(s32[9]{0:T(128)S(1)} %stack.47.info, bf16[4,8,36,256]{3,2,1,0:T(8,128)(2,1)S(1)} %pad_maximum_fusion.xc, bf16[2,8,36,256]{3,2,1,0:T(8,128)(2,1)S(1)} %collective-permute-done.5.xf, bf16[2,6,32,768]{3,2,1,0:T(8,128)(2,1)S(1)} %get-tuple-element.12.keep, ...), custom_call_target="tpu_custom_call" | custom-call | flops 2264924160 | bytes 1048576 | tf_op jit(solution)/shard_map/far/pallas_call | solution.py:199
  43.4 0.1 constant_dynamic-slice_fusion.1
  43.5 1.6 %collective-permute-start.6 = (bf16[2,4,32,128]{3,2,1,0:T(8,128)(2,1)S(1)}, bf16[2,4,32,128]{3,2,1,0:T(8,128)(2,1)S(1)}, u32[]{:S(2)}, u32[]{:S(2)}) collective-permute-start(bf16[2,4,32,128]{3,2,1,0:T(8,128)(2,1)S(1)} %get-tuple-element.24), channel_id=1, source_target_pairs={{0,1},{1,0},{2,3},{3,2},{4,5},{5,4},{6,7},{7,6},{8,9},{9,8},{10,11... | collective-permute-start | bytes 196616 | tf_op jit(solution)/shard_map/ppermute | solution.py:59
  45.0 0.5 %collective-permute-start.4 = (bf16[2,4,32,128]{3,2,1,0:T(8,128)(2,1)S(1)}, bf16[2,4,32,128]{3,2,1,0:T(8,128)(2,1)S(1)}, u32[]{:S(2)}, u32[]{:S(2)}) collective-permute-start(bf16[2,4,32,128]{3,2,1,0:T(8,128)(2,1)S(1)} %get-tuple-element.25), channel_id=1, source_target_pairs={{0,1},{1,0},{2,3},{3,2},{4,5},{5,4},{6,7},{7,6},{8,9},{9,8},{10,11... | collective-permute-start | bytes 196616 | tf_op jit(solution)/shard_map/ppermute | solution.py:59
  45.5 2.2 %collective-permute-done.6 = bf16[2,4,32,128]{3,2,1,0:T(8,128)(2,1)S(1)} collective-permute-done((bf16[2,4,32,128]{3,2,1,0:T(8,128)(2,1)S(1)}, bf16[2,4,32,128]{3,2,1,0:T(8,128)(2,1)S(1)}, u32[]{:S(2)}, u32[]{:S(2)}) %collective-permute-start.6) | collective-permute-done | bytes 65568 | tf_op jit(solution)/shard_map/ppermute | solution.py:59
  47.8 1.5 %collective-permute-done.4 = bf16[2,4,32,128]{3,2,1,0:T(8,128)(2,1)S(1)} collective-permute-done((bf16[2,4,32,128]{3,2,1,0:T(8,128)(2,1)S(1)}, bf16[2,4,32,128]{3,2,1,0:T(8,128)(2,1)S(1)}, u32[]{:S(2)}, u32[]{:S(2)}) %collective-permute-start.4) | collective-permute-done | bytes 65568 | tf_op jit(solution)/shard_map/ppermute | solution.py:59
  49.3 0.7 %maximum_select_fusion.1 = bf16[4,4,64,128]{3,2,1,0:T(8,128)(2,1)} fusion(bf16[2,4,64,128]{3,2,1,0:T(8,128)(2,1)S(1)} %maximum_select_fusion.3, bf16[2,4,64,128]{3,2,1,0:T(8,128)(2,1)S(1)} %maximum_select_fusion.2, pred[]{:T(512)S(6)} %eq.40), kind=kLoop, calls=%fused_computation.6 | loop fusion | flops 393216 | bytes 524289 | tf_op jit(solution)/shard_map/jit(_where)/select_n | solution.py:241
  (5 shorter events, 0.2 us)
Async XLA Ops:
  1.1 6.0 %collective-permute-start = (bf16[4,4,36,128]{3,2,1,0:T(8,128)(2,1)S(1)}, bf16[4,4,36,128]{3,2,1,0:T(8,128)(2,1)S(1)}, u32[]{:S(2)}, u32[]{:S(2)}) collective-permute-start(bf16[4,4,36,128]{3,2,1,0:T(8,128)(2,1)S(1)} %get-tuple-element.20), channel_id=1, source_target_pairs={{0,1},{1,0},{2,3},{3,2},{4,5},{5,4},{6,7},{7,6},{8,9},{9,8},{10,11... | collective-permute-start | bytes 442376 | tf_op jit(solution)/shard_map/ppermute | solution.py:59
  7.3 5.4 %collective-permute-start.1 = (bf16[4,2,36,256]{3,2,1,0:T(8,128)(2,1)S(1)}, bf16[4,2,36,256]{3,2,1,0:T(8,128)(2,1)S(1)}, u32[]{:S(2)}, u32[]{:S(2)}) collective-permute-start(bf16[4,2,36,256]{3,2,1,0:T(8,128)(2,1)S(1)} %get-tuple-element.17), channel_id=1, source_target_pairs={{0,2},{4,6},{2,0},{6,4},{1,3},{5,7},{3,1},{7,5},{8,10},{12,14},{10... | collective-permute-start | bytes 442376 | tf_op jit(solution)/shard_map/ppermute | solution.py:31
  8.9 7.2 %collective-permute-start.2 = (bf16[4,2,36,256]{3,2,1,0:T(8,128)(2,1)S(1)}, bf16[4,2,36,256]{3,2,1,0:T(8,128)(2,1)S(1)}, u32[]{:S(2)}, u32[]{:S(2)}) collective-permute-start(bf16[4,2,36,256]{3,2,1,0:T(8,128)(2,1)S(1)} %get-tuple-element.18), channel_id=1, source_target_pairs={{2,4},{4,2},{0,0},{6,6},{3,5},{5,3},{1,1},{7,7},{10,12},{12,10},{8... | collective-permute-start | bytes 442376 | tf_op jit(solution)/shard_map/ppermute | solution.py:32
  16.3 11.1 %collective-permute-start.3 = (bf16[2,8,36,256]{3,2,1,0:T(8,128)(2,1)S(1)}, bf16[2,8,36,256]{3,2,1,0:T(8,128)(2,1)S(1)}, u32[]{:S(2)}, u32[]{:S(2)}) collective-permute-start(bf16[2,8,36,256]{3,2,1,0:T(8,128)(2,1)S(1)} %get-tuple-element.13), channel_id=1, source_target_pairs={{0,8},{16,24},{8,0},{24,16},{1,9},{17,25},{9,1},{25,17},{2,10},{18... | collective-permute-start | bytes 884744 | tf_op jit(solution)/shard_map/ppermute | solution.py:31
  16.4 2.0 %copy-start = (bf16[3,3,3,256,256]{4,3,2,1,0:T(8,128)(2,1)S(1)}, bf16[3,3,3,256,256]{4,3,2,1,0:T(8,128)(2,1)}, u32[]{:S(2)}) copy-start(bf16[3,3,3,256,256]{4,3,2,1,0:T(8,128)(2,1)} %k1.1) | copy-start | bytes 10616836
  18.4 2.0 %copy-start.1 = (bf16[3,3,3,256,256]{4,3,2,1,0:T(8,128)(2,1)S(1)}, bf16[3,3,3,256,256]{4,3,2,1,0:T(8,128)(2,1)}, u32[]{:S(2)}) copy-start(bf16[3,3,3,256,256]{4,3,2,1,0:T(8,128)(2,1)} %k2.1) | copy-start | bytes 10616836
  20.4 7.0 %copy-start.6 = (f32[256]{0:T(256)S(1)}, f32[256]{0:T(256)}, u32[]{:S(2)}) copy-start(f32[256]{0:T(256)} %param.7) | copy-start | bytes 3076
  20.4 7.0 %copy-start.7 = (f32[256]{0:T(256)S(1)}, f32[256]{0:T(256)}, u32[]{:S(2)}) copy-start(f32[256]{0:T(256)} %param.9) | copy-start | bytes 3076
  21.3 1.8 %copy-start.2 = (bf16[3,3,3,256,256]{4,3,2,1,0:T(8,128)(2,1)}, bf16[3,3,3,256,256]{4,3,2,1,0:T(8,128)(2,1)S(1)}, u32[]{:S(2)}) copy-start(bf16[3,3,3,256,256]{4,3,2,1,0:T(8,128)(2,1)S(1)} %get-tuple-element.9.k1) | copy-start | bytes 10616836
  23.0 1.8 %copy-start.4 = (bf16[3,3,3,256,256]{4,3,2,1,0:T(8,128)(2,1)}, bf16[3,3,3,256,256]{4,3,2,1,0:T(8,128)(2,1)S(1)}, u32[]{:S(2)}) copy-start(bf16[3,3,3,256,256]{4,3,2,1,0:T(8,128)(2,1)S(1)} %get-tuple-element.10.k2) | copy-start | bytes 10616836
  24.9 13.0 %collective-permute-start.5 = (bf16[2,8,36,256]{3,2,1,0:T(8,128)(2,1)S(1)}, bf16[2,8,36,256]{3,2,1,0:T(8,128)(2,1)S(1)}, u32[]{:S(2)}, u32[]{:S(2)}) collective-permute-start(bf16[2,8,36,256]{3,2,1,0:T(8,128)(2,1)S(1)} %get-tuple-element.14), channel_id=1, source_target_pairs={{8,16},{16,8},{0,0},{24,24},{9,17},{17,9},{1,1},{25,25},{10,18},{1... | collective-permute-start | bytes 884744 | tf_op jit(solution)/shard_map/ppermute | solution.py:32
  27.5 2.0 %copy-start.3 = (bf16[3,3,3,256,256]{4,3,2,1,0:T(8,128)(2,1)S(1)}, bf16[3,3,3,256,256]{4,3,2,1,0:T(8,128)(2,1)}, u32[]{:S(2)}) copy-start(bf16[3,3,3,256,256]{4,3,2,1,0:T(8,128)(2,1)} %copy-done.2) | copy-start | bytes 10616836
  29.5 2.0 %copy-start.5 = (bf16[3,3,3,256,256]{4,3,2,1,0:T(8,128)(2,1)S(1)}, bf16[3,3,3,256,256]{4,3,2,1,0:T(8,128)(2,1)}, u32[]{:S(2)}) copy-start(bf16[3,3,3,256,256]{4,3,2,1,0:T(8,128)(2,1)} %copy-done.4) | copy-start | bytes 10616836
  43.5 4.3 %collective-permute-start.6 = (bf16[2,4,32,128]{3,2,1,0:T(8,128)(2,1)S(1)}, bf16[2,4,32,128]{3,2,1,0:T(8,128)(2,1)S(1)}, u32[]{:S(2)}, u32[]{:S(2)}) collective-permute-start(bf16[2,4,32,128]{3,2,1,0:T(8,128)(2,1)S(1)} %get-tuple-element.24), channel_id=1, source_target_pairs={{0,1},{1,0},{2,3},{3,2},{4,5},{5,4},{6,7},{7,6},{8,9},{9,8},{10,11... | collective-permute-start | bytes 196616 | tf_op jit(solution)/shard_map/ppermute | solution.py:59
  45.0 4.3 %collective-permute-start.4 = (bf16[2,4,32,128]{3,2,1,0:T(8,128)(2,1)S(1)}, bf16[2,4,32,128]{3,2,1,0:T(8,128)(2,1)S(1)}, u32[]{:S(2)}, u32[]{:S(2)}) collective-permute-start(bf16[2,4,32,128]{3,2,1,0:T(8,128)(2,1)S(1)} %get-tuple-element.25), channel_id=1, source_target_pairs={{0,1},{1,0},{2,3},{3,2},{4,5},{5,4},{6,7},{7,6},{8,9},{9,8},{10,11... | collective-permute-start | bytes 196616 | tf_op jit(solution)/shard_map/ppermute | solution.py:59

commit v3 on v2

v3 whole, which is shorter than its diff:
```python
import functools

import jax
import jax.numpy as jnp
from jax import lax
from jax.experimental import pallas as pl
from jax.experimental.pallas import tpu as pltpu
from jax.sharding import PartitionSpec as P

VMEM = pl.BlockSpec(memory_space=pltpu.VMEM)
SMEM = pl.BlockSpec(memory_space=pltpu.SMEM)
HBM = pl.BlockSpec(memory_space=pltpu.HBM)


def leaky(value):
    return jnp.where(value > 0, value, 0.3 * value)


def pairings(peers):
    rounds = []
    for start in (0, 1):
        pairs = [(i, i + 1) for i in range(start, peers - 1, 2)]
        busy = {i for pair in pairs for i in pair}
        rounds.append(pairs + [(j, i) for i, j in pairs] + [(i, i) for i in range(peers) if i not in busy])
    return rounds


def exchange(first, last, axis):
    odd = lax.axis_index(axis) % 2 == 1
    near, far = pairings(lax.axis_size(axis))
    one = lax.ppermute(jnp.where(odd, first, last), axis, near)
    two = lax.ppermute(jnp.where(odd, last, first), axis, far)
    return one, two


def beside(one, two, axis):
    peers, index = lax.axis_size(axis), lax.axis_index(axis)
    odd = index % 2 == 1
    before = jnp.where(odd, one, two)
    after = jnp.where(odd, two, one)
    before = jnp.where(index == 0, jnp.zeros_like(before), before)
    after = jnp.where(index == peers - 1, jnp.zeros_like(after), after)
    return before, after


def by_origin(parts, axis, dim):
    peers, index = lax.axis_size(axis), lax.axis_index(axis)
    if peers == 2:
        return jnp.where(index == 0, jnp.concatenate(parts, dim), jnp.concatenate(parts[::-1], dim))
    stacked = jnp.stack(parts)
    order = (index - jnp.arange(peers)) % peers
    return jnp.concatenate([stacked[order[c]] for c in range(peers)], dim)


def swapped(piece, axis):
    peers, index = lax.axis_size(axis), lax.axis_index(axis)
    parts = [piece(index)]
    for s in range(1, peers):
        parts.append(lax.ppermute(piece((index + s) % peers), axis, [(i, (i + s) % peers) for i in range(peers)]))
    return parts


def in_order(parts, axis):
    return by_origin(parts, axis, 3)


def gathered(x, columns, rows):
    nc, nr = lax.axis_size(columns), lax.axis_size(rows)
    c, r = lax.axis_index(columns), lax.axis_index(rows)
    own = x.shape[2] // nc
    odd = r % 2 == 1
    padded = jnp.pad(x, ((0, 0), (0, 0), (2, 2), (0, 0)))
    windows = [lax.dynamic_slice_in_dim(padded, (c + s) % nc * own, own + 4, 2) for s in range(nc)]
    windows = lax.optimization_barrier(windows)
    parts, ones, twos = [windows[0]], [], []
    near, far = pairings(nr)
    for s in range(1, nc):
        parts.append(lax.ppermute(windows[s], columns, [(i, (i + s) % nc) for i in range(nc)]))
    for s in range(nc):
        first, last = windows[s][:, :2], windows[s][:, -2:]
        for to, edge, pairs in ((ones, jnp.where(odd, first, last), near), (twos, jnp.where(odd, last, first), far)):
            moves = [(i * nc + k, j * nc + (k + s) % nc) for i, j in pairs for k in range(nc)]
            to.append(lax.ppermute(edge, (rows, columns), moves))
    one, two = in_order(ones, columns), in_order(twos, columns)
    before, after = beside(one, two, rows)
    return jnp.concatenate([before, in_order(parts, columns), after], 1)


def spread(source, rows, at, sides, info, x3, ef, e3, eb):
    H, Wp, C = source.shape[1:]
    own = Wp - 4

    def step(d, carry):
        x, row = source[d], at + d
        for c in range(3):
            x3[row, :, :, c * C:(c + 1) * C] = x[:, 1 + c:1 + c + own, :]
        for s in range(sides):
            low, high = x[:, 0:3, :], x[:, Wp - 3:Wp, :]
            pick = jnp.where(info[4] == 0, high, low) if sides == 1 else (low, high)[s]
            pick = pick.astype(jnp.float32)
            for l in range(0, C, 128):
                for h in range(H):
                    ef[s, l // 128, pl.ds(h * 8, 3), :] = pick[h, :, l:l + 128]
                for c in range(3):
                    e3[s, 0:H, c * C + l:c * C + l + 128] = ef[s, l // 128, pl.ds(c, H, stride=8), :]
            for b in range(3):
                eb[s, b, row] = e3[s, b:b + H, :].astype(jnp.bfloat16)
        return carry

    lax.fori_loop(0, rows, step, 0)


def clear(rows, at, x3, eb):
    for d in range(rows):
        x3[at + d] = jnp.zeros(x3.shape[1:], x3.dtype)
        for s in range(eb.shape[0]):
            for b in range(3):
                eb[s, b, at + d] = jnp.zeros(eb.shape[3:], eb.dtype)


def hidden_sums(d, sides, x3, eb, k1, bias, raw, ready):
    H, own, C = x3.shape[1], x3.shape[2], x3.shape[3] // 3
    H1 = H - 2
    main = 2 * H1 * own
    acc = jnp.zeros((main + sides * 2 * H, C), jnp.float32)
    for a in range(3):
        ready(a)
        for b in range(3):
            lhs = [x3[pl.ds(d + a, 2), b:b + H1].reshape(main, 3 * C)]
            lhs += [eb[s, b, pl.ds(d + a, 2)].reshape(2 * H, 3 * C) for s in range(sides)]
            acc += jnp.dot(jnp.concatenate(lhs, 0), k1[a, b].reshape(3 * C, C), preferred_element_type=jnp.float32)
    raw[...] = leaky(acc + bias)


def hidden_rows(at, depth, sides, info, own, H, raw, h3):
    C = raw.shape[1]
    H1 = H - 2
    main = 2 * H1 * own
    column = lax.broadcasted_iota(jnp.int32, (own, C), 0)
    none = jnp.zeros((1, C), jnp.float32)

    def step(i, carry):
        q, h = i // H1, i % H1
        ok = jnp.logical_and(depth + q >= 0, depth + q < info[1])
        ok = jnp.logical_and(ok, jnp.logical_or(h > 0, info[2] == 0))
        ok = jnp.logical_and(ok, jnp.logical_or(h < H1 - 1, info[3] == 0))
        row = jnp.where(ok, raw[pl.ds(pl.multiple_of(i * own, 8), own), :], 0.0)
        ends = [raw[pl.ds(main + (s * 2 + q) * H + h, 1), :] for s in range(sides)]
        left = jnp.where(jnp.logical_and(ok, info[4] > 0), ends[0], none)
        right = jnp.where(jnp.logical_and(ok, info[4] < info[5] - 1), ends[sides - 1], none)
        h3[at + q, h, :, 0:C] = jnp.where(column == 0, left, pltpu.roll(row, 1, 0)).astype(jnp.bfloat16)
        h3[at + q, h, :, C:2 * C] = row.astype(jnp.bfloat16)
        h3[at + q, h, :, 2 * C:] = jnp.where(column == own - 1, right, pltpu.roll(row, own - 1, 0)).astype(jnp.bfloat16)
        return carry

    lax.fori_loop(0, 2 * H1, step, 0)


def feature_rows(h3, k2, bias, o_ref, ready):
    H1, own, C = h3.shape[1], h3.shape[2], h3.shape[3] // 3
    H0 = H1 - 2
    acc = jnp.zeros((2 * H0 * own, C), jnp.float32)
    for a in range(3):
        ready(a)
        for b in range(3):
            lhs = h3[a:a + 2, b:b + H0].reshape(2 * H0 * own, 3 * C)
            acc += jnp.dot(lhs, k2[a, b].reshape(3 * C, C), preferred_element_type=jnp.float32)
    o_ref[...] = leaky(acc + bias).astype(jnp.bfloat16).reshape(2, H0, own, C)


def fetched(k1h, k2h, k1, k2, sems):
    copies = [pltpu.make_async_copy(k1h.at[a], k1.at[a], sems.at[a]) for a in range(3)]
    copies += [pltpu.make_async_copy(k2h.at[a], k2.at[a], sems.at[3 + a]) for a in range(3)]
    for copy in copies:
        copy.start()
    return copies


def near_kernel(sides, info, xc, xn, k1h, b1, k2h, b2, o_ref, keep, x3, ef, e3, eb, h3, raw, k1, k2, sems):
    copies = fetched(k1h, k2h, k1, k2, sems)
    D, H, own = xc.shape[0], xc.shape[1], xc.shape[2] - 4
    odd = info[6]
    scratch = (x3, ef, e3, eb)
    spread(xc, D, 2 * odd, sides, info, *scratch)
    spread(xn, 2, D * (1 - odd), sides, info, *scratch)

    @pl.when(info[7] > 0)
    def _():
        clear(2, D * (1 - odd), x3, eb)

    def step(t, carry):
        def ready(a):
            @pl.when(t == 0)
            def _():
                copies[a].wait()
        hidden_sums(2 * t, sides, x3, eb, k1, b1[...], raw, ready)
        hidden_rows(2 * t, info[0] - 1 + 2 * (1 - odd) + 2 * t, sides, info, own, H, raw, h3)
        return carry

    lax.fori_loop(0, D // 2, step, 0)
    keep[...] = h3[pl.ds((D - 2) * odd, 2)]
    for a in range(3):
        copies[3 + a].wait()

    @pl.when(info[5] > 0)
    def _():
        feature_rows(h3, k2, b2[...], o_ref, lambda a: None)


def far_kernel(sides, info, xc, xf, keep, k1h, b1, k2h, b2, o_ref, x3, ef, e3, eb, h3, raw, k1, k2, sems):
    copies = fetched(k1h, k2h, k1, k2, sems)
    D, H, own = xc.shape[0], xc.shape[1], xc.shape[2] - 4
    odd = info[6]
    scratch = (x3, ef, e3, eb)
    spread(xc.at[pl.ds((D - 2) * odd, 2)], 2, 2 * (1 - odd), sides, info, *scratch)
    spread(xf, 2, 2 * odd, sides, info, *scratch)

    @pl.when(info[8] > 0)
    def _():
        clear(2, 2 * odd, x3, eb)

    h3[pl.ds(2 * (1 - odd), 2)] = keep[...]

    hidden_sums(0, sides, x3, eb, k1, b1[...], raw, lambda a: copies[a].wait())
    hidden_rows(2 * odd, info[0] - 1 + D * odd, sides, info, own, H, raw, h3)

    feature_rows(h3, k2, b2[...], o_ref, lambda a: copies[3 + a].wait())


def kernel_call(kernel, name, rows, sides, xc, near, operands):
    D, H, Wp, C = xc.shape
    own = Wp - 4
    out = [jax.ShapeDtypeStruct((2, H - 4, own, C), jnp.bfloat16)]
    scratch = [
        pltpu.VMEM((rows, H, own, 3 * C), jnp.bfloat16),
        pltpu.VMEM((sides, C // 128, H * 8, 128), jnp.float32),
        pltpu.VMEM((sides, 2 * H, 3 * C), jnp.float32),
        pltpu.VMEM((sides, 3, rows, H, 3 * C), jnp.bfloat16),
        pltpu.VMEM((4, H - 2, own, 3 * C), jnp.bfloat16),
        pltpu.VMEM((2 * (H - 2) * own + sides * 2 * H, C), jnp.float32),
        pltpu.VMEM((3, 3, 3, C, C), jnp.bfloat16),
        pltpu.VMEM((3, 3, 3, C, C), jnp.bfloat16),
        pltpu.SemaphoreType.DMA((6,)),
    ]
    specs = [SMEM] + [VMEM] * (len(operands) - 1)
    specs[-4] = specs[-2] = HBM
    if near:
        out += [jax.ShapeDtypeStruct((2, H - 2, own, 3 * C), jnp.bfloat16)]
    hid = (rows - 2) * (H - 2) * own
    return pl.pallas_call(
        functools.partial(kernel, sides),
        out_shape=out,
        in_specs=specs,
        out_specs=[VMEM] * len(out),
        scratch_shapes=scratch,
        compiler_params=pltpu.CompilerParams(vmem_limit_bytes=56 * 2**20),
        cost_estimate=pl.CostEstimate(flops=2 * 27 * C * C * (hid + 2 * (H - 4) * own), bytes_accessed=2**20, transcendentals=0),
        name=name,
    )(*operands)


def body(volume, kernel_one, bias_one, kernel_two, bias_two):
    b1, b2 = bias_one.reshape(1, -1), bias_two.reshape(1, -1)
    d, h, f = (lax.axis_index(a) for a in ("depth", "height", "filt"))
    nd, nh, nf = (lax.axis_size(a) for a in ("depth", "height", "filt"))
    rows = volume.shape[0]
    odd = d % 2
    info = jnp.stack([
        d * rows, jnp.int32(nd * rows), (h == 0).astype(jnp.int32), (h == nh - 1).astype(jnp.int32), f, jnp.int32(nf), odd,
        jnp.logical_and(odd == 0, d == nd - 1).astype(jnp.int32),
        jnp.where(odd == 1, d == nd - 1, d == 0).astype(jnp.int32),
    ])
    sides = 1 if nf == 2 else 2

    tall = gathered(volume, "filt", "height")
    near, far = exchange(tall[:2], tall[-2:], "depth")
    out_near, keep = kernel_call(near_kernel, "near", rows + 2, sides, tall, True, (info, tall, near, kernel_one, b1, kernel_two, b2))
    shard = volume.shape[3]
    near_parts = swapped(lambda i: lax.dynamic_slice_in_dim(out_near, i * shard, shard, 3), "filt")
    out_far, = kernel_call(far_kernel, "far", 4, sides, tall, False, (info, tall, far, keep, kernel_one, b1, kernel_two, b2))
    far_parts = swapped(lambda i: lax.dynamic_slice_in_dim(out_far, i * shard, shard, 3), "filt")
    out_near, out_far = by_origin(near_parts, "filt", 2), by_origin(far_parts, "filt", 2)
    return jnp.where(odd == 1, jnp.concatenate([out_near, out_far], 0), jnp.concatenate([out_far, out_near], 0))


def solution(mesh):
    in_specs = (P("depth", "height", None, "filt"), P(), P(), P(), P())
    out_specs = P("depth", "height", None, "filt")
    return jax.shard_map(body, mesh=mesh, in_specs=in_specs, out_specs=out_specs, check_vma=False)
```

time: 50.4 us -> 48.6 us (0.964)
  the two profiles are of different devices: /device:TPU:18 before, /device:TPU:1 now
where the time goes in v3:
time: 48.6 us; the launch traced here: 48.3 us
  Pallas kernels  19.1 us (39%)
  starting transfers between devices  15.4 us (32%)
  waiting for transfers between devices  8.19 us (17%)
  local copies, waits for them, and re-layouts  4.12 us (8%)
  other arithmetic  1.33 us (3%)
    pallas_call x2, Pallas kernels, kernel_call(): pl.pallas_call(functools.partial(kernel, sides), out_shape=out, in_specs=...  19.1 us
    ppermute x4, starting transfers between devices, gathered(): to.append(lax.ppermute(edge, (rows, columns), moves))  7.93 us
    ppermute x1, waiting for transfers between devices, gathered(): lax.ppermute(windows[s], columns, [(i, (i + s) % nc) for i in range(nc)])  3.21 us
    ppermute x1, starting transfers between devices, exchange(): two = lax.ppermute(jnp.where(odd, last, first), axis, far)  3.04 us
    ppermute x4, waiting for transfers between devices, gathered(): to.append(lax.ppermute(edge, (rows, columns), moves))  2.66 us
    ppermute x2, waiting for transfers between devices, swapped(): lax.ppermute(piece((index + s) % peers), axis, [(i, (i + s) % peers) for...  2.31 us
    ppermute x1, starting transfers between devices, exchange(): one = lax.ppermute(jnp.where(odd, first, last), axis, near)  1.67 us
    ppermute x2, starting transfers between devices, swapped(): lax.ppermute(piece((index + s) % peers), axis, [(i, (i + s) % peers) for...  1.53 us
  transfers between devices with their start and end apart: 9, of which 5 were waited for; matrix products, arithmetic and copies ran while one was open for 2% of the time, Pallas kernels for 22%

profile of v3, /device:TPU:1, one launch (start us, length us, event | category | flops | bytes accessed | tf_op | source)
XLA Modules:
  0.0 48.3 jit_solution(4055363981265373507)
XLA Ops:
  0.0 1.1 %pad_dynamic-slice_fusion = (bf16[4,4,36,128]{3,2,1,0:T(8,128)(2,1)S(1)}, bf16[4,4,36,128]{3,2,1,0:T(8,128)(2,1)S(1)}) fusion(s32[]{:T(128)S(6)} %select_n.151, bf16[4,4,64,128]{3,2,1,0:T(8,128)(2,1)} %param.5, s32[]{:T(128)S(6)} %select_n.149), kind=kLoop, calls=%fused_computation.4 | loop fusion | bytes 557064 | tf_op jit(solution)/shard_map/dynamic_slice | solution.py:73
  1.2 2.2 %collective-permute-start = (bf16[4,2,36,128]{3,2,1,0:T(8,128)(2,1)S(1)}, bf16[4,2,36,128]{3,2,1,0:T(8,128)(2,1)S(1)}, u32[]{:S(2)}, u32[]{:S(2)}) collective-permute-start(bf16[4,2,36,128]{3,2,1,0:T(8,128)(2,1)S(1)} %get-tuple-element.19), channel_id=1, source_target_pairs={{0,2},{1,3},{4,6},{5,7},{2,0},{3,1},{6,4},{7,5},{8,10},{9,11},{12,... | collective-permute-start | bytes 221192 | tf_op jit(solution)/shard_map/ppermute | solution.py:83
  3.3 0.7 %collective-permute-start.2 = (bf16[4,2,36,128]{3,2,1,0:T(8,128)(2,1)S(1)}, bf16[4,2,36,128]{3,2,1,0:T(8,128)(2,1)S(1)}, u32[]{:S(2)}, u32[]{:S(2)}) collective-permute-start(bf16[4,2,36,128]{3,2,1,0:T(8,128)(2,1)S(1)} %get-tuple-element.20), channel_id=1, source_target_pairs={{2,4},{3,5},{4,2},{5,3},{0,0},{1,1},{6,6},{7,7},{10,12},{11,13},{1... | collective-permute-start | bytes 221192 | tf_op jit(solution)/shard_map/ppermute | solution.py:83
  4.0 4.9 %collective-permute-start.1 = (bf16[4,2,36,128]{3,2,1,0:T(8,128)(2,1)S(1)}, bf16[4,2,36,128]{3,2,1,0:T(8,128)(2,1)S(1)}, u32[]{:S(2)}, u32[]{:S(2)}) collective-permute-start(bf16[4,2,36,128]{3,2,1,0:T(8,128)(2,1)S(1)} %get-tuple-element.17), channel_id=1, source_target_pairs={{0,3},{1,2},{4,7},{5,6},{2,1},{3,0},{6,5},{7,4},{8,11},{9,10},{12,... | collective-permute-start | bytes 221192 | tf_op jit(solution)/shard_map/ppermute | solution.py:83
  8.9 0.2 collective-permute-start.3
  9.1 1.2 %collective-permute-start.4 = (bf16[4,4,36,128]{3,2,1,0:T(8,128)(2,1)S(1)}, bf16[4,4,36,128]{3,2,1,0:T(8,128)(2,1)S(1)}, u32[]{:S(2)}, u32[]{:S(2)}) collective-permute-start(bf16[4,4,36,128]{3,2,1,0:T(8,128)(2,1)S(1)} %get-tuple-element.10), channel_id=1, source_target_pairs={{0,1},{1,0},{2,3},{3,2},{4,5},{5,4},{6,7},{7,6},{8,9},{9,8},{10,11... | collective-permute-start | bytes 442376 | tf_op jit(solution)/shard_map/ppermute | solution.py:78
  10.4 0.0 collective-permute-done
  10.4 0.0 collective-permute-done.2
  10.4 0.4 collective-permute-done.1
  10.7 2.3 %collective-permute-done.3 = bf16[4,2,36,128]{3,2,1,0:T(8,128)(2,1)S(1)} collective-permute-done((bf16[4,2,36,128]{3,2,1,0:T(8,128)(2,1)S(1)}, bf16[4,2,36,128]{3,2,1,0:T(8,128)(2,1)S(1)}, u32[]{:S(2)}, u32[]{:S(2)}) %collective-permute-start.3) | collective-permute-done | bytes 73760 | tf_op jit(solution)/shard_map/ppermute | solution.py:83
  13.0 0.1 select_select_fusion
  13.2 0.1 select_select_fusion.1
  13.3 3.2 %collective-permute-done.4 = bf16[4,4,36,128]{3,2,1,0:T(8,128)(2,1)S(1)} collective-permute-done((bf16[4,4,36,128]{3,2,1,0:T(8,128)(2,1)S(1)}, bf16[4,4,36,128]{3,2,1,0:T(8,128)(2,1)S(1)}, u32[]{:S(2)}, u32[]{:S(2)}) %collective-permute-start.4) | collective-permute-done | bytes 147488 | tf_op jit(solution)/shard_map/ppermute | solution.py:78
  16.5 0.1 maximum_select_fusion
  16.6 0.1 pad_maximum_fusion.xc
  16.7 0.0 copy-start
  16.8 1.7 %collective-permute-start.5 = (bf16[2,8,36,256]{3,2,1,0:T(8,128)(2,1)S(1)}, bf16[2,8,36,256]{3,2,1,0:T(8,128)(2,1)S(1)}, u32[]{:S(2)}, u32[]{:S(2)}) collective-permute-start(bf16[2,8,36,256]{3,2,1,0:T(8,128)(2,1)S(1)} %get-tuple-element.13), channel_id=1, source_target_pairs={{0,8},{16,24},{8,0},{24,16},{1,9},{17,25},{9,1},{25,17},{2,10},{18... | collective-permute-start | bytes 884744 | tf_op jit(solution)/shard_map/ppermute | solution.py:31
  18.4 0.7 %stack.47.info = s32[9]{0:T(128)} concatenate(s32[1]{0:T(128)} %bitcast, s32[1]{0:T(128)} %constant.57.clone.1, s32[1]{0:T(128)} %bitcast.1, s32[1]{0:T(128)} %bitcast.2, s32[1]{0:T(128)} %bitcast.3, s32[1]{0:T(128)} %constant.59.clone.1, s32[1]{0:T(128)} %bitcast.4, s32[1]{0:T(128)} %bitcast.5, s32[1]{0:T(128)} %bitcast.6), dimensions={0} | concatenate | bytes 72 | tf_op jit(solution)/shard_map/stack | solution.py:268
  19.1 3.0 %collective-permute-start.7 = (bf16[2,8,36,256]{3,2,1,0:T(8,128)(2,1)S(1)}, bf16[2,8,36,256]{3,2,1,0:T(8,128)(2,1)S(1)}, u32[]{:S(2)}, u32[]{:S(2)}) collective-permute-start(bf16[2,8,36,256]{3,2,1,0:T(8,128)(2,1)S(1)} %get-tuple-element.14), channel_id=1, source_target_pairs={{8,16},{16,8},{0,0},{24,24},{9,17},{17,9},{1,1},{25,25},{10,18},{1... | collective-permute-start | bytes 884744 | tf_op jit(solution)/shard_map/ppermute | solution.py:32
  22.2 0.0 collective-permute-done.5.xn
  22.2 0.0 copy-start.3
  22.2 0.0 copy-done
  22.2 0.7 %copy-done.3 = bf16[2,8,36,256]{3,2,1,0:T(8,128)(2,1)} copy-done((bf16[2,8,36,256]{3,2,1,0:T(8,128)(2,1)}, bf16[2,8,36,256]{3,2,1,0:T(8,128)(2,1)S(1)}, u32[]{:S(2)}) %copy-start.3) | copy-done | bytes 294936
  22.9 10.7 %near.1 = (bf16[2,4,32,256]{3,2,1,0:T(8,128)(2,1)}, bf16[2,6,32,768]{3,2,1,0:T(8,128)(2,1)}) custom-call(s32[9]{0:T(128)} %stack.47.info, bf16[4,8,36,256]{3,2,1,0:T(8,128)(2,1)} %copy-done, bf16[2,8,36,256]{3,2,1,0:T(8,128)(2,1)} %copy-done.3, bf16[3,3,3,256,256]{4,3,2,1,0:T(8,128)(2,1)} %k1h.3, f32[1,256]{1,0:T(1,128)} %bitcast.9, ...), custom_call_target="tpu_custom_call" | custom-call | flops 3623878656 | bytes 1048576 | tf_op jit(solution)/shard_map/near/pallas_call | solution.py:250
  33.6 0.0 collective-permute-done.7.xf
  33.6 0.0 copy-start.1
  33.6 0.7 %copy-done.1 = bf16[2,8,36,256]{3,2,1,0:T(8,128)(2,1)} copy-done((bf16[2,8,36,256]{3,2,1,0:T(8,128)(2,1)}, bf16[2,8,36,256]{3,2,1,0:T(8,128)(2,1)S(1)}, u32[]{:S(2)}) %copy-start.1) | copy-done | bytes 294936
  34.3 0.0 copy-start.2
  34.3 8.4 %far.1 = bf16[2,4,32,256]{3,2,1,0:T(8,128)(2,1)} custom-call(s32[9]{0:T(128)} %stack.47.info, bf16[4,8,36,256]{3,2,1,0:T(8,128)(2,1)} %copy-done, bf16[2,8,36,256]{3,2,1,0:T(8,128)(2,1)} %copy-done.1, bf16[2,6,32,768]{3,2,1,0:T(8,128)(2,1)} %get-tuple-element.12.keep, bf16[3,3,3,256,256]{4,3,2,1,0:T(8,128)(2,1)} %k1h.3, f32[1,256]{1,0:T(1,128)} %bitcast.10, ...), custom_call_target="tpu_custom_call" | custom-call | flops 2264924160 | bytes 1048576 | tf_op jit(solution)/shard_map/far/pallas_call | solution.py:250
  42.8 0.0 copy-done.2
  42.8 0.9 %constant_dynamic-slice_fusion.1 = (bf16[2,4,32,128]{3,2,1,0:T(8,128)(2,1)S(1)}, bf16[2,4,32,128]{3,2,1,0:T(8,128)(2,1)S(1)}, bf16[2,4,32,128]{3,2,1,0:T(8,128)(2,1)S(1)}, bf16[2,4,32,128]{3,2,1,0:T(8,128)(2,1)S(1)}) fusion(bf16[2,4,32,256]{3,2,1,0:T(8,128)(2,1)} %far.1, s32[]{:T(128)S(6)} %select_n.167, s32[]{:T(128)S(6)} %select_n.168, ...), kind=kLoop, calls=%fused_computation.18 | loop fusion | bytes 524296 | tf_op jit(solution)/shard_map/dynamic_slice | solution.py:281
  43.7 0.3 collective-permute-start.8
  44.0 1.2 %collective-permute-start.6 = (bf16[2,4,32,128]{3,2,1,0:T(8,128)(2,1)S(1)}, bf16[2,4,32,128]{3,2,1,0:T(8,128)(2,1)S(1)}, u32[]{:S(2)}, u32[]{:S(2)}) collective-permute-start(bf16[2,4,32,128]{3,2,1,0:T(8,128)(2,1)S(1)} %get-tuple-element.25), channel_id=1, source_target_pairs={{0,1},{1,0},{2,3},{3,2},{4,5},{5,4},{6,7},{7,6},{8,9},{9,8},{10,11... | collective-permute-start | bytes 196616 | tf_op jit(solution)/shard_map/ppermute | solution.py:59
  45.2 1.6 %collective-permute-done.8 = bf16[2,4,32,128]{3,2,1,0:T(8,128)(2,1)S(1)} collective-permute-done((bf16[2,4,32,128]{3,2,1,0:T(8,128)(2,1)S(1)}, bf16[2,4,32,128]{3,2,1,0:T(8,128)(2,1)S(1)}, u32[]{:S(2)}, u32[]{:S(2)}) %collective-permute-start.8) | collective-permute-done | bytes 65568 | tf_op jit(solution)/shard_map/ppermute | solution.py:59
  46.9 0.7 %collective-permute-done.6 = bf16[2,4,32,128]{3,2,1,0:T(8,128)(2,1)S(1)} collective-permute-done((bf16[2,4,32,128]{3,2,1,0:T(8,128)(2,1)S(1)}, bf16[2,4,32,128]{3,2,1,0:T(8,128)(2,1)S(1)}, u32[]{:S(2)}, u32[]{:S(2)}) %collective-permute-start.6) | collective-permute-done | bytes 65568 | tf_op jit(solution)/shard_map/ppermute | solution.py:59
  47.6 0.7 %maximum_select_fusion.1 = bf16[4,4,64,128]{3,2,1,0:T(8,128)(2,1)} fusion(bf16[2,4,64,128]{3,2,1,0:T(8,128)(2,1)S(1)} %maximum_select_fusion.5, bf16[2,4,64,128]{3,2,1,0:T(8,128)(2,1)S(1)} %maximum_select_fusion.4, pred[]{:T(512)S(6)} %eq.43), kind=kLoop, calls=%fused_computation.6 | loop fusion | flops 393216 | bytes 524289 | tf_op jit(solution)/shard_map/jit(_where)/select_n | solution.py:283
  (5 shorter events, 0.2 us)
Async XLA Ops:
  1.2 9.2 %collective-permute-start = (bf16[4,2,36,128]{3,2,1,0:T(8,128)(2,1)S(1)}, bf16[4,2,36,128]{3,2,1,0:T(8,128)(2,1)S(1)}, u32[]{:S(2)}, u32[]{:S(2)}) collective-permute-start(bf16[4,2,36,128]{3,2,1,0:T(8,128)(2,1)S(1)} %get-tuple-element.19), channel_id=1, source_target_pairs={{0,2},{1,3},{4,6},{5,7},{2,0},{3,1},{6,4},{7,5},{8,10},{9,11},{12,... | collective-permute-start | bytes 221192 | tf_op jit(solution)/shard_map/ppermute | solution.py:83
  3.3 7.0 %collective-permute-start.2 = (bf16[4,2,36,128]{3,2,1,0:T(8,128)(2,1)S(1)}, bf16[4,2,36,128]{3,2,1,0:T(8,128)(2,1)S(1)}, u32[]{:S(2)}, u32[]{:S(2)}) collective-permute-start(bf16[4,2,36,128]{3,2,1,0:T(8,128)(2,1)S(1)} %get-tuple-element.20), channel_id=1, source_target_pairs={{2,4},{3,5},{4,2},{5,3},{0,0},{1,1},{6,6},{7,7},{10,12},{11,13},{1... | collective-permute-start | bytes 221192 | tf_op jit(solution)/shard_map/ppermute | solution.py:83
  4.0 6.7 %collective-permute-start.1 = (bf16[4,2,36,128]{3,2,1,0:T(8,128)(2,1)S(1)}, bf16[4,2,36,128]{3,2,1,0:T(8,128)(2,1)S(1)}, u32[]{:S(2)}, u32[]{:S(2)}) collective-permute-start(bf16[4,2,36,128]{3,2,1,0:T(8,128)(2,1)S(1)} %get-tuple-element.17), channel_id=1, source_target_pairs={{0,3},{1,2},{4,7},{5,6},{2,1},{3,0},{6,5},{7,4},{8,11},{9,10},{12,... | collective-permute-start | bytes 221192 | tf_op jit(solution)/shard_map/ppermute | solution.py:83
  8.9 4.1 %collective-permute-start.3 = (bf16[4,2,36,128]{3,2,1,0:T(8,128)(2,1)S(1)}, bf16[4,2,36,128]{3,2,1,0:T(8,128)(2,1)S(1)}, u32[]{:S(2)}, u32[]{:S(2)}) collective-permute-start(bf16[4,2,36,128]{3,2,1,0:T(8,128)(2,1)S(1)} %get-tuple-element.18), channel_id=1, source_target_pairs={{2,5},{3,4},{4,3},{5,2},{0,1},{1,0},{6,7},{7,6},{10,13},{11,12},{1... | collective-permute-start | bytes 221192 | tf_op jit(solution)/shard_map/ppermute | solution.py:83
  9.1 7.4 %collective-permute-start.4 = (bf16[4,4,36,128]{3,2,1,0:T(8,128)(2,1)S(1)}, bf16[4,4,36,128]{3,2,1,0:T(8,128)(2,1)S(1)}, u32[]{:S(2)}, u32[]{:S(2)}) collective-permute-start(bf16[4,4,36,128]{3,2,1,0:T(8,128)(2,1)S(1)} %get-tuple-element.10), channel_id=1, source_target_pairs={{0,1},{1,0},{2,3},{3,2},{4,5},{5,4},{6,7},{7,6},{8,9},{9,8},{10,11... | collective-permute-start | bytes 442376 | tf_op jit(solution)/shard_map/ppermute | solution.py:78
  16.7 5.5 %copy-start = (bf16[4,8,36,256]{3,2,1,0:T(8,128)(2,1)}, bf16[4,8,36,256]{3,2,1,0:T(8,128)(2,1)S(1)}, u32[]{:S(2)}) copy-start(bf16[4,8,36,256]{3,2,1,0:T(8,128)(2,1)S(1)} %pad_maximum_fusion.xc) | copy-start | bytes 1769476
  16.8 5.4 %collective-permute-start.5 = (bf16[2,8,36,256]{3,2,1,0:T(8,128)(2,1)S(1)}, bf16[2,8,36,256]{3,2,1,0:T(8,128)(2,1)S(1)}, u32[]{:S(2)}, u32[]{:S(2)}) collective-permute-start(bf16[2,8,36,256]{3,2,1,0:T(8,128)(2,1)S(1)} %get-tuple-element.13), channel_id=1, source_target_pairs={{0,8},{16,24},{8,0},{24,16},{1,9},{17,25},{9,1},{25,17},{2,10},{18... | collective-permute-start | bytes 884744 | tf_op jit(solution)/shard_map/ppermute | solution.py:31
  19.1 14.5 %collective-permute-start.7 = (bf16[2,8,36,256]{3,2,1,0:T(8,128)(2,1)S(1)}, bf16[2,8,36,256]{3,2,1,0:T(8,128)(2,1)S(1)}, u32[]{:S(2)}, u32[]{:S(2)}) collective-permute-start(bf16[2,8,36,256]{3,2,1,0:T(8,128)(2,1)S(1)} %get-tuple-element.14), channel_id=1, source_target_pairs={{8,16},{16,8},{0,0},{24,24},{9,17},{17,9},{1,1},{25,25},{10,18},{1... | collective-permute-start | bytes 884744 | tf_op jit(solution)/shard_map/ppermute | solution.py:32
  22.2 0.7 %copy-start.3 = (bf16[2,8,36,256]{3,2,1,0:T(8,128)(2,1)}, bf16[2,8,36,256]{3,2,1,0:T(8,128)(2,1)S(1)}, u32[]{:S(2)}) copy-start(bf16[2,8,36,256]{3,2,1,0:T(8,128)(2,1)S(1)} %collective-permute-done.5.xn) | copy-start | bytes 884740
  33.6 0.7 %copy-start.1 = (bf16[2,8,36,256]{3,2,1,0:T(8,128)(2,1)}, bf16[2,8,36,256]{3,2,1,0:T(8,128)(2,1)S(1)}, u32[]{:S(2)}) copy-start(bf16[2,8,36,256]{3,2,1,0:T(8,128)(2,1)S(1)} %collective-permute-done.7.xf) | copy-start | bytes 884740
  34.3 8.4 %copy-start.2 = (bf16[2,4,32,256]{3,2,1,0:T(8,128)(2,1)S(1)}, bf16[2,4,32,256]{3,2,1,0:T(8,128)(2,1)}, u32[]{:S(2)}) copy-start(bf16[2,4,32,256]{3,2,1,0:T(8,128)(2,1)} %get-tuple-element.11) | copy-start | bytes 393220
  43.7 3.2 %collective-permute-start.8 = (bf16[2,4,32,128]{3,2,1,0:T(8,128)(2,1)S(1)}, bf16[2,4,32,128]{3,2,1,0:T(8,128)(2,1)S(1)}, u32[]{:S(2)}, u32[]{:S(2)}) collective-permute-start(bf16[2,4,32,128]{3,2,1,0:T(8,128)(2,1)S(1)} %get-tuple-element.24), channel_id=1, source_target_pairs={{0,1},{1,0},{2,3},{3,2},{4,5},{5,4},{6,7},{7,6},{8,9},{9,8},{10,11... | collective-permute-start | bytes 196616 | tf_op jit(solution)/shard_map/ppermute | solution.py:59
  44.0 3.6 %collective-permute-start.6 = (bf16[2,4,32,128]{3,2,1,0:T(8,128)(2,1)S(1)}, bf16[2,4,32,128]{3,2,1,0:T(8,128)(2,1)S(1)}, u32[]{:S(2)}, u32[]{:S(2)}) collective-permute-start(bf16[2,4,32,128]{3,2,1,0:T(8,128)(2,1)S(1)} %get-tuple-element.25), channel_id=1, source_target_pairs={{0,1},{1,0},{2,3},{3,2},{4,5},{5,4},{6,7},{7,6},{8,9},{9,8},{10,11... | collective-permute-start | bytes 196616 | tf_op jit(solution)/shard_map/ppermute | solution.py:59

commit v4 on v3

--- a/solution.py
+++ b/solution.py
@@ -8,7 +8,6 @@
 from jax.sharding import PartitionSpec as P
 
 VMEM = pl.BlockSpec(memory_space=pltpu.VMEM)
-SMEM = pl.BlockSpec(memory_space=pltpu.SMEM)
 HBM = pl.BlockSpec(memory_space=pltpu.HBM)
 
 
@@ -90,7 +89,7 @@
     H, Wp, C = source.shape[1:]
     own = Wp - 4
 
-    def step(d, carry):
+    def step(d):
         x, row = source[d], at + d
         for c in range(3):
             x3[row, :, :, c * C:(c + 1) * C] = x[:, 1 + c:1 + c + own, :]
@@ -105,9 +104,9 @@
                     e3[s, 0:H, c * C + l:c * C + l + 128] = ef[s, l // 128, pl.ds(c, H, stride=8), :]
             for b in range(3):
                 eb[s, b, row] = e3[s, b:b + H, :].astype(jnp.bfloat16)
-        return carry
-
-    lax.fori_loop(0, rows, step, 0)
+
+    for d in range(rows):
+        step(d)
 
 
 def clear(rows, at, x3, eb):
@@ -139,7 +138,7 @@
     column = lax.broadcasted_iota(jnp.int32, (own, C), 0)
     none = jnp.zeros((1, C), jnp.float32)
 
-    def step(i, carry):
+    def step(i):
         q, h = i // H1, i % H1
         ok = jnp.logical_and(depth + q >= 0, depth + q < info[1])
         ok = jnp.logical_and(ok, jnp.logical_or(h > 0, info[2] == 0))
@@ -151,9 +150,9 @@
         h3[at + q, h, :, 0:C] = jnp.where(column == 0, left, pltpu.roll(row, 1, 0)).astype(jnp.bfloat16)
         h3[at + q, h, :, C:2 * C] = row.astype(jnp.bfloat16)
         h3[at + q, h, :, 2 * C:] = jnp.where(column == own - 1, right, pltpu.roll(row, own - 1, 0)).astype(jnp.bfloat16)
-        return carry
-
-    lax.fori_loop(0, 2 * H1, step, 0)
+
+    for i in range(2 * H1):
+        step(i)
 
 
 def feature_rows(h3, k2, bias, o_ref, ready):
@@ -168,17 +167,111 @@
     o_ref[...] = leaky(acc + bias).astype(jnp.bfloat16).reshape(2, H0, own, C)
 
 
-def fetched(k1h, k2h, k1, k2, sems):
+def spread(source, rows, at, sides, info, x3, ef, e3, eb):
+    H, Wp, C = source.shape[1:]
+    own = Wp - 4
+
+    def step(d):
+        x, row = source[d], at + d
+        for c in range(3):
+            x3[row, :, :, c * C:(c + 1) * C] = x[:, 1 + c:1 + c + own, :]
+        for s in range(sides):
+            low, high = x[:, 0:3, :], x[:, Wp - 3:Wp, :]
+            pick = jnp.where(info[4] == 0, high, low) if sides == 1 else (low, high)[s]
+            pick = pick.astype(jnp.float32)
+            for l in range(0, C, 128):
+                for h in range(H):
+                    ef[s, l // 128, pl.ds(h * 8, 3), :] = pick[h, :, l:l + 128]
+                for c in range(3):
+                    e3[s, 0:H, c * C + l:c * C + l + 128] = ef[s, l // 128, pl.ds(c, H, stride=8), :]
+            for b in range(3):
+                eb[s, b, row] = e3[s, b:b + H, :].astype(jnp.bfloat16)
+
+    for d in range(rows):
+        step(d)
+
+
+def clear(rows, at, x3, eb):
+    for d in range(rows):
+        x3[at + d] = jnp.zeros(x3.shape[1:], x3.dtype)
+        for s in range(eb.shape[0]):
+            for b in range(3):
+                eb[s, b, at + d] = jnp.zeros(eb.shape[3:], eb.dtype)
+
+
+def hidden_sums(d, sides, x3, eb, k1, bias, raw, ready):
+    H, own, C = x3.shape[1], x3.shape[2], x3.shape[3] // 3
+    H1 = H - 2
+    main = 2 * H1 * own
+    acc = jnp.zeros((main + sides * 2 * H, C), jnp.float32)
+    for a in range(3):
+        ready(a)
+        for b in range(3):
+            lhs = [x3[pl.ds(d + a, 2), b:b + H1].reshape(main, 3 * C)]
+            lhs += [eb[s, b, pl.ds(d + a, 2)].reshape(2 * H, 3 * C) for s in range(sides)]
+            acc += jnp.dot(jnp.concatenate(lhs, 0), k1[a, b].reshape(3 * C, C), preferred_element_type=jnp.float32)
+    raw[...] = leaky(acc + bias)
+
+
+def hidden_rows(at, depth, sides, info, own, H, raw, h3):
+    C = raw.shape[1]
+    H1 = H - 2
+    main = 2 * H1 * own
+    column = lax.broadcasted_iota(jnp.int32, (own, C), 0)
+    none = jnp.zeros((1, C), jnp.float32)
+
+    def step(i):
+        q, h = i // H1, i % H1
+        ok = jnp.logical_and(depth + q >= 0, depth + q < info[1])
+        ok = jnp.logical_and(ok, jnp.logical_or(h > 0, info[2] == 0))
+        ok = jnp.logical_and(ok, jnp.logical_or(h < H1 - 1, info[3] == 0))
+        row = jnp.where(ok, raw[pl.ds(pl.multiple_of(i * own, 8), own), :], 0.0)
+        ends = [raw[pl.ds(main + (s * 2 + q) * H + h, 1), :] for s in range(sides)]
+        left = jnp.where(jnp.logical_and(ok, info[4] > 0), ends[0], none)
+        right = jnp.where(jnp.logical_and(ok, info[4] < info[5] - 1), ends[sides - 1], none)
+        h3[at + q, h, :, 0:C] = jnp.where(column == 0, left, pltpu.roll(row, 1, 0)).astype(jnp.bfloat16)
+        h3[at + q, h, :, C:2 * C] = row.astype(jnp.bfloat16)
+        h3[at + q, h, :, 2 * C:] = jnp.where(column == own - 1, right, pltpu.roll(row, own - 1, 0)).astype(jnp.bfloat16)
+
+    for i in range(2 * H1):
+        step(i)
+
+
+def feature_rows(h3, k2, bias, o_ref, ready):
+    H1, own, C = h3.shape[1], h3.shape[2], h3.shape[3] // 3
+    H0 = H1 - 2
+    acc = jnp.zeros((2 * H0 * own, C), jnp.float32)
+    for a in range(3):
+        ready(a)
+        for b in range(3):
+            lhs = h3[a:a + 2, b:b + H0].reshape(2 * H0 * own, 3 * C)
+            acc += jnp.dot(lhs, k2[a, b].reshape(3 * C, C), preferred_element_type=jnp.float32)
+    o_ref[...] = leaky(acc + bias).astype(jnp.bfloat16).reshape(2, H0, own, C)
+
+
+def places(rows):
+    d, h, f = (lax.axis_index(a) for a in ("depth", "height", "filt"))
+    nd, nh, nf = (lax.axis_size(a) for a in ("depth", "height", "filt"))
+    odd = lax.rem(d, 2)
+    end = (d == nd - 1).astype(jnp.int32)
+    start = (d == 0).astype(jnp.int32)
+    return (d * rows, nd * rows, (h == 0).astype(jnp.int32), (h == nh - 1).astype(jnp.int32), f, nf, odd,
+            end * (1 - odd), jnp.where(odd == 1, end, start))
+
+
+def near_kernel(sides, xc, xn, k1h, b1, k2h, b2, o_ref, keep, k1, k2, x3, ef, e3, eb, h3, raw, sems):
     copies = [pltpu.make_async_copy(k1h.at[a], k1.at[a], sems.at[a]) for a in range(3)]
     copies += [pltpu.make_async_copy(k2h.at[a], k2.at[a], sems.at[3 + a]) for a in range(3)]
-    for copy in copies:
+    for copy in copies[:2]:
         copy.start()
-    return copies
-
-
-def near_kernel(sides, info, xc, xn, k1h, b1, k2h, b2, o_ref, keep, x3, ef, e3, eb, h3, raw, k1, k2, sems):
-    copies = fetched(k1h, k2h, k1, k2, sems)
+
+    def take(i):
+        copies[i].wait()
+        if i + 2 < len(copies):
+            copies[i + 2].start()
+
     D, H, own = xc.shape[0], xc.shape[1], xc.shape[2] - 4
+    info = places(D)
     odd = info[6]
     scratch = (x3, ef, e3, eb)
     spread(xc, D, 2 * odd, sides, info, *scratch)
@@ -188,28 +281,21 @@
     def _():
         clear(2, D * (1 - odd), x3, eb)
 
-    def step(t, carry):
-        def ready(a):
-            @pl.when(t == 0)
-            def _():
-                copies[a].wait()
-        hidden_sums(2 * t, sides, x3, eb, k1, b1[...], raw, ready)
-        hidden_rows(2 * t, info[0] - 1 + 2 * (1 - odd) + 2 * t, sides, info, own, H, raw, h3)
-        return carry
-
-    lax.fori_loop(0, D // 2, step, 0)
+    for t in range(0, D, 2):
+        hidden_sums(t, sides, x3, eb, k1, b1[...], raw, (lambda a: take(a)) if t == 0 else (lambda a: None))
+        hidden_rows(t, info[0] - 1 + 2 * (1 - odd) + t, sides, info, own, H, raw, h3)
     keep[...] = h3[pl.ds((D - 2) * odd, 2)]
     for a in range(3):
-        copies[3 + a].wait()
-
-    @pl.when(info[5] > 0)
+        take(3 + a)
+
+    @pl.when(odd >= 0)
     def _():
         feature_rows(h3, k2, b2[...], o_ref, lambda a: None)
 
 
-def far_kernel(sides, info, xc, xf, keep, k1h, b1, k2h, b2, o_ref, x3, ef, e3, eb, h3, raw, k1, k2, sems):
-    copies = fetched(k1h, k2h, k1, k2, sems)
+def far_kernel(sides, xc, xf, keep, k1, b1, k2, b2, o_ref, x3, ef, e3, eb, h3, raw):
     D, H, own = xc.shape[0], xc.shape[1], xc.shape[2] - 4
+    info = places(D)
     odd = info[6]
     scratch = (x3, ef, e3, eb)
     spread(xc.at[pl.ds((D - 2) * odd, 2)], 2, 2 * (1 - odd), sides, info, *scratch)
@@ -221,15 +307,20 @@
 
     h3[pl.ds(2 * (1 - odd), 2)] = keep[...]
 
-    hidden_sums(0, sides, x3, eb, k1, b1[...], raw, lambda a: copies[a].wait())
+    @pl.when(odd >= 0)
+    def _():
+        hidden_sums(0, sides, x3, eb, k1, b1[...], raw, lambda a: None)
     hidden_rows(2 * odd, info[0] - 1 + D * odd, sides, info, own, H, raw, h3)
 
-    feature_rows(h3, k2, b2[...], o_ref, lambda a: copies[3 + a].wait())
+    @pl.when(odd >= 0)
+    def _():
+        feature_rows(h3, k2, b2[...], o_ref, lambda a: None)
 
 
 def kernel_call(kernel, name, rows, sides, xc, near, operands):
     D, H, Wp, C = xc.shape
     own = Wp - 4
+    weights = jax.ShapeDtypeStruct((3, 3, 3, C, C), jnp.bfloat16)
     out = [jax.ShapeDtypeStruct((2, H - 4, own, C), jnp.bfloat16)]
     scratch = [
         pltpu.VMEM((rows, H, own, 3 * C), jnp.bfloat16),
@@ -238,14 +329,12 @@
         pltpu.VMEM((sides, 3, rows, H, 3 * C), jnp.bfloat16),
         pltpu.VMEM((4, H - 2, own, 3 * C), jnp.bfloat16),
         pltpu.VMEM((2 * (H - 2) * own + sides * 2 * H, C), jnp.float32),
-        pltpu.VMEM((3, 3, 3, C, C), jnp.bfloat16),
-        pltpu.VMEM((3, 3, 3, C, C), jnp.bfloat16),
-        pltpu.SemaphoreType.DMA((6,)),
     ]
-    specs = [SMEM] + [VMEM] * (len(operands) - 1)
-    specs[-4] = specs[-2] = HBM
+    specs = [VMEM] * len(operands)
     if near:
-        out += [jax.ShapeDtypeStruct((2, H - 2, own, 3 * C), jnp.bfloat16)]
+        out += [jax.ShapeDtypeStruct((2, H - 2, own, 3 * C), jnp.bfloat16), weights, weights]
+        scratch.append(pltpu.SemaphoreType.DMA((6,)))
+        specs[2] = specs[4] = HBM
     hid = (rows - 2) * (H - 2) * own
     return pl.pallas_call(
         functools.partial(kernel, sides),
@@ -253,7 +342,7 @@
         in_specs=specs,
         out_specs=[VMEM] * len(out),
         scratch_shapes=scratch,
-        compiler_params=pltpu.CompilerParams(vmem_limit_bytes=56 * 2**20),
+        compiler_params=pltpu.CompilerParams(vmem_limit_bytes=(43 if near else 24) * 2**20),
         cost_estimate=pl.CostEstimate(flops=2 * 27 * C * C * (hid + 2 * (H - 4) * own), bytes_accessed=2**20, transcendentals=0),
         name=name,
     )(*operands)
@@ -261,23 +350,15 @@
 
 def body(volume, kernel_one, bias_one, kernel_two, bias_two):
     b1, b2 = bias_one.reshape(1, -1), bias_two.reshape(1, -1)
-    d, h, f = (lax.axis_index(a) for a in ("depth", "height", "filt"))
-    nd, nh, nf = (lax.axis_size(a) for a in ("depth", "height", "filt"))
-    rows = volume.shape[0]
-    odd = d % 2
-    info = jnp.stack([
-        d * rows, jnp.int32(nd * rows), (h == 0).astype(jnp.int32), (h == nh - 1).astype(jnp.int32), f, jnp.int32(nf), odd,
-        jnp.logical_and(odd == 0, d == nd - 1).astype(jnp.int32),
-        jnp.where(odd == 1, d == nd - 1, d == 0).astype(jnp.int32),
-    ])
-    sides = 1 if nf == 2 else 2
+    rows, odd = volume.shape[0], lax.axis_index("depth") % 2
+    sides = 1 if lax.axis_size("filt") == 2 else 2
 
     tall = gathered(volume, "filt", "height")
     near, far = exchange(tall[:2], tall[-2:], "depth")
-    out_near, keep = kernel_call(near_kernel, "near", rows + 2, sides, tall, True, (info, tall, near, kernel_one, b1, kernel_two, b2))
+    out_near, keep, k1, k2 = kernel_call(near_kernel, "near", rows + 2, sides, tall, True, (tall, near, kernel_one, b1, kernel_two, b2))
     shard = volume.shape[3]
     near_parts = swapped(lambda i: lax.dynamic_slice_in_dim(out_near, i * shard, shard, 3), "filt")
-    out_far, = kernel_call(far_kernel, "far", 4, sides, tall, False, (info, tall, far, keep, kernel_one, b1, kernel_two, b2))
+    out_far, = kernel_call(far_kernel, "far", 4, sides, tall, False, (tall, far, keep, k1, b1, k2, b2))
     far_parts = swapped(lambda i: lax.dynamic_slice_in_dim(out_far, i * shard, shard, 3), "filt")
     out_near, out_far = by_origin(near_parts, "filt", 2), by_origin(far_parts, "filt", 2)
     return jnp.where(odd == 1, jnp.concatenate([out_near, out_far], 0), jnp.concatenate([out_far, out_near], 0))

time: 48.6 us -> 39.2 us (0.81)
  Pallas kernels: 19.1 us -> 12.3 us
  local copies, waits for them, and re-layouts: 4.12 us -> 1.22 us
    pallas_call x2, Pallas kernels: 19.1 us -> 12.3 us  [kernel_call(): pl.pallas_call(functools.partial(kernel, sides), out_shape=out, in_specs=...]
    unnamed x8 -> x4, local copies, waits for them, and re-layouts: 1.41 us -> 0.01 us
    dynamic_slice x1, local copies, waits for them, and re-layouts: 0.91 us -> 0.06 us  [body(): lax.dynamic_slice_in_dim(out_far, i * shard, shard, 3)]
    another operation x1 -> x0, local copies, waits for them, and re-layouts: 0.67 us -> none  [body(): jnp.stack([d * rows, jnp.int32(nd * rows), (h == 0).astype(jnp.int32), (h...]
  transfers between devices with their start and end apart: 9 -> 9, of which waited for: 5 -> 5; matrix products, arithmetic and copies ran while one was open for 2% -> 1% of each run, Pallas kernels for 22% -> 23%
where the time goes in v4:
time: 39.2 us; the launch traced here: 39 us
  starting transfers between devices  15.4 us (39%)
  Pallas kernels  12.3 us (31%)
  waiting for transfers between devices  8.65 us (22%)
  other arithmetic  1.33 us (3%)
  local copies, waits for them, and re-layouts  1.22 us (3%)
    pallas_call x2, Pallas kernels, kernel_call(): pl.pallas_call(functools.partial(kernel, sides), out_shape=out, in_specs=...  12.3 us
    ppermute x4, starting transfers between devices, gathered(): to.append(lax.ppermute(edge, (rows, columns), moves))  7.93 us
    ppermute x1, waiting for transfers between devices, gathered(): lax.ppermute(windows[s], columns, [(i, (i + s) % nc) for i in range(nc)])  3.21 us
    ppermute x1, starting transfers between devices, exchange(): two = lax.ppermute(jnp.where(odd, last, first), axis, far)  3.03 us
    ppermute x2, waiting for transfers between devices, swapped(): lax.ppermute(piece((index + s) % peers), axis, [(i, (i + s) % peers) for...  2.78 us
    ppermute x4, waiting for transfers between devices, gathered(): to.append(lax.ppermute(edge, (rows, columns), moves))  2.66 us
    ppermute x1, starting transfers between devices, exchange(): one = lax.ppermute(jnp.where(odd, first, last), axis, near)  1.67 us
    ppermute x2, starting transfers between devices, swapped(): lax.ppermute(piece((index + s) % peers), axis, [(i, (i + s) % peers) for...  1.53 us
  transfers between devices with their start and end apart: 9, of which 5 were waited for; matrix products, arithmetic and copies ran while one was open for 1% of the time, Pallas kernels for 23%

profile of v4, /device:TPU:1, one launch (start us, length us, event | category | flops | bytes accessed | tf_op | source)
XLA Modules:
  0.0 39.0 jit_solution(2638349301908060400)
XLA Ops:
  0.0 0.0 copy-start.1
  0.0 0.0 copy-start
  0.0 1.2 %pad_dynamic-slice_fusion = (bf16[4,4,36,128]{3,2,1,0:T(8,128)(2,1)S(1)}, bf16[4,4,36,128]{3,2,1,0:T(8,128)(2,1)S(1)}) fusion(s32[]{:T(128)S(6)} %select_n.146, bf16[4,4,64,128]{3,2,1,0:T(8,128)(2,1)} %param.5, s32[]{:T(128)S(6)} %select_n.144), kind=kLoop, calls=%fused_computation.4 | loop fusion | bytes 557064 | tf_op jit(solution)/shard_map/dynamic_slice | solution.py:72
  1.2 2.2 %collective-permute-start = (bf16[4,2,36,128]{3,2,1,0:T(8,128)(2,1)S(1)}, bf16[4,2,36,128]{3,2,1,0:T(8,128)(2,1)S(1)}, u32[]{:S(2)}, u32[]{:S(2)}) collective-permute-start(bf16[4,2,36,128]{3,2,1,0:T(8,128)(2,1)S(1)} %get-tuple-element.23), channel_id=1, source_target_pairs={{0,2},{1,3},{4,6},{5,7},{2,0},{3,1},{6,4},{7,5},{8,10},{9,11},{12,... | collective-permute-start | bytes 221192 | tf_op jit(solution)/shard_map/ppermute | solution.py:82
  3.4 0.7 %collective-permute-start.2 = (bf16[4,2,36,128]{3,2,1,0:T(8,128)(2,1)S(1)}, bf16[4,2,36,128]{3,2,1,0:T(8,128)(2,1)S(1)}, u32[]{:S(2)}, u32[]{:S(2)}) collective-permute-start(bf16[4,2,36,128]{3,2,1,0:T(8,128)(2,1)S(1)} %get-tuple-element.24), channel_id=1, source_target_pairs={{2,4},{3,5},{4,2},{5,3},{0,0},{1,1},{6,6},{7,7},{10,12},{11,13},{1... | collective-permute-start | bytes 221192 | tf_op jit(solution)/shard_map/ppermute | solution.py:82
  4.1 4.9 %collective-permute-start.1 = (bf16[4,2,36,128]{3,2,1,0:T(8,128)(2,1)S(1)}, bf16[4,2,36,128]{3,2,1,0:T(8,128)(2,1)S(1)}, u32[]{:S(2)}, u32[]{:S(2)}) collective-permute-start(bf16[4,2,36,128]{3,2,1,0:T(8,128)(2,1)S(1)} %get-tuple-element.21), channel_id=1, source_target_pairs={{0,3},{1,2},{4,7},{5,6},{2,1},{3,0},{6,5},{7,4},{8,11},{9,10},{12,... | collective-permute-start | bytes 221192 | tf_op jit(solution)/shard_map/ppermute | solution.py:82
  8.9 0.2 collective-permute-start.3
  9.1 1.2 %collective-permute-start.4 = (bf16[4,4,36,128]{3,2,1,0:T(8,128)(2,1)S(1)}, bf16[4,4,36,128]{3,2,1,0:T(8,128)(2,1)S(1)}, u32[]{:S(2)}, u32[]{:S(2)}) collective-permute-start(bf16[4,4,36,128]{3,2,1,0:T(8,128)(2,1)S(1)} %get-tuple-element.12), channel_id=1, source_target_pairs={{0,1},{1,0},{2,3},{3,2},{4,5},{5,4},{6,7},{7,6},{8,9},{9,8},{10,11... | collective-permute-start | bytes 442376 | tf_op jit(solution)/shard_map/ppermute | solution.py:77
  10.4 0.0 collective-permute-done
  10.4 0.0 collective-permute-done.2
  10.4 0.4 collective-permute-done.1
  10.8 2.3 %collective-permute-done.3 = bf16[4,2,36,128]{3,2,1,0:T(8,128)(2,1)S(1)} collective-permute-done((bf16[4,2,36,128]{3,2,1,0:T(8,128)(2,1)S(1)}, bf16[4,2,36,128]{3,2,1,0:T(8,128)(2,1)S(1)}, u32[]{:S(2)}, u32[]{:S(2)}) %collective-permute-start.3) | collective-permute-done | bytes 73760 | tf_op jit(solution)/shard_map/ppermute | solution.py:82
  13.1 0.1 select_select_fusion
  13.2 0.1 select_select_fusion.1
  13.3 3.2 %collective-permute-done.4 = bf16[4,4,36,128]{3,2,1,0:T(8,128)(2,1)S(1)} collective-permute-done((bf16[4,4,36,128]{3,2,1,0:T(8,128)(2,1)S(1)}, bf16[4,4,36,128]{3,2,1,0:T(8,128)(2,1)S(1)}, u32[]{:S(2)}, u32[]{:S(2)}) %collective-permute-start.4) | collective-permute-done | bytes 147488 | tf_op jit(solution)/shard_map/ppermute | solution.py:77
  16.5 0.1 maximum_select_fusion
  16.6 0.1 pad_maximum_fusion.xc
  16.8 1.7 %collective-permute-start.5 = (bf16[2,8,36,256]{3,2,1,0:T(8,128)(2,1)S(1)}, bf16[2,8,36,256]{3,2,1,0:T(8,128)(2,1)S(1)}, u32[]{:S(2)}, u32[]{:S(2)}) collective-permute-start(bf16[2,8,36,256]{3,2,1,0:T(8,128)(2,1)S(1)} %get-tuple-element.17), channel_id=1, source_target_pairs={{0,8},{16,24},{8,0},{24,16},{1,9},{17,25},{9,1},{25,17},{2,10},{18... | collective-permute-start | bytes 884744 | tf_op jit(solution)/shard_map/ppermute | solution.py:30
  18.5 3.0 %collective-permute-start.7 = (bf16[2,8,36,256]{3,2,1,0:T(8,128)(2,1)S(1)}, bf16[2,8,36,256]{3,2,1,0:T(8,128)(2,1)S(1)}, u32[]{:S(2)}, u32[]{:S(2)}) collective-permute-start(bf16[2,8,36,256]{3,2,1,0:T(8,128)(2,1)S(1)} %get-tuple-element.18), channel_id=1, source_target_pairs={{8,16},{16,8},{0,0},{24,24},{9,17},{17,9},{1,1},{25,25},{10,18},{1... | collective-permute-start | bytes 884744 | tf_op jit(solution)/shard_map/ppermute | solution.py:31
  21.5 0.0 collective-permute-done.5.xn
  21.5 0.0 copy-done.1
  21.5 0.0 copy-done
  21.5 9.0 %near.1 = (bf16[2,4,32,256]{3,2,1,0:T(8,128)(2,1)S(1)}, bf16[2,6,32,768]{3,2,1,0:T(8,128)(2,1)S(1)}, bf16[3,3,3,256,256]{4,3,2,1,0:T(8,128)(2,1)S(1)}, bf16[3,3,3,256,256]{4,3,2,1,0:T(8,128)(2,1)S(1)}) custom-call(bf16[4,8,36,256]{3,2,1,0:T(8,128)(2,1)S(1)} %pad_maximum_fusion.xc, bf16[2,8,36,256]{3,2,1,0:T(8,128)(2,1)S(1)} %collective-permute-done.5.xn, ...), custom_call_target="tpu_custom_call" | custom-call | flops 3623878656 | bytes 1048576 | tf_op jit(solution)/shard_map/near/pallas_call | solution.py:339
  30.5 0.0 collective-permute-done.7.xf
  30.5 3.3 %far.1 = bf16[2,4,32,256]{3,2,1,0:T(8,128)(2,1)S(1)} custom-call(bf16[4,8,36,256]{3,2,1,0:T(8,128)(2,1)S(1)} %pad_maximum_fusion.xc, bf16[2,8,36,256]{3,2,1,0:T(8,128)(2,1)S(1)} %collective-permute-done.7.xf, bf16[2,6,32,768]{3,2,1,0:T(8,128)(2,1)S(1)} %get-tuple-element.14.keep, bf16[3,3,3,256,256]{4,3,2,1,0:T(8,128)(2,1)S(1)} %get-tuple-element.15.k1, ...), custom_call_target="tpu_custom_call" | custom-call | flops 2264924160 | bytes 1048576 | tf_op jit(solution)/shard_map/far/pallas_call | solution.py:339
  33.8 0.1 constant_dynamic-slice_fusion.1
  33.9 0.3 collective-permute-start.8
  34.2 1.2 %collective-permute-start.6 = (bf16[2,4,32,128]{3,2,1,0:T(8,128)(2,1)S(1)}, bf16[2,4,32,128]{3,2,1,0:T(8,128)(2,1)S(1)}, u32[]{:S(2)}, u32[]{:S(2)}) collective-permute-start(bf16[2,4,32,128]{3,2,1,0:T(8,128)(2,1)S(1)} %get-tuple-element.29), channel_id=1, source_target_pairs={{0,1},{1,0},{2,3},{3,2},{4,5},{5,4},{6,7},{7,6},{8,9},{9,8},{10,11... | collective-permute-start | bytes 196616 | tf_op jit(solution)/shard_map/ppermute | solution.py:58
  35.4 2.2 %collective-permute-done.8 = bf16[2,4,32,128]{3,2,1,0:T(8,128)(2,1)S(1)} collective-permute-done((bf16[2,4,32,128]{3,2,1,0:T(8,128)(2,1)S(1)}, bf16[2,4,32,128]{3,2,1,0:T(8,128)(2,1)S(1)}, u32[]{:S(2)}, u32[]{:S(2)}) %collective-permute-start.8) | collective-permute-done | bytes 65568 | tf_op jit(solution)/shard_map/ppermute | solution.py:58
  37.6 0.6 %collective-permute-done.6 = bf16[2,4,32,128]{3,2,1,0:T(8,128)(2,1)S(1)} collective-permute-done((bf16[2,4,32,128]{3,2,1,0:T(8,128)(2,1)S(1)}, bf16[2,4,32,128]{3,2,1,0:T(8,128)(2,1)S(1)}, u32[]{:S(2)}, u32[]{:S(2)}) %collective-permute-start.6) | collective-permute-done | bytes 65568 | tf_op jit(solution)/shard_map/ppermute | solution.py:58
  38.3 0.7 %maximum_select_fusion.1 = bf16[4,4,64,128]{3,2,1,0:T(8,128)(2,1)} fusion(bf16[2,4,64,128]{3,2,1,0:T(8,128)(2,1)S(1)} %maximum_select_fusion.5, bf16[2,4,64,128]{3,2,1,0:T(8,128)(2,1)S(1)} %maximum_select_fusion.4, pred[]{:T(512)S(6)} %eq.30), kind=kLoop, calls=%fused_computation.6 | loop fusion | flops 393216 | bytes 524289 | tf_op jit(solution)/shard_map/jit(_where)/select_n | solution.py:364
  (5 shorter events, 0.2 us)
Async XLA Ops:
  0.0 21.5 %copy-start.1 = (f32[256]{0:T(256)S(1)}, f32[256]{0:T(256)}, u32[]{:S(2)}) copy-start(f32[256]{0:T(256)} %param.9) | copy-start | bytes 3076
  0.0 21.5 %copy-start = (f32[256]{0:T(256)S(1)}, f32[256]{0:T(256)}, u32[]{:S(2)}) copy-start(f32[256]{0:T(256)} %param.7) | copy-start | bytes 3076
  1.2 9.2 %collective-permute-start = (bf16[4,2,36,128]{3,2,1,0:T(8,128)(2,1)S(1)}, bf16[4,2,36,128]{3,2,1,0:T(8,128)(2,1)S(1)}, u32[]{:S(2)}, u32[]{:S(2)}) collective-permute-start(bf16[4,2,36,128]{3,2,1,0:T(8,128)(2,1)S(1)} %get-tuple-element.23), channel_id=1, source_target_pairs={{0,2},{1,3},{4,6},{5,7},{2,0},{3,1},{6,4},{7,5},{8,10},{9,11},{12,... | collective-permute-start | bytes 221192 | tf_op jit(solution)/shard_map/ppermute | solution.py:82
  3.4 7.0 %collective-permute-start.2 = (bf16[4,2,36,128]{3,2,1,0:T(8,128)(2,1)S(1)}, bf16[4,2,36,128]{3,2,1,0:T(8,128)(2,1)S(1)}, u32[]{:S(2)}, u32[]{:S(2)}) collective-permute-start(bf16[4,2,36,128]{3,2,1,0:T(8,128)(2,1)S(1)} %get-tuple-element.24), channel_id=1, source_target_pairs={{2,4},{3,5},{4,2},{5,3},{0,0},{1,1},{6,6},{7,7},{10,12},{11,13},{1... | collective-permute-start | bytes 221192 | tf_op jit(solution)/shard_map/ppermute | solution.py:82
  4.1 6.7 %collective-permute-start.1 = (bf16[4,2,36,128]{3,2,1,0:T(8,128)(2,1)S(1)}, bf16[4,2,36,128]{3,2,1,0:T(8,128)(2,1)S(1)}, u32[]{:S(2)}, u32[]{:S(2)}) collective-permute-start(bf16[4,2,36,128]{3,2,1,0:T(8,128)(2,1)S(1)} %get-tuple-element.21), channel_id=1, source_target_pairs={{0,3},{1,2},{4,7},{5,6},{2,1},{3,0},{6,5},{7,4},{8,11},{9,10},{12,... | collective-permute-start | bytes 221192 | tf_op jit(solution)/shard_map/ppermute | solution.py:82
  8.9 4.1 %collective-permute-start.3 = (bf16[4,2,36,128]{3,2,1,0:T(8,128)(2,1)S(1)}, bf16[4,2,36,128]{3,2,1,0:T(8,128)(2,1)S(1)}, u32[]{:S(2)}, u32[]{:S(2)}) collective-permute-start(bf16[4,2,36,128]{3,2,1,0:T(8,128)(2,1)S(1)} %get-tuple-element.22), channel_id=1, source_target_pairs={{2,5},{3,4},{4,3},{5,2},{0,1},{1,0},{6,7},{7,6},{10,13},{11,12},{1... | collective-permute-start | bytes 221192 | tf_op jit(solution)/shard_map/ppermute | solution.py:82
  9.1 7.4 %collective-permute-start.4 = (bf16[4,4,36,128]{3,2,1,0:T(8,128)(2,1)S(1)}, bf16[4,4,36,128]{3,2,1,0:T(8,128)(2,1)S(1)}, u32[]{:S(2)}, u32[]{:S(2)}) collective-permute-start(bf16[4,4,36,128]{3,2,1,0:T(8,128)(2,1)S(1)} %get-tuple-element.12), channel_id=1, source_target_pairs={{0,1},{1,0},{2,3},{3,2},{4,5},{5,4},{6,7},{7,6},{8,9},{9,8},{10,11... | collective-permute-start | bytes 442376 | tf_op jit(solution)/shard_map/ppermute | solution.py:77
  16.8 4.7 %collective-permute-start.5 = (bf16[2,8,36,256]{3,2,1,0:T(8,128)(2,1)S(1)}, bf16[2,8,36,256]{3,2,1,0:T(8,128)(2,1)S(1)}, u32[]{:S(2)}, u32[]{:S(2)}) collective-permute-start(bf16[2,8,36,256]{3,2,1,0:T(8,128)(2,1)S(1)} %get-tuple-element.17), channel_id=1, source_target_pairs={{0,8},{16,24},{8,0},{24,16},{1,9},{17,25},{9,1},{25,17},{2,10},{18... | collective-permute-start | bytes 884744 | tf_op jit(solution)/shard_map/ppermute | solution.py:30
  18.5 12.0 %collective-permute-start.7 = (bf16[2,8,36,256]{3,2,1,0:T(8,128)(2,1)S(1)}, bf16[2,8,36,256]{3,2,1,0:T(8,128)(2,1)S(1)}, u32[]{:S(2)}, u32[]{:S(2)}) collective-permute-start(bf16[2,8,36,256]{3,2,1,0:T(8,128)(2,1)S(1)} %get-tuple-element.18), channel_id=1, source_target_pairs={{8,16},{16,8},{0,0},{24,24},{9,17},{17,9},{1,1},{25,25},{10,18},{1... | collective-permute-start | bytes 884744 | tf_op jit(solution)/shard_map/ppermute | solution.py:31
  33.9 3.7 %collective-permute-start.8 = (bf16[2,4,32,128]{3,2,1,0:T(8,128)(2,1)S(1)}, bf16[2,4,32,128]{3,2,1,0:T(8,128)(2,1)S(1)}, u32[]{:S(2)}, u32[]{:S(2)}) collective-permute-start(bf16[2,4,32,128]{3,2,1,0:T(8,128)(2,1)S(1)} %get-tuple-element.28), channel_id=1, source_target_pairs={{0,1},{1,0},{2,3},{3,2},{4,5},{5,4},{6,7},{7,6},{8,9},{9,8},{10,11... | collective-permute-start | bytes 196616 | tf_op jit(solution)/shard_map/ppermute | solution.py:58
  34.2 4.1 %collective-permute-start.6 = (bf16[2,4,32,128]{3,2,1,0:T(8,128)(2,1)S(1)}, bf16[2,4,32,128]{3,2,1,0:T(8,128)(2,1)S(1)}, u32[]{:S(2)}, u32[]{:S(2)}) collective-permute-start(bf16[2,4,32,128]{3,2,1,0:T(8,128)(2,1)S(1)} %get-tuple-element.29), channel_id=1, source_target_pairs={{0,1},{1,0},{2,3},{3,2},{4,5},{5,4},{6,7},{7,6},{8,9},{9,8},{10,11... | collective-permute-start | bytes 196616 | tf_op jit(solution)/shard_map/ppermute | solution.py:58

commit v5 on v4

--- a/solution.py
+++ b/solution.py
@@ -51,12 +51,10 @@
     return jnp.concatenate([stacked[order[c]] for c in range(peers)], dim)
 
 
-def swapped(piece, axis):
-    peers, index = lax.axis_size(axis), lax.axis_index(axis)
-    parts = [piece(index)]
-    for s in range(1, peers):
-        parts.append(lax.ppermute(piece((index + s) % peers), axis, [(i, (i + s) % peers) for i in range(peers)]))
-    return parts
+def swapped(pieces, axis):
+    peers = lax.axis_size(axis)
+    moves = [[(i, (i + s) % peers) for i in range(peers)] for s in range(peers)]
+    return [pieces[0]] + [lax.ppermute(pieces[s], axis, moves[s]) for s in range(1, peers)]
 
 
 def in_order(parts, axis):
@@ -117,18 +115,16 @@
                 eb[s, b, at + d] = jnp.zeros(eb.shape[3:], eb.dtype)
 
 
-def hidden_sums(d, sides, x3, eb, k1, bias, raw, ready):
+def hidden_sums(d, taps, sides, x3, eb, k1, acc):
     H, own, C = x3.shape[1], x3.shape[2], x3.shape[3] // 3
     H1 = H - 2
     main = 2 * H1 * own
-    acc = jnp.zeros((main + sides * 2 * H, C), jnp.float32)
-    for a in range(3):
-        ready(a)
+    for a in taps:
         for b in range(3):
-            lhs = [x3[pl.ds(d + a, 2), b:b + H1].reshape(main, 3 * C)]
-            lhs += [eb[s, b, pl.ds(d + a, 2)].reshape(2 * H, 3 * C) for s in range(sides)]
+            lhs = [x3[d + a:d + a + 2, b:b + H1].reshape(main, 3 * C)]
+            lhs += [eb[s, b, d + a:d + a + 2].reshape(2 * H, 3 * C) for s in range(sides)]
             acc += jnp.dot(jnp.concatenate(lhs, 0), k1[a, b].reshape(3 * C, C), preferred_element_type=jnp.float32)
-    raw[...] = leaky(acc + bias)
+    return acc
 
 
 def hidden_rows(at, depth, sides, info, own, H, raw, h3):
@@ -155,12 +151,11 @@
         step(i)
 
 
-def feature_rows(h3, k2, bias, o_ref, ready):
+def feature_rows(h3, k2, bias, o_ref):
     H1, own, C = h3.shape[1], h3.shape[2], h3.shape[3] // 3
     H0 = H1 - 2
     acc = jnp.zeros((2 * H0 * own, C), jnp.float32)
     for a in range(3):
-        ready(a)
         for b in range(3):
             lhs = h3[a:a + 2, b:b + H0].reshape(2 * H0 * own, 3 * C)
             acc += jnp.dot(lhs, k2[a, b].reshape(3 * C, C), preferred_element_type=jnp.float32)
@@ -199,18 +194,16 @@
                 eb[s, b, at + d] = jnp.zeros(eb.shape[3:], eb.dtype)
 
 
-def hidden_sums(d, sides, x3, eb, k1, bias, raw, ready):
+def hidden_sums(d, taps, sides, x3, eb, k1, acc):
     H, own, C = x3.shape[1], x3.shape[2], x3.shape[3] // 3
     H1 = H - 2
     main = 2 * H1 * own
-    acc = jnp.zeros((main + sides * 2 * H, C), jnp.float32)
-    for a in range(3):
-        ready(a)
+    for a in taps:
         for b in range(3):
-            lhs = [x3[pl.ds(d + a, 2), b:b + H1].reshape(main, 3 * C)]
-            lhs += [eb[s, b, pl.ds(d + a, 2)].reshape(2 * H, 3 * C) for s in range(sides)]
+            lhs = [x3[d + a:d + a + 2, b:b + H1].reshape(main, 3 * C)]
+            lhs += [eb[s, b, d + a:d + a + 2].reshape(2 * H, 3 * C) for s in range(sides)]
             acc += jnp.dot(jnp.concatenate(lhs, 0), k1[a, b].reshape(3 * C, C), preferred_element_type=jnp.float32)
-    raw[...] = leaky(acc + bias)
+    return acc
 
 
 def hidden_rows(at, depth, sides, info, own, H, raw, h3):
@@ -237,12 +230,11 @@
         step(i)
 
 
-def feature_rows(h3, k2, bias, o_ref, ready):
+def feature_rows(h3, k2, bias, o_ref):
     H1, own, C = h3.shape[1], h3.shape[2], h3.shape[3] // 3
     H0 = H1 - 2
     acc = jnp.zeros((2 * H0 * own, C), jnp.float32)
     for a in range(3):
-        ready(a)
         for b in range(3):
             lhs = h3[a:a + 2, b:b + H0].reshape(2 * H0 * own, 3 * C)
             acc += jnp.dot(lhs, k2[a, b].reshape(3 * C, C), preferred_element_type=jnp.float32)
@@ -261,14 +253,9 @@
 
 def near_kernel(sides, xc, xn, k1h, b1, k2h, b2, o_ref, keep, k1, k2, x3, ef, e3, eb, h3, raw, sems):
     copies = [pltpu.make_async_copy(k1h.at[a], k1.at[a], sems.at[a]) for a in range(3)]
-    copies += [pltpu.make_async_copy(k2h.at[a], k2.at[a], sems.at[3 + a]) for a in range(3)]
+    copies.append(pltpu.make_async_copy(k2h, k2, sems.at[3]))
     for copy in copies[:2]:
         copy.start()
-
-    def take(i):
-        copies[i].wait()
-        if i + 2 < len(copies):
-            copies[i + 2].start()
 
     D, H, own = xc.shape[0], xc.shape[1], xc.shape[2] - 4
     info = places(D)
@@ -281,16 +268,25 @@
     def _():
         clear(2, D * (1 - odd), x3, eb)
 
+    for a in range(3):
+        copies[a].wait()
+        if a < 2:
+            copies[a + 2].start()
+
+        @pl.when(odd >= 0)
+        def _():
+            for t in range(0, D, 2):
+                acc = jnp.zeros(raw.shape[1:], jnp.float32) if a == 0 else raw[t // 2]
+                raw[t // 2] = hidden_sums(t, [a], sides, x3, eb, k1, acc)
     for t in range(0, D, 2):
-        hidden_sums(t, sides, x3, eb, k1, b1[...], raw, (lambda a: take(a)) if t == 0 else (lambda a: None))
-        hidden_rows(t, info[0] - 1 + 2 * (1 - odd) + t, sides, info, own, H, raw, h3)
+        raw[t // 2] = leaky(raw[t // 2] + b1[...])
+        hidden_rows(t, info[0] - 1 + 2 * (1 - odd) + t, sides, info, own, H, raw.at[t // 2], h3)
     keep[...] = h3[pl.ds((D - 2) * odd, 2)]
-    for a in range(3):
-        take(3 + a)
+    copies[3].wait()
 
     @pl.when(odd >= 0)
     def _():
-        feature_rows(h3, k2, b2[...], o_ref, lambda a: None)
+        feature_rows(h3, k2, b2[...], o_ref)
 
 
 def far_kernel(sides, xc, xf, keep, k1, b1, k2, b2, o_ref, x3, ef, e3, eb, h3, raw):
@@ -309,12 +305,12 @@
 
     @pl.when(odd >= 0)
     def _():
-        hidden_sums(0, sides, x3, eb, k1, b1[...], raw, lambda a: None)
-    hidden_rows(2 * odd, info[0] - 1 + D * odd, sides, info, own, H, raw, h3)
+        raw[0] = leaky(hidden_sums(0, range(3), sides, x3, eb, k1, jnp.zeros(raw.shape[1:], jnp.float32)) + b1[...])
+    hidden_rows(2 * odd, info[0] - 1 + D * odd, sides, info, own, H, raw.at[0], h3)
 
     @pl.when(odd >= 0)
     def _():
-        feature_rows(h3, k2, b2[...], o_ref, lambda a: None)
+        feature_rows(h3, k2, b2[...], o_ref)
 
 
 def kernel_call(kernel, name, rows, sides, xc, near, operands):
@@ -328,12 +324,12 @@
         pltpu.VMEM((sides, 2 * H, 3 * C), jnp.float32),
         pltpu.VMEM((sides, 3, rows, H, 3 * C), jnp.bfloat16),
         pltpu.VMEM((4, H - 2, own, 3 * C), jnp.bfloat16),
-        pltpu.VMEM((2 * (H - 2) * own + sides * 2 * H, C), jnp.float32),
+        pltpu.VMEM((rows // 2 - 1, 2 * (H - 2) * own + sides * 2 * H, C), jnp.float32),
     ]
     specs = [VMEM] * len(operands)
     if near:
         out += [jax.ShapeDtypeStruct((2, H - 2, own, 3 * C), jnp.bfloat16), weights, weights]
-        scratch.append(pltpu.SemaphoreType.DMA((6,)))
+        scratch.append(pltpu.SemaphoreType.DMA((4,)))
         specs[2] = specs[4] = HBM
     hid = (rows - 2) * (H - 2) * own
     return pl.pallas_call(
@@ -357,9 +353,13 @@
     near, far = exchange(tall[:2], tall[-2:], "depth")
     out_near, keep, k1, k2 = kernel_call(near_kernel, "near", rows + 2, sides, tall, True, (tall, near, kernel_one, b1, kernel_two, b2))
     shard = volume.shape[3]
-    near_parts = swapped(lambda i: lax.dynamic_slice_in_dim(out_near, i * shard, shard, 3), "filt")
+    def pieces(y):
+        f, n = lax.axis_index("filt"), lax.axis_size("filt")
+        return [lax.dynamic_slice_in_dim(y, (f + s) % n * shard, shard, 3) for s in range(n)]
+    near_pieces, keep = lax.optimization_barrier((pieces(out_near), keep))
+    near_parts = swapped(near_pieces, "filt")
     out_far, = kernel_call(far_kernel, "far", 4, sides, tall, False, (tall, far, keep, k1, b1, k2, b2))
-    far_parts = swapped(lambda i: lax.dynamic_slice_in_dim(out_far, i * shard, shard, 3), "filt")
+    far_parts = swapped(pieces(out_far), "filt")
     out_near, out_far = by_origin(near_parts, "filt", 2), by_origin(far_parts, "filt", 2)
     return jnp.where(odd == 1, jnp.concatenate([out_near, out_far], 0), jnp.concatenate([out_far, out_near], 0))
 

time: 39.2 us -> 35.5 us (0.906)
  the two profiles are of different devices: /device:TPU:1 before, /device:TPU:0 now
where the time goes in v5:
time: 35.5 us; the launch traced here: 35.4 us
  starting transfers between devices  14.1 us (40%)
  Pallas kernels  9.49 us (27%)
  waiting for transfers between devices  9.09 us (26%)
  other arithmetic  1.33 us (4%)
  local copies, waits for them, and re-layouts  1.23 us (3%)
    ppermute x4, starting transfers between devices, gathered(): to.append(lax.ppermute(edge, (rows, columns), moves))  9.67 us
    pallas_call x2, Pallas kernels, kernel_call(): pl.pallas_call(functools.partial(kernel, sides), out_shape=out, in_specs=...  9.49 us
    ppermute x4, waiting for transfers between devices, gathered(): to.append(lax.ppermute(edge, (rows, columns), moves))  3.35 us
    ppermute x2, waiting for transfers between devices, swapped(): lax.ppermute(pieces[s], axis, moves[s])  2.78 us
    ppermute x2, starting transfers between devices, swapped(): lax.ppermute(pieces[s], axis, moves[s])  2.16 us
    ppermute x1, waiting for transfers between devices, gathered(): lax.ppermute(windows[s], columns, [(i, (i + s) % nc) for i in range(nc)])  2.05 us
    ppermute x1, starting transfers between devices, gathered(): lax.ppermute(windows[s], columns, [(i, (i + s) % nc) for i in range(nc)])  1.52 us
    dynamic_slice x1, local copies, waits for them, and re-layouts, gathered(): lax.dynamic_slice_in_dim(padded, (c + s) % nc * own, own + 4, 2)  1.15 us
  transfers between devices with their start and end apart: 9, of which 5 were waited for; matrix products, arithmetic and copies ran while one was open for 1% of the time, Pallas kernels for 27%

profile of v5, /device:TPU:0, one launch (start us, length us, event | category | flops | bytes accessed | tf_op | source)
XLA Modules:
  0.0 35.4 jit_solution(8704773751771868249)
XLA Ops:
  0.0 0.0 copy-start.1
  0.0 0.0 copy-start
  0.0 1.2 %pad_dynamic-slice_fusion = (bf16[4,4,36,128]{3,2,1,0:T(8,128)(2,1)S(1)}, bf16[4,4,36,128]{3,2,1,0:T(8,128)(2,1)S(1)}) fusion(s32[]{:T(128)S(6)} %select_n.150, bf16[4,4,64,128]{3,2,1,0:T(8,128)(2,1)} %param.5, s32[]{:T(128)S(6)} %select_n.148), kind=kLoop, calls=%fused_computation.4 | loop fusion | bytes 557064 | tf_op jit(solution)/shard_map/dynamic_slice | solution.py:70
  1.2 3.1 %collective-permute-start = (bf16[4,2,36,128]{3,2,1,0:T(8,128)(2,1)S(1)}, bf16[4,2,36,128]{3,2,1,0:T(8,128)(2,1)S(1)}, u32[]{:S(2)}, u32[]{:S(2)}) collective-permute-start(bf16[4,2,36,128]{3,2,1,0:T(8,128)(2,1)S(1)} %get-tuple-element.29), channel_id=1, source_target_pairs={{0,2},{1,3},{4,6},{5,7},{2,0},{3,1},{6,4},{7,5},{8,10},{9,11},{12,... | collective-permute-start | bytes 221192 | tf_op jit(solution)/shard_map/ppermute | solution.py:80
  4.3 0.7 %collective-permute-start.2 = (bf16[4,2,36,128]{3,2,1,0:T(8,128)(2,1)S(1)}, bf16[4,2,36,128]{3,2,1,0:T(8,128)(2,1)S(1)}, u32[]{:S(2)}, u32[]{:S(2)}) collective-permute-start(bf16[4,2,36,128]{3,2,1,0:T(8,128)(2,1)S(1)} %get-tuple-element.30), channel_id=1, source_target_pairs={{2,4},{3,5},{4,2},{5,3},{0,0},{1,1},{6,6},{7,7},{10,12},{11,13},{1... | collective-permute-start | bytes 221192 | tf_op jit(solution)/shard_map/ppermute | solution.py:80
  5.0 5.4 %collective-permute-start.1 = (bf16[4,2,36,128]{3,2,1,0:T(8,128)(2,1)S(1)}, bf16[4,2,36,128]{3,2,1,0:T(8,128)(2,1)S(1)}, u32[]{:S(2)}, u32[]{:S(2)}) collective-permute-start(bf16[4,2,36,128]{3,2,1,0:T(8,128)(2,1)S(1)} %get-tuple-element.27), channel_id=1, source_target_pairs={{0,3},{1,2},{4,7},{5,6},{2,1},{3,0},{6,5},{7,4},{8,11},{9,10},{12,... | collective-permute-start | bytes 221192 | tf_op jit(solution)/shard_map/ppermute | solution.py:80
  10.4 0.5 %collective-permute-start.3 = (bf16[4,2,36,128]{3,2,1,0:T(8,128)(2,1)S(1)}, bf16[4,2,36,128]{3,2,1,0:T(8,128)(2,1)S(1)}, u32[]{:S(2)}, u32[]{:S(2)}) collective-permute-start(bf16[4,2,36,128]{3,2,1,0:T(8,128)(2,1)S(1)} %get-tuple-element.28), channel_id=1, source_target_pairs={{2,5},{3,4},{4,3},{5,2},{0,1},{1,0},{6,7},{7,6},{10,13},{11,12},{1... | collective-permute-start | bytes 221192 | tf_op jit(solution)/shard_map/ppermute | solution.py:80
  10.9 1.5 %collective-permute-start.4 = (bf16[4,4,36,128]{3,2,1,0:T(8,128)(2,1)S(1)}, bf16[4,4,36,128]{3,2,1,0:T(8,128)(2,1)S(1)}, u32[]{:S(2)}, u32[]{:S(2)}) collective-permute-start(bf16[4,4,36,128]{3,2,1,0:T(8,128)(2,1)S(1)} %get-tuple-element.15), channel_id=1, source_target_pairs={{0,1},{1,0},{2,3},{3,2},{4,5},{5,4},{6,7},{7,6},{8,9},{9,8},{10,11... | collective-permute-start | bytes 442376 | tf_op jit(solution)/shard_map/ppermute | solution.py:75
  12.4 0.0 collective-permute-done
  12.4 0.0 collective-permute-done.2
  12.4 0.5 %collective-permute-done.1 = bf16[4,2,36,128]{3,2,1,0:T(8,128)(2,1)S(1)} collective-permute-done((bf16[4,2,36,128]{3,2,1,0:T(8,128)(2,1)S(1)}, bf16[4,2,36,128]{3,2,1,0:T(8,128)(2,1)S(1)}, u32[]{:S(2)}, u32[]{:S(2)}) %collective-permute-start.1) | collective-permute-done | bytes 73760 | tf_op jit(solution)/shard_map/ppermute | solution.py:80
  12.9 2.9 %collective-permute-done.3 = bf16[4,2,36,128]{3,2,1,0:T(8,128)(2,1)S(1)} collective-permute-done((bf16[4,2,36,128]{3,2,1,0:T(8,128)(2,1)S(1)}, bf16[4,2,36,128]{3,2,1,0:T(8,128)(2,1)S(1)}, u32[]{:S(2)}, u32[]{:S(2)}) %collective-permute-start.3) | collective-permute-done | bytes 73760 | tf_op jit(solution)/shard_map/ppermute | solution.py:80
  15.8 0.1 select_select_fusion
  15.9 0.1 select_select_fusion.1
  16.0 2.0 %collective-permute-done.4 = bf16[4,4,36,128]{3,2,1,0:T(8,128)(2,1)S(1)} collective-permute-done((bf16[4,4,36,128]{3,2,1,0:T(8,128)(2,1)S(1)}, bf16[4,4,36,128]{3,2,1,0:T(8,128)(2,1)S(1)}, u32[]{:S(2)}, u32[]{:S(2)}) %collective-permute-start.4) | collective-permute-done | bytes 147488 | tf_op jit(solution)/shard_map/ppermute | solution.py:75
  18.1 0.1 maximum_select_fusion
  18.2 0.1 pad_maximum_fusion.xc
  18.3 0.1 collective-permute-start.5
  18.4 0.7 %collective-permute-start.7 = (bf16[2,8,36,256]{3,2,1,0:T(8,128)(2,1)S(1)}, bf16[2,8,36,256]{3,2,1,0:T(8,128)(2,1)S(1)}, u32[]{:S(2)}, u32[]{:S(2)}) collective-permute-start(bf16[2,8,36,256]{3,2,1,0:T(8,128)(2,1)S(1)} %get-tuple-element.24), channel_id=1, source_target_pairs={{8,16},{16,8},{0,0},{24,24},{9,17},{17,9},{1,1},{25,25},{10,18},{1... | collective-permute-start | bytes 884744 | tf_op jit(solution)/shard_map/ppermute | solution.py:31
  19.1 0.9 %collective-permute-done.5.xn = bf16[2,8,36,256]{3,2,1,0:T(8,128)(2,1)S(1)} collective-permute-done((bf16[2,8,36,256]{3,2,1,0:T(8,128)(2,1)S(1)}, bf16[2,8,36,256]{3,2,1,0:T(8,128)(2,1)S(1)}, u32[]{:S(2)}, u32[]{:S(2)}) %collective-permute-start.5) | collective-permute-done | bytes 294944 | tf_op jit(solution)/shard_map/ppermute | solution.py:30
  20.0 0.0 copy-done.1
  20.0 0.0 copy-done
  20.0 6.2 %near.1 = (bf16[2,4,32,256]{3,2,1,0:T(8,128)(2,1)S(1)}, bf16[2,6,32,768]{3,2,1,0:T(8,128)(2,1)S(1)}, bf16[3,3,3,256,256]{4,3,2,1,0:T(8,128)(2,1)S(1)}, bf16[3,3,3,256,256]{4,3,2,1,0:T(8,128)(2,1)S(1)}) custom-call(bf16[4,8,36,256]{3,2,1,0:T(8,128)(2,1)S(1)} %pad_maximum_fusion.xc, bf16[2,8,36,256]{3,2,1,0:T(8,128)(2,1)S(1)} %collective-permute-done.5.xn, ...), custom_call_target="tpu_custom_call" | custom-call | flops 3623878656 | bytes 1048576 | tf_op jit(solution)/shard_map/near/pallas_call | solution.py:335
  26.3 0.6 %collective-permute-start.6 = (bf16[2,4,32,128]{3,2,1,0:T(8,128)(2,1)S(1)}, bf16[2,4,32,128]{3,2,1,0:T(8,128)(2,1)S(1)}, u32[]{:S(2)}, u32[]{:S(2)}) collective-permute-start(bf16[2,4,32,128]{3,2,1,0:T(8,128)(2,1)S(1)} %get-tuple-element.19), channel_id=1, source_target_pairs={{0,1},{1,0},{2,3},{3,2},{4,5},{5,4},{6,7},{7,6},{8,9},{9,8},{10,11... | collective-permute-start | bytes 196616 | tf_op jit(solution)/shard_map/ppermute | solution.py:57
  26.8 0.0 collective-permute-done.7.xf
  26.8 3.3 %far.1 = bf16[2,4,32,256]{3,2,1,0:T(8,128)(2,1)S(1)} custom-call(bf16[4,8,36,256]{3,2,1,0:T(8,128)(2,1)S(1)} %pad_maximum_fusion.xc, bf16[2,8,36,256]{3,2,1,0:T(8,128)(2,1)S(1)} %collective-permute-done.7.xf, bf16[2,6,32,768]{3,2,1,0:T(8,128)(2,1)S(1)} %get-tuple-element.20.keep, bf16[3,3,3,256,256]{4,3,2,1,0:T(8,128)(2,1)S(1)} %get-tuple-element.21.k1, ...), custom_call_target="tpu_custom_call" | custom-call | flops 2264924160 | bytes 1048576 | tf_op jit(solution)/shard_map/far/pallas_call | solution.py:335
  30.2 1.6 %collective-permute-start.8 = (bf16[2,4,32,128]{3,2,1,0:T(8,128)(2,1)S(1)}, bf16[2,4,32,128]{3,2,1,0:T(8,128)(2,1)S(1)}, u32[]{:S(2)}, u32[]{:S(2)}) collective-permute-start(bf16[2,4,32,128]{3,2,1,0:T(8,128)(2,1)S(1)} %get-tuple-element.32), channel_id=1, source_target_pairs={{0,1},{1,0},{2,3},{3,2},{4,5},{5,4},{6,7},{7,6},{8,9},{9,8},{10,11... | collective-permute-start | bytes 196616 | tf_op jit(solution)/shard_map/ppermute | solution.py:57
  31.8 0.0 collective-permute-done.6
  31.8 2.8 %collective-permute-done.8 = bf16[2,4,32,128]{3,2,1,0:T(8,128)(2,1)S(1)} collective-permute-done((bf16[2,4,32,128]{3,2,1,0:T(8,128)(2,1)S(1)}, bf16[2,4,32,128]{3,2,1,0:T(8,128)(2,1)S(1)}, u32[]{:S(2)}, u32[]{:S(2)}) %collective-permute-start.8) | collective-permute-done | bytes 65568 | tf_op jit(solution)/shard_map/ppermute | solution.py:57
  34.6 0.7 %maximum_select_fusion.1 = bf16[4,4,64,128]{3,2,1,0:T(8,128)(2,1)} fusion(bf16[2,4,64,128]{3,2,1,0:T(8,128)(2,1)S(1)} %maximum_select_fusion.5, bf16[2,4,64,128]{3,2,1,0:T(8,128)(2,1)S(1)} %maximum_select_fusion.4, pred[]{:T(512)S(6)} %eq.32), kind=kLoop, calls=%fused_computation.6 | loop fusion | flops 393216 | bytes 524289 | tf_op jit(solution)/shard_map/jit(_where)/select_n | solution.py:364
  (7 shorter events, 0.2 us)
Async XLA Ops:
  0.0 20.0 %copy-start.1 = (f32[256]{0:T(256)S(1)}, f32[256]{0:T(256)}, u32[]{:S(2)}) copy-start(f32[256]{0:T(256)} %param.9) | copy-start | bytes 3076
  0.0 20.0 %copy-start = (f32[256]{0:T(256)S(1)}, f32[256]{0:T(256)}, u32[]{:S(2)}) copy-start(f32[256]{0:T(256)} %param.7) | copy-start | bytes 3076
  1.2 11.2 %collective-permute-start = (bf16[4,2,36,128]{3,2,1,0:T(8,128)(2,1)S(1)}, bf16[4,2,36,128]{3,2,1,0:T(8,128)(2,1)S(1)}, u32[]{:S(2)}, u32[]{:S(2)}) collective-permute-start(bf16[4,2,36,128]{3,2,1,0:T(8,128)(2,1)S(1)} %get-tuple-element.29), channel_id=1, source_target_pairs={{0,2},{1,3},{4,6},{5,7},{2,0},{3,1},{6,4},{7,5},{8,10},{9,11},{12,... | collective-permute-start | bytes 221192 | tf_op jit(solution)/shard_map/ppermute | solution.py:80
  4.3 8.1 %collective-permute-start.2 = (bf16[4,2,36,128]{3,2,1,0:T(8,128)(2,1)S(1)}, bf16[4,2,36,128]{3,2,1,0:T(8,128)(2,1)S(1)}, u32[]{:S(2)}, u32[]{:S(2)}) collective-permute-start(bf16[4,2,36,128]{3,2,1,0:T(8,128)(2,1)S(1)} %get-tuple-element.30), channel_id=1, source_target_pairs={{2,4},{3,5},{4,2},{5,3},{0,0},{1,1},{6,6},{7,7},{10,12},{11,13},{1... | collective-permute-start | bytes 221192 | tf_op jit(solution)/shard_map/ppermute | solution.py:80
  5.0 7.9 %collective-permute-start.1 = (bf16[4,2,36,128]{3,2,1,0:T(8,128)(2,1)S(1)}, bf16[4,2,36,128]{3,2,1,0:T(8,128)(2,1)S(1)}, u32[]{:S(2)}, u32[]{:S(2)}) collective-permute-start(bf16[4,2,36,128]{3,2,1,0:T(8,128)(2,1)S(1)} %get-tuple-element.27), channel_id=1, source_target_pairs={{0,3},{1,2},{4,7},{5,6},{2,1},{3,0},{6,5},{7,4},{8,11},{9,10},{12,... | collective-permute-start | bytes 221192 | tf_op jit(solution)/shard_map/ppermute | solution.py:80
  10.4 5.4 %collective-permute-start.3 = (bf16[4,2,36,128]{3,2,1,0:T(8,128)(2,1)S(1)}, bf16[4,2,36,128]{3,2,1,0:T(8,128)(2,1)S(1)}, u32[]{:S(2)}, u32[]{:S(2)}) collective-permute-start(bf16[4,2,36,128]{3,2,1,0:T(8,128)(2,1)S(1)} %get-tuple-element.28), channel_id=1, source_target_pairs={{2,5},{3,4},{4,3},{5,2},{0,1},{1,0},{6,7},{7,6},{10,13},{11,12},{1... | collective-permute-start | bytes 221192 | tf_op jit(solution)/shard_map/ppermute | solution.py:80
  10.9 7.2 %collective-permute-start.4 = (bf16[4,4,36,128]{3,2,1,0:T(8,128)(2,1)S(1)}, bf16[4,4,36,128]{3,2,1,0:T(8,128)(2,1)S(1)}, u32[]{:S(2)}, u32[]{:S(2)}) collective-permute-start(bf16[4,4,36,128]{3,2,1,0:T(8,128)(2,1)S(1)} %get-tuple-element.15), channel_id=1, source_target_pairs={{0,1},{1,0},{2,3},{3,2},{4,5},{5,4},{6,7},{7,6},{8,9},{9,8},{10,11... | collective-permute-start | bytes 442376 | tf_op jit(solution)/shard_map/ppermute | solution.py:75
  18.3 1.7 %collective-permute-start.5 = (bf16[2,8,36,256]{3,2,1,0:T(8,128)(2,1)S(1)}, bf16[2,8,36,256]{3,2,1,0:T(8,128)(2,1)S(1)}, u32[]{:S(2)}, u32[]{:S(2)}) collective-permute-start(bf16[2,8,36,256]{3,2,1,0:T(8,128)(2,1)S(1)} %get-tuple-element.23), channel_id=1, source_target_pairs={{0,8},{16,24},{8,0},{24,16},{1,9},{17,25},{9,1},{25,17},{2,10},{18... | collective-permute-start | bytes 884744 | tf_op jit(solution)/shard_map/ppermute | solution.py:30
  18.4 8.4 %collective-permute-start.7 = (bf16[2,8,36,256]{3,2,1,0:T(8,128)(2,1)S(1)}, bf16[2,8,36,256]{3,2,1,0:T(8,128)(2,1)S(1)}, u32[]{:S(2)}, u32[]{:S(2)}) collective-permute-start(bf16[2,8,36,256]{3,2,1,0:T(8,128)(2,1)S(1)} %get-tuple-element.24), channel_id=1, source_target_pairs={{8,16},{16,8},{0,0},{24,24},{9,17},{17,9},{1,1},{25,25},{10,18},{1... | collective-permute-start | bytes 884744 | tf_op jit(solution)/shard_map/ppermute | solution.py:31
  26.3 5.5 %collective-permute-start.6 = (bf16[2,4,32,128]{3,2,1,0:T(8,128)(2,1)S(1)}, bf16[2,4,32,128]{3,2,1,0:T(8,128)(2,1)S(1)}, u32[]{:S(2)}, u32[]{:S(2)}) collective-permute-start(bf16[2,4,32,128]{3,2,1,0:T(8,128)(2,1)S(1)} %get-tuple-element.19), channel_id=1, source_target_pairs={{0,1},{1,0},{2,3},{3,2},{4,5},{5,4},{6,7},{7,6},{8,9},{9,8},{10,11... | collective-permute-start | bytes 196616 | tf_op jit(solution)/shard_map/ppermute | solution.py:57
  30.2 4.4 %collective-permute-start.8 = (bf16[2,4,32,128]{3,2,1,0:T(8,128)(2,1)S(1)}, bf16[2,4,32,128]{3,2,1,0:T(8,128)(2,1)S(1)}, u32[]{:S(2)}, u32[]{:S(2)}) collective-permute-start(bf16[2,4,32,128]{3,2,1,0:T(8,128)(2,1)S(1)} %get-tuple-element.32), channel_id=1, source_target_pairs={{0,1},{1,0},{2,3},{3,2},{4,5},{5,4},{6,7},{7,6},{8,9},{9,8},{10,11... | collective-permute-start | bytes 196616 | tf_op jit(solution)/shard_map/ppermute | solution.py:57

commit v6 on v5

v6 whole, which is shorter than its diff:
```python
import functools

import jax
import jax.numpy as jnp
from jax import lax
from jax.experimental import pallas as pl
from jax.experimental.pallas import tpu as pltpu
from jax.sharding import PartitionSpec as P

VMEM = pl.BlockSpec(memory_space=pltpu.VMEM)
HBM = pl.BlockSpec(memory_space=pltpu.HBM)


def leaky(value):
    return jnp.where(value > 0, value, 0.3 * value)


def pairings(peers):
    rounds = []
    for start in (0, 1):
        pairs = [(i, i + 1) for i in range(start, peers - 1, 2)]
        busy = {i for pair in pairs for i in pair}
        rounds.append(pairs + [(j, i) for i, j in pairs] + [(i, i) for i in range(peers) if i not in busy])
    return rounds


def exchange(first, last, axis):
    odd = lax.axis_index(axis) % 2 == 1
    near, far = pairings(lax.axis_size(axis))
    one = lax.ppermute(jnp.where(odd, first, last), axis, near)
    two = lax.ppermute(jnp.where(odd, last, first), axis, far)
    return one, two


def beside(one, two, axis):
    peers, index = lax.axis_size(axis), lax.axis_index(axis)
    odd = index % 2 == 1
    before = jnp.where(odd, one, two)
    after = jnp.where(odd, two, one)
    before = jnp.where(index == 0, jnp.zeros_like(before), before)
    after = jnp.where(index == peers - 1, jnp.zeros_like(after), after)
    return before, after


def by_origin(parts, axis, dim):
    peers, index = lax.axis_size(axis), lax.axis_index(axis)
    if peers == 2:
        return jnp.where(index == 0, jnp.concatenate(parts, dim), jnp.concatenate(parts[::-1], dim))
    stacked = jnp.stack(parts)
    order = (index - jnp.arange(peers)) % peers
    return jnp.concatenate([stacked[order[c]] for c in range(peers)], dim)


def swapped(pieces, axis):
    peers = lax.axis_size(axis)
    moves = [[(i, (i + s) % peers) for i in range(peers)] for s in range(peers)]
    return [pieces[0]] + [lax.ppermute(pieces[s], axis, moves[s]) for s in range(1, peers)]


def in_order(parts, axis):
    return by_origin(parts, axis, 3)


def gathered(x, columns, rows):
    nc, nr = lax.axis_size(columns), lax.axis_size(rows)
    c, r = lax.axis_index(columns), lax.axis_index(rows)
    own = x.shape[2] // nc
    odd = r % 2 == 1
    padded = jnp.pad(x, ((0, 0), (0, 0), (2, 2), (0, 0)))
    windows = [lax.dynamic_slice_in_dim(padded, (c + s) % nc * own, own + 4, 2) for s in range(nc)]
    windows = lax.optimization_barrier(windows)
    parts, ones, twos = [windows[0]], [], []
    near, far = pairings(nr)
    for s in range(1, nc):
        parts.append(lax.ppermute(windows[s], columns, [(i, (i + s) % nc) for i in range(nc)]))
    for s in range(nc):
        first, last = parts[s][:, :2], parts[s][:, -2:]
        ones.append(lax.ppermute(jnp.where(odd, first, last), rows, near))
        twos.append(lax.ppermute(jnp.where(odd, last, first), rows, far))
    one, two = in_order(ones, columns), in_order(twos, columns)
    before, after = beside(one, two, rows)
    return jnp.concatenate([before, in_order(parts, columns), after], 1)


def spread(source, rows, at, sides, info, x3, ef, e3, eb):
    H, Wp, C = source.shape[1:]
    own = Wp - 4

    def step(d):
        x, row = source[d], at + d
        for c in range(3):
            x3[row, :, :, c * C:(c + 1) * C] = x[:, 1 + c:1 + c + own, :]
        for s in range(sides):
            low, high = x[:, 0:3, :], x[:, Wp - 3:Wp, :]
            pick = jnp.where(info[4] == 0, high, low) if sides == 1 else (low, high)[s]
            pick = pick.astype(jnp.float32)
            for l in range(0, C, 128):
                for h in range(H):
                    ef[s, l // 128, pl.ds(h * 8, 3), :] = pick[h, :, l:l + 128]
                for c in range(3):
                    e3[s, 0:H, c * C + l:c * C + l + 128] = ef[s, l // 128, pl.ds(c, H, stride=8), :]
            for b in range(3):
                eb[s, b, row] = e3[s, b:b + H, :].astype(jnp.bfloat16)

    for d in range(rows):
        step(d)


def clear(rows, at, x3, eb):
    for d in range(rows):
        x3[at + d] = jnp.zeros(x3.shape[1:], x3.dtype)
        for s in range(eb.shape[0]):
            for b in range(3):
                eb[s, b, at + d] = jnp.zeros(eb.shape[3:], eb.dtype)


def hidden_sums(d, taps, ends, x3, eb, k1, acc):
    H, own, C = x3.shape[1], x3.shape[2], x3.shape[3] // 3
    main = (H - 2) * own
    for a in taps:
        for b in range(3):
            lhs = [x3[d + a, b:b + H - 2].reshape(main, 3 * C)]
            if ends:
                lhs += [eb[s, b, a:a + ends].reshape(ends * H, 3 * C) for s in range(eb.shape[0])]
            acc += jnp.dot(jnp.concatenate(lhs, 0), k1[a, b].reshape(3 * C, C), preferred_element_type=jnp.float32)
    return acc


def hidden_rows(d, at, depth, sides, info, own, H, raw, ends, h3):
    C = raw.shape[2]
    count = ends.shape[0] // (sides * H)
    column = lax.broadcasted_iota(jnp.int32, (own, C), 0)
    none = jnp.zeros((1, C), jnp.float32)
    inside = jnp.logical_and(depth >= 0, depth < info[1])
    for h in range(H - 2):
        ok = inside
        if h == 0:
            ok = jnp.logical_and(ok, info[2] == 0)
        if h == H - 3:
            ok = jnp.logical_and(ok, info[3] == 0)
        row = jnp.where(ok, raw[d, h * own:(h + 1) * own, :], 0.0)
        edge = [ends[(s * count + d) * H + h:(s * count + d) * H + h + 1, :] for s in range(sides)]
        left = jnp.where(jnp.logical_and(ok, info[4] > 0), edge[0], none)
        right = jnp.where(jnp.logical_and(ok, info[4] < info[5] - 1), edge[sides - 1], none)
        h3[at, h, :, 0:C] = jnp.where(column == 0, left, pltpu.roll(row, 1, 0)).astype(jnp.bfloat16)
        h3[at, h, :, C:2 * C] = row.astype(jnp.bfloat16)
        h3[at, h, :, 2 * C:] = jnp.where(column == own - 1, right, pltpu.roll(row, own - 1, 0)).astype(jnp.bfloat16)


def hidden_part(d, taps, x3, eb, k1, bias, raw, ends):
    main, C = raw.shape[1:]
    size = ends.shape[0] if d == 0 else 0
    if taps[0] == 0:
        acc = jnp.zeros((main + size, C), jnp.float32)
    else:
        acc = jnp.concatenate([raw[d], ends[...]], 0) if size else raw[d]
    acc = hidden_sums(d, taps, raw.shape[0] if size else 0, x3, eb, k1, acc)
    if taps[-1] == 2:
        acc = leaky(acc + bias[...])
    raw[d] = acc[:main]
    if size:
        ends[...] = acc[main:]


def feature_sums(taps, h3, k2, acc):
    H1, own, C = h3.shape[1], h3.shape[2], h3.shape[3] // 3
    H0 = H1 - 2
    for a in taps:
        for b in range(3):
            lhs = h3[a:a + 2, b:b + H0].reshape(2 * H0 * own, 3 * C)
            acc += jnp.dot(lhs, k2[a, b].reshape(3 * C, C), preferred_element_type=jnp.float32)
    return acc


def features(acc, bias, o_ref):
    o_ref[...] = leaky(acc + bias[...]).astype(jnp.bfloat16).reshape(o_ref.shape)


def places(rows):
    d, h, f = (lax.axis_index(a) for a in ("depth", "height", "filt"))
    nd, nh, nf = (lax.axis_size(a) for a in ("depth", "height", "filt"))
    odd = lax.rem(d, 2)
    end = (d == nd - 1).astype(jnp.int32)
    start = (d == 0).astype(jnp.int32)
    return (d * rows, nd * rows, (h == 0).astype(jnp.int32), (h == nh - 1).astype(jnp.int32), f, nf, odd,
            end * (1 - odd), jnp.where(odd == 1, end, start))


def near_kernel(sides, xc, xn, k1h, b1, k2h, b2, o_ref, keep, k1, k2, x3, ef, e3, eb, h3, raw, ends, total, sems):
    copies = [pltpu.make_async_copy(k1h.at[a], k1.at[a], sems.at[a]) for a in range(3)]
    copies += [pltpu.make_async_copy(k2h.at[a], k2.at[a], sems.at[3 + a]) for a in range(3)]
    for copy in copies[:3]:
        copy.start()

    D, H, own = xc.shape[0], xc.shape[1], xc.shape[2] - 4
    info = places(D)
    odd = info[6]
    scratch = (x3, ef, e3, eb)
    spread(xc, D, 2 * odd, sides, info, *scratch)
    spread(xn, 2, D * (1 - odd), sides, info, *scratch)

    @pl.when(info[7] > 0)
    def _():
        clear(2, D * (1 - odd), x3, eb)

    first = info[0] - 1 + 2 * (1 - odd)

    def block(run):
        pl.when(odd >= 0)(run)

    def part(d, taps):
        hidden_part(d, taps, x3, eb, k1, b1, raw, ends)

    def rows(d):
        hidden_rows(d, d, first + d, sides, info, own, H, raw, ends, h3)

    for a in range(3):
        copies[a].wait()
        if a == 0:
            for copy in copies[3:]:
                copy.start()

        @block
        def _():
            for d in range(D):
                part(d, [a])
                if a == 2:
                    rows(d)
    for copy in copies[3:]:
        copy.wait()

    @block
    def _():
        keep[...] = h3[pl.ds((D - 2) * odd, 2)]
        features(feature_sums(range(3), h3, k2, jnp.zeros(total.shape, jnp.float32)), b2, o_ref)


def far_kernel(sides, xc, xf, keep, k1, b1, k2, b2, o_ref, x3, ef, e3, eb, h3, raw, ends, total):
    D, H, own = xc.shape[0], xc.shape[1], xc.shape[2] - 4
    info = places(D)
    odd = info[6]
    scratch = (x3, ef, e3, eb)
    spread(xc.at[pl.ds((D - 2) * odd, 2)], 2, 2 * (1 - odd), sides, info, *scratch)
    spread(xf, 2, 2 * odd, sides, info, *scratch)

    @pl.when(info[8] > 0)
    def _():
        clear(2, 2 * odd, x3, eb)

    h3[pl.ds(2 * (1 - odd), 2)] = keep[...]

    first = info[0] - 1 + D * odd

    @pl.when(odd >= 0)
    def _():
        for d in range(2):
            hidden_part(d, range(3), x3, eb, k1, b1, raw, ends)
        for d in range(2):
            hidden_rows(d, 2 * odd + d, first + d, sides, info, own, H, raw, ends, h3)

    @pl.when(odd >= 0)
    def _():
        features(feature_sums(range(3), h3, k2, jnp.zeros(total.shape, jnp.float32)), b2, o_ref)


def kernel_call(kernel, name, rows, sides, xc, near, operands):
    D, H, Wp, C = xc.shape
    own = Wp - 4
    weights = jax.ShapeDtypeStruct((3, 3, 3, C, C), jnp.bfloat16)
    out = [jax.ShapeDtypeStruct((2, H - 4, own, C), jnp.bfloat16)]
    scratch = [
        pltpu.VMEM((rows, H, own, 3 * C), jnp.bfloat16),
        pltpu.VMEM((sides, C // 128, H * 8, 128), jnp.float32),
        pltpu.VMEM((sides, 2 * H, 3 * C), jnp.float32),
        pltpu.VMEM((sides, 3, rows, H, 3 * C), jnp.bfloat16),
        pltpu.VMEM((4, H - 2, own, 3 * C), jnp.bfloat16),
        pltpu.VMEM((rows - 2, (H - 2) * own, C), jnp.float32),
        pltpu.VMEM((sides * (rows - 2) * H, C), jnp.float32),
        pltpu.VMEM((2 * (H - 4) * own, C), jnp.float32),
    ]
    specs = [VMEM] * len(operands)
    if near:
        out += [jax.ShapeDtypeStruct((2, H - 2, own, 3 * C), jnp.bfloat16), weights, weights]
        scratch.append(pltpu.SemaphoreType.DMA((6,)))
        specs[2] = specs[4] = HBM
    hid = (rows - 2) * (H - 2) * own
    return pl.pallas_call(
        functools.partial(kernel, sides),
        out_shape=out,
        in_specs=specs,
        out_specs=[VMEM] * len(out),
        scratch_shapes=scratch,
        compiler_params=pltpu.CompilerParams(vmem_limit_bytes=(43 if near else 24) * 2**20),
        cost_estimate=pl.CostEstimate(flops=2 * 27 * C * C * (hid + 2 * (H - 4) * own), bytes_accessed=2**20, transcendentals=0),
        name=name,
    )(*operands)


def body(volume, kernel_one, bias_one, kernel_two, bias_two):
    b1, b2 = bias_one.reshape(1, -1), bias_two.reshape(1, -1)
    rows, odd = volume.shape[0], lax.axis_index("depth") % 2
    sides = 1 if lax.axis_size("filt") == 2 else 2

    tall = gathered(volume, "filt", "height")
    near, far = exchange(tall[:2], tall[-2:], "depth")
    out_near, keep, k1, k2 = kernel_call(near_kernel, "near", rows + 2, sides, tall, True, (tall, near, kernel_one, b1, kernel_two, b2))
    shard = volume.shape[3]
    def pieces(y):
        f, n = lax.axis_index("filt"), lax.axis_size("filt")
        return [lax.dynamic_slice_in_dim(y, (f + s) % n * shard, shard, 3) for s in range(n)]
    out_far, = kernel_call(far_kernel, "far", 4, sides, tall, False, (tall, far, keep, k1, b1, k2, b2))
    out = jnp.where(odd == 1, jnp.concatenate([out_near, out_far], 0), jnp.concatenate([out_far, out_near], 0))
    return by_origin(swapped(pieces(out), "filt"), "filt", 2)


def solution(mesh):
    in_specs = (P("depth", "height", None, "filt"), P(), P(), P(), P())
    out_specs = P("depth", "height", None, "filt")
    return jax.shard_map(body, mesh=mesh, in_specs=in_specs, out_specs=out_specs, check_vma=False)
```

time: 35.5 us -> 34.1 us (0.961)
  the two profiles are of different devices: /device:TPU:0 before, /device:TPU:18 now
where the time goes in v6:
time: 34.1 us; the launch traced here: 33.5 us
  starting transfers between devices  12.9 us (38%)
  Pallas kernels  9.31 us (27%)
  waiting for transfers between devices  8.53 us (25%)
  other arithmetic  1.37 us (4%)
  local copies, waits for them, and re-layouts  1.22 us (4%)
    pallas_call x2, Pallas kernels, kernel_call(): pl.pallas_call(functools.partial(kernel, sides), out_shape=out, in_specs=...  9.31 us
    ppermute x2, starting transfers between devices, gathered(): twos.append(lax.ppermute(jnp.where(odd, last, first), rows, far))  3.82 us
    ppermute x2, waiting for transfers between devices, gathered(): twos.append(lax.ppermute(jnp.where(odd, last, first), rows, far))  3.46 us
    ppermute x1, waiting for transfers between devices, swapped(): lax.ppermute(pieces[s], axis, moves[s])  3.44 us
    ppermute x2, starting transfers between devices, gathered(): ones.append(lax.ppermute(jnp.where(odd, first, last), rows, near))  3.28 us
    ppermute x1, starting transfers between devices, exchange(): two = lax.ppermute(jnp.where(odd, last, first), axis, far)  2.52 us
    ppermute x1, starting transfers between devices, swapped(): lax.ppermute(pieces[s], axis, moves[s])  1.59 us
    ppermute x1, starting transfers between devices, gathered(): lax.ppermute(windows[s], columns, [(i, (i + s) % nc) for i in range(nc)])  1.59 us
  transfers between devices with their start and end apart: 8, of which 4 were waited for; matrix products, arithmetic and copies ran while one was open for 0% of the time, Pallas kernels for 18%

profile of v6, /device:TPU:18, one launch (start us, length us, event | category | flops | bytes accessed | tf_op | source)
XLA Modules:
  0.0 33.5 jit_solution(4887263642417835427)
XLA Ops:
  0.0 0.0 copy-start.1
  0.0 0.0 copy-start
  0.0 1.2 %pad_dynamic-slice_fusion = (bf16[4,4,36,128]{3,2,1,0:T(8,128)(2,1)S(1)}, bf16[4,4,36,128]{3,2,1,0:T(8,128)(2,1)S(1)}) fusion(s32[]{:T(128)S(6)} %select_n.140, bf16[4,4,64,128]{3,2,1,0:T(8,128)(2,1)} %param.5, s32[]{:T(128)S(6)} %select_n.138), kind=kLoop, calls=%fused_computation.4 | loop fusion | bytes 557064 | tf_op jit(solution)/shard_map/dynamic_slice | solution.py:70
  1.2 1.6 %collective-permute-start.1 = (bf16[4,4,36,128]{3,2,1,0:T(8,128)(2,1)S(1)}, bf16[4,4,36,128]{3,2,1,0:T(8,128)(2,1)S(1)}, u32[]{:S(2)}, u32[]{:S(2)}) collective-permute-start(bf16[4,4,36,128]{3,2,1,0:T(8,128)(2,1)S(1)} %get-tuple-element.12), channel_id=1, source_target_pairs={{0,1},{1,0},{2,3},{3,2},{4,5},{5,4},{6,7},{7,6},{8,9},{9,8},{10,11... | collective-permute-start | bytes 442376 | tf_op jit(solution)/shard_map/ppermute | solution.py:75
  2.8 1.6 %collective-permute-start = (bf16[4,2,36,128]{3,2,1,0:T(8,128)(2,1)S(1)}, bf16[4,2,36,128]{3,2,1,0:T(8,128)(2,1)S(1)}, u32[]{:S(2)}, u32[]{:S(2)}) collective-permute-start(bf16[4,2,36,128]{3,2,1,0:T(8,128)(2,1)S(1)} %get-tuple-element.25), channel_id=1, source_target_pairs={{0,2},{4,6},{2,0},{6,4},{1,3},{5,7},{3,1},{7,5},{8,10},{12,14},{10... | collective-permute-start | bytes 221192 | tf_op jit(solution)/shard_map/ppermute | solution.py:78
  4.4 1.9 %collective-permute-start.3 = (bf16[4,2,36,128]{3,2,1,0:T(8,128)(2,1)S(1)}, bf16[4,2,36,128]{3,2,1,0:T(8,128)(2,1)S(1)}, u32[]{:S(2)}, u32[]{:S(2)}) collective-permute-start(bf16[4,2,36,128]{3,2,1,0:T(8,128)(2,1)S(1)} %get-tuple-element.26), channel_id=1, source_target_pairs={{2,4},{4,2},{0,0},{6,6},{3,5},{5,3},{1,1},{7,7},{10,12},{12,10},{8... | collective-permute-start | bytes 221192 | tf_op jit(solution)/shard_map/ppermute | solution.py:79
  6.4 0.8 %collective-permute-done.1 = bf16[4,4,36,128]{3,2,1,0:T(8,128)(2,1)S(1)} collective-permute-done((bf16[4,4,36,128]{3,2,1,0:T(8,128)(2,1)S(1)}, bf16[4,4,36,128]{3,2,1,0:T(8,128)(2,1)S(1)}, u32[]{:S(2)}, u32[]{:S(2)}) %collective-permute-start.1) | collective-permute-done | bytes 147488 | tf_op jit(solution)/shard_map/ppermute | solution.py:75
  7.2 1.6 %collective-permute-start.2 = (bf16[4,2,36,128]{3,2,1,0:T(8,128)(2,1)S(1)}, bf16[4,2,36,128]{3,2,1,0:T(8,128)(2,1)S(1)}, u32[]{:S(2)}, u32[]{:S(2)}) collective-permute-start(bf16[4,2,36,128]{3,2,1,0:T(8,128)(2,1)S(1)} %get-tuple-element.23), channel_id=1, source_target_pairs={{0,2},{4,6},{2,0},{6,4},{1,3},{5,7},{3,1},{7,5},{8,10},{12,14},{10... | collective-permute-start | bytes 221192 | tf_op jit(solution)/shard_map/ppermute | solution.py:78
  8.8 1.9 %collective-permute-start.4 = (bf16[4,2,36,128]{3,2,1,0:T(8,128)(2,1)S(1)}, bf16[4,2,36,128]{3,2,1,0:T(8,128)(2,1)S(1)}, u32[]{:S(2)}, u32[]{:S(2)}) collective-permute-start(bf16[4,2,36,128]{3,2,1,0:T(8,128)(2,1)S(1)} %get-tuple-element.24), channel_id=1, source_target_pairs={{2,4},{4,2},{0,0},{6,6},{3,5},{5,3},{1,1},{7,7},{10,12},{12,10},{8... | collective-permute-start | bytes 221192 | tf_op jit(solution)/shard_map/ppermute | solution.py:79
  10.7 0.1 maximum_select_fusion
  10.9 0.0 collective-permute-done
  10.9 0.0 collective-permute-done.3
  10.9 0.8 %collective-permute-done.2 = bf16[4,2,36,128]{3,2,1,0:T(8,128)(2,1)S(1)} collective-permute-done((bf16[4,2,36,128]{3,2,1,0:T(8,128)(2,1)S(1)}, bf16[4,2,36,128]{3,2,1,0:T(8,128)(2,1)S(1)}, u32[]{:S(2)}, u32[]{:S(2)}) %collective-permute-start.2) | collective-permute-done | bytes 73760 | tf_op jit(solution)/shard_map/ppermute | solution.py:78
  11.7 3.5 %collective-permute-done.4 = bf16[4,2,36,128]{3,2,1,0:T(8,128)(2,1)S(1)} collective-permute-done((bf16[4,2,36,128]{3,2,1,0:T(8,128)(2,1)S(1)}, bf16[4,2,36,128]{3,2,1,0:T(8,128)(2,1)S(1)}, u32[]{:S(2)}, u32[]{:S(2)}) %collective-permute-start.4) | collective-permute-done | bytes 73760 | tf_op jit(solution)/shard_map/ppermute | solution.py:79
  15.2 0.1 select_select_fusion
  15.3 0.1 select_select_fusion.1
  15.4 0.1 pad_maximum_fusion.xc
  15.6 0.1 collective-permute-start.5
  15.7 2.5 %collective-permute-start.6 = (bf16[2,8,36,256]{3,2,1,0:T(8,128)(2,1)S(1)}, bf16[2,8,36,256]{3,2,1,0:T(8,128)(2,1)S(1)}, u32[]{:S(2)}, u32[]{:S(2)}) collective-permute-start(bf16[2,8,36,256]{3,2,1,0:T(8,128)(2,1)S(1)} %get-tuple-element.18), channel_id=1, source_target_pairs={{8,16},{16,8},{0,0},{24,24},{9,17},{17,9},{1,1},{25,25},{10,18},{1... | collective-permute-start | bytes 884744 | tf_op jit(solution)/shard_map/ppermute | solution.py:31
  18.2 0.0 collective-permute-done.5.xn
  18.2 0.0 copy-done.1
  18.2 0.0 copy-done
  18.2 6.0 %near.1 = (bf16[2,4,32,256]{3,2,1,0:T(8,128)(2,1)S(1)}, bf16[2,6,32,768]{3,2,1,0:T(8,128)(2,1)S(1)}, bf16[3,3,3,256,256]{4,3,2,1,0:T(8,128)(2,1)S(1)}, bf16[3,3,3,256,256]{4,3,2,1,0:T(8,128)(2,1)S(1)}) custom-call(bf16[4,8,36,256]{3,2,1,0:T(8,128)(2,1)S(1)} %pad_maximum_fusion.xc, bf16[2,8,36,256]{3,2,1,0:T(8,128)(2,1)S(1)} %collective-permute-done.5.xn, ...), custom_call_target="tpu_custom_call" | custom-call | flops 3623878656 | bytes 1048576 | tf_op jit(solution)/shard_map/near/pallas_call | solution.py:287
  24.2 0.0 collective-permute-done.6.xf
  24.2 3.4 %far.1 = bf16[2,4,32,256]{3,2,1,0:T(8,128)(2,1)S(1)} custom-call(bf16[4,8,36,256]{3,2,1,0:T(8,128)(2,1)S(1)} %pad_maximum_fusion.xc, bf16[2,8,36,256]{3,2,1,0:T(8,128)(2,1)S(1)} %collective-permute-done.6.xf, bf16[2,6,32,768]{3,2,1,0:T(8,128)(2,1)S(1)} %get-tuple-element.14.keep, bf16[3,3,3,256,256]{4,3,2,1,0:T(8,128)(2,1)S(1)} %get-tuple-element.15.k1, ...), custom_call_target="tpu_custom_call" | custom-call | flops 2264924160 | bytes 1048576 | tf_op jit(solution)/shard_map/far/pallas_call | solution.py:287
  27.6 0.1 constant_dynamic-slice_fusion.1
  27.6 1.6 %collective-permute-start.7 = (bf16[4,4,32,128]{3,2,1,0:T(8,128)(2,1)S(1)}, bf16[4,4,32,128]{3,2,1,0:T(8,128)(2,1)S(1)}, u32[]{:S(2)}, u32[]{:S(2)}) collective-permute-start(bf16[4,4,32,128]{3,2,1,0:T(8,128)(2,1)S(1)} %get-tuple-element.20), channel_id=1, source_target_pairs={{0,1},{1,0},{2,3},{3,2},{4,5},{5,4},{6,7},{7,6},{8,9},{9,8},{10,11... | collective-permute-start | bytes 393224 | tf_op jit(solution)/shard_map/ppermute | solution.py:57
  29.2 3.4 %collective-permute-done.7 = bf16[4,4,32,128]{3,2,1,0:T(8,128)(2,1)S(1)} collective-permute-done((bf16[4,4,32,128]{3,2,1,0:T(8,128)(2,1)S(1)}, bf16[4,4,32,128]{3,2,1,0:T(8,128)(2,1)S(1)}, u32[]{:S(2)}, u32[]{:S(2)}) %collective-permute-start.7) | collective-permute-done | bytes 131104 | tf_op jit(solution)/shard_map/ppermute | solution.py:57
  32.7 0.8 %maximum_select_fusion.2 = bf16[4,4,64,128]{3,2,1,0:T(8,128)(2,1)} fusion(bf16[4,4,32,128]{3,2,1,0:T(8,128)(2,1)S(1)} %collective-permute-done.7, bf16[4,4,32,128]{3,2,1,0:T(8,128)(2,1)S(1)} %get-tuple-element.19, pred[]{:T(512)S(6)} %eq.29), kind=kLoop, calls=%fused_computation.7 | loop fusion | flops 1179648 | bytes 524289 | tf_op jit(solution)/shard_map/jit(_where)/select_n | solution.py:48
  (4 shorter events, 0.1 us)
Async XLA Ops:
  0.0 18.2 %copy-start.1 = (f32[256]{0:T(256)S(1)}, f32[256]{0:T(256)}, u32[]{:S(2)}) copy-start(f32[256]{0:T(256)} %param.9) | copy-start | bytes 3076
  0.0 18.2 %copy-start = (f32[256]{0:T(256)S(1)}, f32[256]{0:T(256)}, u32[]{:S(2)}) copy-start(f32[256]{0:T(256)} %param.7) | copy-start | bytes 3076
  1.2 6.0 %collective-permute-start.1 = (bf16[4,4,36,128]{3,2,1,0:T(8,128)(2,1)S(1)}, bf16[4,4,36,128]{3,2,1,0:T(8,128)(2,1)S(1)}, u32[]{:S(2)}, u32[]{:S(2)}) collective-permute-start(bf16[4,4,36,128]{3,2,1,0:T(8,128)(2,1)S(1)} %get-tuple-element.12), channel_id=1, source_target_pairs={{0,1},{1,0},{2,3},{3,2},{4,5},{5,4},{6,7},{7,6},{8,9},{9,8},{10,11... | collective-permute-start | bytes 442376 | tf_op jit(solution)/shard_map/ppermute | solution.py:75
  2.8 8.1 %collective-permute-start = (bf16[4,2,36,128]{3,2,1,0:T(8,128)(2,1)S(1)}, bf16[4,2,36,128]{3,2,1,0:T(8,128)(2,1)S(1)}, u32[]{:S(2)}, u32[]{:S(2)}) collective-permute-start(bf16[4,2,36,128]{3,2,1,0:T(8,128)(2,1)S(1)} %get-tuple-element.25), channel_id=1, source_target_pairs={{0,2},{4,6},{2,0},{6,4},{1,3},{5,7},{3,1},{7,5},{8,10},{12,14},{10... | collective-permute-start | bytes 221192 | tf_op jit(solution)/shard_map/ppermute | solution.py:78
  4.4 6.5 %collective-permute-start.3 = (bf16[4,2,36,128]{3,2,1,0:T(8,128)(2,1)S(1)}, bf16[4,2,36,128]{3,2,1,0:T(8,128)(2,1)S(1)}, u32[]{:S(2)}, u32[]{:S(2)}) collective-permute-start(bf16[4,2,36,128]{3,2,1,0:T(8,128)(2,1)S(1)} %get-tuple-element.26), channel_id=1, source_target_pairs={{2,4},{4,2},{0,0},{6,6},{3,5},{5,3},{1,1},{7,7},{10,12},{12,10},{8... | collective-permute-start | bytes 221192 | tf_op jit(solution)/shard_map/ppermute | solution.py:79
  7.2 4.5 %collective-permute-start.2 = (bf16[4,2,36,128]{3,2,1,0:T(8,128)(2,1)S(1)}, bf16[4,2,36,128]{3,2,1,0:T(8,128)(2,1)S(1)}, u32[]{:S(2)}, u32[]{:S(2)}) collective-permute-start(bf16[4,2,36,128]{3,2,1,0:T(8,128)(2,1)S(1)} %get-tuple-element.23), channel_id=1, source_target_pairs={{0,2},{4,6},{2,0},{6,4},{1,3},{5,7},{3,1},{7,5},{8,10},{12,14},{10... | collective-permute-start | bytes 221192 | tf_op jit(solution)/shard_map/ppermute | solution.py:78
  8.8 6.3 %collective-permute-start.4 = (bf16[4,2,36,128]{3,2,1,0:T(8,128)(2,1)S(1)}, bf16[4,2,36,128]{3,2,1,0:T(8,128)(2,1)S(1)}, u32[]{:S(2)}, u32[]{:S(2)}) collective-permute-start(bf16[4,2,36,128]{3,2,1,0:T(8,128)(2,1)S(1)} %get-tuple-element.24), channel_id=1, source_target_pairs={{2,4},{4,2},{0,0},{6,6},{3,5},{5,3},{1,1},{7,7},{10,12},{12,10},{8... | collective-permute-start | bytes 221192 | tf_op jit(solution)/shard_map/ppermute | solution.py:79
  15.6 2.6 %collective-permute-start.5 = (bf16[2,8,36,256]{3,2,1,0:T(8,128)(2,1)S(1)}, bf16[2,8,36,256]{3,2,1,0:T(8,128)(2,1)S(1)}, u32[]{:S(2)}, u32[]{:S(2)}) collective-permute-start(bf16[2,8,36,256]{3,2,1,0:T(8,128)(2,1)S(1)} %get-tuple-element.17), channel_id=1, source_target_pairs={{0,8},{16,24},{8,0},{24,16},{1,9},{17,25},{9,1},{25,17},{2,10},{18... | collective-permute-start | bytes 884744 | tf_op jit(solution)/shard_map/ppermute | solution.py:30
  15.7 8.5 %collective-permute-start.6 = (bf16[2,8,36,256]{3,2,1,0:T(8,128)(2,1)S(1)}, bf16[2,8,36,256]{3,2,1,0:T(8,128)(2,1)S(1)}, u32[]{:S(2)}, u32[]{:S(2)}) collective-permute-start(bf16[2,8,36,256]{3,2,1,0:T(8,128)(2,1)S(1)} %get-tuple-element.18), channel_id=1, source_target_pairs={{8,16},{16,8},{0,0},{24,24},{9,17},{17,9},{1,1},{25,25},{10,18},{1... | collective-permute-start | bytes 884744 | tf_op jit(solution)/shard_map/ppermute | solution.py:31
  27.6 5.0 %collective-permute-start.7 = (bf16[4,4,32,128]{3,2,1,0:T(8,128)(2,1)S(1)}, bf16[4,4,32,128]{3,2,1,0:T(8,128)(2,1)S(1)}, u32[]{:S(2)}, u32[]{:S(2)}) collective-permute-start(bf16[4,4,32,128]{3,2,1,0:T(8,128)(2,1)S(1)} %get-tuple-element.20), channel_id=1, source_target_pairs={{0,1},{1,0},{2,3},{3,2},{4,5},{5,4},{6,7},{7,6},{8,9},{9,8},{10,11... | collective-permute-start | bytes 393224 | tf_op jit(solution)/shard_map/ppermute | solution.py:57

commit v7 on v6

--- a/solution.py
+++ b/solution.py
@@ -61,25 +61,30 @@
     return by_origin(parts, axis, 3)
 
 
-def gathered(x, columns, rows):
+def gathered(x, columns, rows, extra):
     nc, nr = lax.axis_size(columns), lax.axis_size(rows)
     c, r = lax.axis_index(columns), lax.axis_index(rows)
     own = x.shape[2] // nc
     odd = r % 2 == 1
-    padded = jnp.pad(x, ((0, 0), (0, 0), (2, 2), (0, 0)))
-    windows = [lax.dynamic_slice_in_dim(padded, (c + s) % nc * own, own + 4, 2) for s in range(nc)]
-    windows = lax.optimization_barrier(windows)
-    parts, ones, twos = [windows[0]], [], []
+    def halves(s, x):
+        padded = jnp.pad(x, ((0, 0), (0, 0), (2, 2), (0, 0)))
+        w = lax.dynamic_slice_in_dim(padded, (c + s) % nc * own, own + 4, 2)
+        return jnp.where(odd, w[:, :2], w[:, -2:]), jnp.where(odd, w[:, -2:], w[:, :2])
+
+    sent = lax.optimization_barrier([halves(s, x) for s in range(1, nc)])
+    again, extra = lax.optimization_barrier((x, extra))
+    kept = halves(0, again)
+    got = []
+    for r in range(2):
+        parts = [kept[r]] + [lax.ppermute(sent[s - 1][r], columns, [(i, (i + s) % nc) for i in range(nc)]) for s in range(1, nc)]
+        got.append(in_order(parts, columns))
     near, far = pairings(nr)
-    for s in range(1, nc):
-        parts.append(lax.ppermute(windows[s], columns, [(i, (i + s) % nc) for i in range(nc)]))
-    for s in range(nc):
-        first, last = parts[s][:, :2], parts[s][:, -2:]
-        ones.append(lax.ppermute(jnp.where(odd, first, last), rows, near))
-        twos.append(lax.ppermute(jnp.where(odd, last, first), rows, far))
-    one, two = in_order(ones, columns), in_order(twos, columns)
+    one = lax.ppermute(got[0], rows, near)
+    two = lax.ppermute(got[1], rows, far)
+    two, one = lax.optimization_barrier((two, one))
     before, after = beside(one, two, rows)
-    return jnp.concatenate([before, in_order(parts, columns), after], 1)
+    whole = jnp.where(odd, jnp.concatenate(got, 1), jnp.concatenate(got[::-1], 1))
+    return jnp.concatenate([before, whole, after], 1), extra
 
 
 def spread(source, rows, at, sides, info, x3, ef, e3, eb):
@@ -186,12 +191,11 @@
             end * (1 - odd), jnp.where(odd == 1, end, start))
 
 
-def near_kernel(sides, xc, xn, k1h, b1, k2h, b2, o_ref, keep, k1, k2, x3, ef, e3, eb, h3, raw, ends, total, sems):
+def near_kernel(sides, xc, xn, k0, k1h, b1, k2h, b2, o_ref, keep, k1, k2, x3, ef, e3, eb, h3, raw, ends, total, sems):
     copies = [pltpu.make_async_copy(k1h.at[a], k1.at[a], sems.at[a]) for a in range(3)]
     copies += [pltpu.make_async_copy(k2h.at[a], k2.at[a], sems.at[3 + a]) for a in range(3)]
-    for copy in copies[:3]:
+    for copy in copies[1:3]:
         copy.start()
-
     D, H, own = xc.shape[0], xc.shape[1], xc.shape[2] - 4
     info = places(D)
     odd = info[6]
@@ -209,15 +213,16 @@
         pl.when(odd >= 0)(run)
 
     def part(d, taps):
-        hidden_part(d, taps, x3, eb, k1, b1, raw, ends)
+        hidden_part(d, taps, x3, eb, k1 if taps[0] else k0, b1, raw, ends)
 
     def rows(d):
         hidden_rows(d, d, first + d, sides, info, own, H, raw, ends, h3)
 
     for a in range(3):
-        copies[a].wait()
-        if a == 0:
-            for copy in copies[3:]:
+        if a > 0:
+            copies[a].wait()
+        if a == 1:
+            for copy in copies[3:] + copies[:1]:
                 copy.start()
 
         @block
@@ -226,7 +231,7 @@
                 part(d, [a])
                 if a == 2:
                     rows(d)
-    for copy in copies[3:]:
+    for copy in copies[3:] + copies[:1]:
         copy.wait()
 
     @block
@@ -282,7 +287,7 @@
     if near:
         out += [jax.ShapeDtypeStruct((2, H - 2, own, 3 * C), jnp.bfloat16), weights, weights]
         scratch.append(pltpu.SemaphoreType.DMA((6,)))
-        specs[2] = specs[4] = HBM
+        specs[3] = specs[5] = HBM
     hid = (rows - 2) * (H - 2) * own
     return pl.pallas_call(
         functools.partial(kernel, sides),
@@ -301,9 +306,9 @@
     rows, odd = volume.shape[0], lax.axis_index("depth") % 2
     sides = 1 if lax.axis_size("filt") == 2 else 2
 
-    tall = gathered(volume, "filt", "height")
+    tall, k0 = gathered(volume, "filt", "height", kernel_one[:1])
     near, far = exchange(tall[:2], tall[-2:], "depth")
-    out_near, keep, k1, k2 = kernel_call(near_kernel, "near", rows + 2, sides, tall, True, (tall, near, kernel_one, b1, kernel_two, b2))
+    out_near, keep, k1, k2 = kernel_call(near_kernel, "near", rows + 2, sides, tall, True, (tall, near, k0, kernel_one, b1, kernel_two, b2))
     shard = volume.shape[3]
     def pieces(y):
         f, n = lax.axis_index("filt"), lax.axis_size("filt")

time: 34.1 us -> 34 us (level)
  the two profiles are of different devices: /device:TPU:18 before, /device:TPU:1 now
where the time goes in v7:
time: 34 us; the launch traced here: 33.7 us
  starting transfers between devices  14 us (41%)
  Pallas kernels  8.7 us (26%)
  waiting for transfers between devices  6.01 us (18%)
  other arithmetic  3.44 us (10%)
  local copies, waits for them, and re-layouts  1.44 us (4%)
    pallas_call x2, Pallas kernels, kernel_call(): pl.pallas_call(functools.partial(kernel, sides), out_shape=out, in_specs=...  8.7 us
    ppermute x1, starting transfers between devices, gathered(): one = lax.ppermute(got[0], rows, near)  3.82 us
    ppermute x1, waiting for transfers between devices, swapped(): lax.ppermute(pieces[s], axis, moves[s])  3.14 us
    ppermute x1, starting transfers between devices, exchange(): two = lax.ppermute(jnp.where(odd, last, first), axis, far)  3.03 us
    ppermute x1, starting transfers between devices, exchange(): one = lax.ppermute(jnp.where(odd, first, last), axis, near)  3.03 us
    ppermute x1, waiting for transfers between devices, gathered(): one = lax.ppermute(got[0], rows, near)  2.66 us
    ppermute x2, starting transfers between devices, gathered(): lax.ppermute(sent[s - 1][r], columns, [(i, (i + s) % nc) for i in range(n...  2.24 us
    slice x1, local copies, waits for them, and re-layouts, body(): tall, k0 = gathered(volume, 'filt', 'height', kernel_one[:1])  1.37 us
  transfers between devices with their start and end apart: 7, of which 3 were waited for; matrix products, arithmetic and copies ran while one was open for 8% of the time, Pallas kernels for 16%

profile of v7, /device:TPU:1, one launch (start us, length us, event | category | flops | bytes accessed | tf_op | source)
XLA Modules:
  0.0 33.7 jit_solution(10608781303885495800)
XLA Ops:
  0.0 1.1 %broadcast_select_fusion.3 = (bf16[4,2,36,128]{3,2,1,0:T(8,128)(2,1)S(1)}, bf16[4,2,36,128]{3,2,1,0:T(8,128)(2,1)S(1)}) fusion(pred[]{:T(512)S(6)} %eq.31, s32[]{:T(128)S(6)} %select_n.141, bf16[4,4,64,128]{3,2,1,0:T(8,128)(2,1)} %param.5, s32[]{:T(128)S(6)} %add.46), kind=kLoop, calls=%fused_computation.15 | loop fusion | flops 73728 | bytes 409609 | tf_op jit(solution)/shard_map/jit(_where)/select_n | solution.py:72
  1.1 2.2 %collective-permute-start = (bf16[4,2,36,128]{3,2,1,0:T(8,128)(2,1)S(1)}, bf16[4,2,36,128]{3,2,1,0:T(8,128)(2,1)S(1)}, u32[]{:S(2)}, u32[]{:S(2)}) collective-permute-start(bf16[4,2,36,128]{3,2,1,0:T(8,128)(2,1)S(1)} %get-tuple-element.16), channel_id=1, source_target_pairs={{0,1},{1,0},{2,3},{3,2},{4,5},{5,4},{6,7},{7,6},{8,9},{9,8},{10,11... | collective-permute-start | bytes 221192 | tf_op jit(solution)/shard_map/ppermute | solution.py:79
  3.3 0.1 collective-permute-start.2
  3.4 0.0 copy-start
  3.4 0.0 copy-start.1
  3.4 1.4 %slice.25.k0 = bf16[1,3,3,256,256]{4,3,2,1,0:T(8,128)(2,1)S(1)} slice(bf16[3,3,3,256,256]{4,3,2,1,0:T(8,128)(2,1)} %k1h.1), slice={[0:1], [0:3], [0:3], [0:256], [0:256]} | slice | bytes 2359296 | tf_op jit(solution)/shard_map/slice | solution.py:309
  4.8 1.2 %broadcast_select_fusion.2 = (bf16[4,2,36,128]{3,2,1,0:T(8,128)(2,1)S(1)}, bf16[4,2,36,128]{3,2,1,0:T(8,128)(2,1)S(1)}) fusion(pred[]{:T(512)S(6)} %eq.31, s32[]{:T(128)S(6)} %select_n.138, bf16[4,4,64,128]{3,2,1,0:T(8,128)(2,1)} %param.5, s32[]{:T(128)S(6)} %add.46), kind=kLoop, calls=%fused_computation.14 | loop fusion | flops 73728 | bytes 409609 | tf_op jit(solution)/shard_map/jit(_where)/select_n | solution.py:72
  5.9 0.0 collective-permute-done
  6.0 0.7 %collective-permute-start.1 = (bf16[4,2,36,256]{3,2,1,0:T(8,128)(2,1)S(1)}, bf16[4,2,36,256]{3,2,1,0:T(8,128)(2,1)S(1)}, u32[]{:S(2)}, u32[]{:S(2)}) collective-permute-start(bf16[4,2,36,256]{3,2,1,0:T(8,128)(2,1)S(1)} %maximum_select_fusion.3), channel_id=1, source_target_pairs={{2,4},{4,2},{0,0},{6,6},{3,5},{5,3},{1,1},{7,7},{10,12},{12,10},{8... | collective-permute-start | bytes 442376 | tf_op jit(solution)/shard_map/ppermute | solution.py:83
  6.7 0.2 collective-permute-done.2
  6.9 3.8 %collective-permute-start.3 = (bf16[4,2,36,256]{3,2,1,0:T(8,128)(2,1)S(1)}, bf16[4,2,36,256]{3,2,1,0:T(8,128)(2,1)S(1)}, u32[]{:S(2)}, u32[]{:S(2)}) collective-permute-start(bf16[4,2,36,256]{3,2,1,0:T(8,128)(2,1)S(1)} %maximum_select_fusion.4), channel_id=1, source_target_pairs={{0,2},{4,6},{2,0},{6,4},{1,3},{5,7},{3,1},{7,5},{8,10},{12,14},{10... | collective-permute-start | bytes 442376 | tf_op jit(solution)/shard_map/ppermute | solution.py:82
  10.8 0.0 collective-permute-done.1
  10.8 2.7 %collective-permute-done.3 = bf16[4,2,36,256]{3,2,1,0:T(8,128)(2,1)S(1)} collective-permute-done((bf16[4,2,36,256]{3,2,1,0:T(8,128)(2,1)S(1)}, bf16[4,2,36,256]{3,2,1,0:T(8,128)(2,1)S(1)}, u32[]{:S(2)}, u32[]{:S(2)}) %collective-permute-start.3) | collective-permute-done | bytes 147488 | tf_op jit(solution)/shard_map/ppermute | solution.py:82
  13.5 0.1 pad_maximum_fusion.xc
  13.6 3.0 %collective-permute-start.4 = (bf16[2,8,36,256]{3,2,1,0:T(8,128)(2,1)S(1)}, bf16[2,8,36,256]{3,2,1,0:T(8,128)(2,1)S(1)}, u32[]{:S(2)}, u32[]{:S(2)}) collective-permute-start(bf16[2,8,36,256]{3,2,1,0:T(8,128)(2,1)S(1)} %get-tuple-element.25), channel_id=1, source_target_pairs={{0,8},{16,24},{8,0},{24,16},{1,9},{17,25},{9,1},{25,17},{2,10},{18... | collective-permute-start | bytes 884744 | tf_op jit(solution)/shard_map/ppermute | solution.py:30
  16.7 3.0 %collective-permute-start.5 = (bf16[2,8,36,256]{3,2,1,0:T(8,128)(2,1)S(1)}, bf16[2,8,36,256]{3,2,1,0:T(8,128)(2,1)S(1)}, u32[]{:S(2)}, u32[]{:S(2)}) collective-permute-start(bf16[2,8,36,256]{3,2,1,0:T(8,128)(2,1)S(1)} %get-tuple-element.26), channel_id=1, source_target_pairs={{8,16},{16,8},{0,0},{24,24},{9,17},{17,9},{1,1},{25,25},{10,18},{1... | collective-permute-start | bytes 884744 | tf_op jit(solution)/shard_map/ppermute | solution.py:31
  19.7 0.0 collective-permute-done.4.xn
  19.7 0.0 copy-done
  19.7 0.0 copy-done.1
  19.7 5.4 %near.1 = (bf16[2,4,32,256]{3,2,1,0:T(8,128)(2,1)S(1)}, bf16[2,6,32,768]{3,2,1,0:T(8,128)(2,1)S(1)}, bf16[3,3,3,256,256]{4,3,2,1,0:T(8,128)(2,1)S(1)}, bf16[3,3,3,256,256]{4,3,2,1,0:T(8,128)(2,1)S(1)}) custom-call(bf16[4,8,36,256]{3,2,1,0:T(8,128)(2,1)S(1)} %pad_maximum_fusion.xc, bf16[2,8,36,256]{3,2,1,0:T(8,128)(2,1)S(1)} %collective-permute-done.4.xn, ...), custom_call_target="tpu_custom_call" | custom-call | flops 3623878656 | bytes 1048576 | tf_op jit(solution)/shard_map/near/pallas_call | solution.py:292
  25.1 0.0 collective-permute-done.5.xf
  25.1 3.3 %far.1 = bf16[2,4,32,256]{3,2,1,0:T(8,128)(2,1)S(1)} custom-call(bf16[4,8,36,256]{3,2,1,0:T(8,128)(2,1)S(1)} %pad_maximum_fusion.xc, bf16[2,8,36,256]{3,2,1,0:T(8,128)(2,1)S(1)} %collective-permute-done.5.xf, bf16[2,6,32,768]{3,2,1,0:T(8,128)(2,1)S(1)} %get-tuple-element.22.keep, bf16[3,3,3,256,256]{4,3,2,1,0:T(8,128)(2,1)S(1)} %get-tuple-element.23.k1, ...), custom_call_target="tpu_custom_call" | custom-call | flops 2264924160 | bytes 1048576 | tf_op jit(solution)/shard_map/far/pallas_call | solution.py:292
  28.5 0.1 constant_dynamic-slice_fusion.1
  28.6 1.2 %collective-permute-start.6 = (bf16[4,4,32,128]{3,2,1,0:T(8,128)(2,1)S(1)}, bf16[4,4,32,128]{3,2,1,0:T(8,128)(2,1)S(1)}, u32[]{:S(2)}, u32[]{:S(2)}) collective-permute-start(bf16[4,4,32,128]{3,2,1,0:T(8,128)(2,1)S(1)} %get-tuple-element.30), channel_id=1, source_target_pairs={{0,1},{1,0},{2,3},{3,2},{4,5},{5,4},{6,7},{7,6},{8,9},{9,8},{10,11... | collective-permute-start | bytes 393224 | tf_op jit(solution)/shard_map/ppermute | solution.py:57
  29.8 3.1 %collective-permute-done.6 = bf16[4,4,32,128]{3,2,1,0:T(8,128)(2,1)S(1)} collective-permute-done((bf16[4,4,32,128]{3,2,1,0:T(8,128)(2,1)S(1)}, bf16[4,4,32,128]{3,2,1,0:T(8,128)(2,1)S(1)}, u32[]{:S(2)}, u32[]{:S(2)}) %collective-permute-start.6) | collective-permute-done | bytes 131104 | tf_op jit(solution)/shard_map/ppermute | solution.py:57
  32.9 0.8 %maximum_select_fusion.2 = bf16[4,4,64,128]{3,2,1,0:T(8,128)(2,1)} fusion(bf16[4,4,32,128]{3,2,1,0:T(8,128)(2,1)S(1)} %collective-permute-done.6, bf16[4,4,32,128]{3,2,1,0:T(8,128)(2,1)S(1)} %get-tuple-element.29, pred[]{:T(512)S(6)} %eq.28), kind=kLoop, calls=%fused_computation.9 | loop fusion | flops 1179648 | bytes 524289 | tf_op jit(solution)/shard_map/jit(_where)/select_n | solution.py:48
  (6 shorter events, 0.2 us)
Async XLA Ops:
  1.1 4.8 %collective-permute-start = (bf16[4,2,36,128]{3,2,1,0:T(8,128)(2,1)S(1)}, bf16[4,2,36,128]{3,2,1,0:T(8,128)(2,1)S(1)}, u32[]{:S(2)}, u32[]{:S(2)}) collective-permute-start(bf16[4,2,36,128]{3,2,1,0:T(8,128)(2,1)S(1)} %get-tuple-element.16), channel_id=1, source_target_pairs={{0,1},{1,0},{2,3},{3,2},{4,5},{5,4},{6,7},{7,6},{8,9},{9,8},{10,11... | collective-permute-start | bytes 221192 | tf_op jit(solution)/shard_map/ppermute | solution.py:79
  3.3 3.6 %collective-permute-start.2 = (bf16[4,2,36,128]{3,2,1,0:T(8,128)(2,1)S(1)}, bf16[4,2,36,128]{3,2,1,0:T(8,128)(2,1)S(1)}, u32[]{:S(2)}, u32[]{:S(2)}) collective-permute-start(bf16[4,2,36,128]{3,2,1,0:T(8,128)(2,1)S(1)} %get-tuple-element.17), channel_id=1, source_target_pairs={{0,1},{1,0},{2,3},{3,2},{4,5},{5,4},{6,7},{7,6},{8,9},{9,8},{10,11... | collective-permute-start | bytes 221192 | tf_op jit(solution)/shard_map/ppermute | solution.py:79
  3.4 16.4 %copy-start = (f32[256]{0:T(256)S(1)}, f32[256]{0:T(256)}, u32[]{:S(2)}) copy-start(f32[256]{0:T(256)} %param.7) | copy-start | bytes 3076
  3.4 16.4 %copy-start.1 = (f32[256]{0:T(256)S(1)}, f32[256]{0:T(256)}, u32[]{:S(2)}) copy-start(f32[256]{0:T(256)} %param.9) | copy-start | bytes 3076
  6.0 4.8 %collective-permute-start.1 = (bf16[4,2,36,256]{3,2,1,0:T(8,128)(2,1)S(1)}, bf16[4,2,36,256]{3,2,1,0:T(8,128)(2,1)S(1)}, u32[]{:S(2)}, u32[]{:S(2)}) collective-permute-start(bf16[4,2,36,256]{3,2,1,0:T(8,128)(2,1)S(1)} %maximum_select_fusion.3), channel_id=1, source_target_pairs={{2,4},{4,2},{0,0},{6,6},{3,5},{5,3},{1,1},{7,7},{10,12},{12,10},{8... | collective-permute-start | bytes 442376 | tf_op jit(solution)/shard_map/ppermute | solution.py:83
  6.9 6.5 %collective-permute-start.3 = (bf16[4,2,36,256]{3,2,1,0:T(8,128)(2,1)S(1)}, bf16[4,2,36,256]{3,2,1,0:T(8,128)(2,1)S(1)}, u32[]{:S(2)}, u32[]{:S(2)}) collective-permute-start(bf16[4,2,36,256]{3,2,1,0:T(8,128)(2,1)S(1)} %maximum_select_fusion.4), channel_id=1, source_target_pairs={{0,2},{4,6},{2,0},{6,4},{1,3},{5,7},{3,1},{7,5},{8,10},{12,14},{10... | collective-permute-start | bytes 442376 | tf_op jit(solution)/shard_map/ppermute | solution.py:82
  13.6 6.1 %collective-permute-start.4 = (bf16[2,8,36,256]{3,2,1,0:T(8,128)(2,1)S(1)}, bf16[2,8,36,256]{3,2,1,0:T(8,128)(2,1)S(1)}, u32[]{:S(2)}, u32[]{:S(2)}) collective-permute-start(bf16[2,8,36,256]{3,2,1,0:T(8,128)(2,1)S(1)} %get-tuple-element.25), channel_id=1, source_target_pairs={{0,8},{16,24},{8,0},{24,16},{1,9},{17,25},{9,1},{25,17},{2,10},{18... | collective-permute-start | bytes 884744 | tf_op jit(solution)/shard_map/ppermute | solution.py:30
  16.7 8.4 %collective-permute-start.5 = (bf16[2,8,36,256]{3,2,1,0:T(8,128)(2,1)S(1)}, bf16[2,8,36,256]{3,2,1,0:T(8,128)(2,1)S(1)}, u32[]{:S(2)}, u32[]{:S(2)}) collective-permute-start(bf16[2,8,36,256]{3,2,1,0:T(8,128)(2,1)S(1)} %get-tuple-element.26), channel_id=1, source_target_pairs={{8,16},{16,8},{0,0},{24,24},{9,17},{17,9},{1,1},{25,25},{10,18},{1... | collective-permute-start | bytes 884744 | tf_op jit(solution)/shard_map/ppermute | solution.py:31
  28.6 4.3 %collective-permute-start.6 = (bf16[4,4,32,128]{3,2,1,0:T(8,128)(2,1)S(1)}, bf16[4,4,32,128]{3,2,1,0:T(8,128)(2,1)S(1)}, u32[]{:S(2)}, u32[]{:S(2)}) collective-permute-start(bf16[4,4,32,128]{3,2,1,0:T(8,128)(2,1)S(1)} %get-tuple-element.30), channel_id=1, source_target_pairs={{0,1},{1,0},{2,3},{3,2},{4,5},{5,4},{6,7},{7,6},{8,9},{9,8},{10,11... | collective-permute-start | bytes 393224 | tf_op jit(solution)/shard_map/ppermute | solution.py:57

commit v8 on v7

--- a/solution.py
+++ b/solution.py
@@ -64,51 +64,116 @@
 def gathered(x, columns, rows, extra):
     nc, nr = lax.axis_size(columns), lax.axis_size(rows)
     c, r = lax.axis_index(columns), lax.axis_index(rows)
-    own = x.shape[2] // nc
+    own, shard = x.shape[2] // nc, x.shape[3]
     odd = r % 2 == 1
-    def halves(s, x):
+
+    def window(s, x):
+        block = (c + s) % nc
+        if nc == 2:
+            return jnp.where(block == 0, x[:, :, :own + 8], x[:, :, own - 8:])
         padded = jnp.pad(x, ((0, 0), (0, 0), (2, 2), (0, 0)))
-        w = lax.dynamic_slice_in_dim(padded, (c + s) % nc * own, own + 4, 2)
-        return jnp.where(odd, w[:, :2], w[:, -2:]), jnp.where(odd, w[:, -2:], w[:, :2])
-
-    sent = lax.optimization_barrier([halves(s, x) for s in range(1, nc)])
+        return lax.dynamic_slice_in_dim(padded, block * own, own + 4, 2)
+
+    def halves(s, near):
+        block = (c + s) % nc
+        if nc == 2:
+            main = jnp.where(block == 0, near[:, :, :own], near[:, :, 8:])
+            ends = jnp.where(block == 0, near[:, :, own:own + 2], near[:, :, 6:8])
+        else:
+            main, ends = near[:, :, 2:-2], jnp.concatenate([near[:, :, :2], near[:, :, -2:]], 2)
+
+        def flat(rows):
+            return jnp.concatenate([main[:, rows].reshape(-1, shard), ends[:, rows].reshape(-1, shard)], 0)
+        first, last = flat(slice(0, 2)), flat(slice(2, 4))
+        return jnp.where(odd, first, last), jnp.where(odd, last, first)
+
+    windows = lax.optimization_barrier([window(s, x) for s in range(1, nc)])
+    sent = [halves(s, windows[s - 1]) for s in range(1, nc)]
     again, extra = lax.optimization_barrier((x, extra))
-    kept = halves(0, again)
+    kept = halves(0, lax.optimization_barrier(window(0, again)))
     got = []
-    for r in range(2):
-        parts = [kept[r]] + [lax.ppermute(sent[s - 1][r], columns, [(i, (i + s) % nc) for i in range(nc)]) for s in range(1, nc)]
-        got.append(in_order(parts, columns))
+    for r_ in range(2):
+        parts = [kept[r_]] + [lax.ppermute(sent[s - 1][r_], columns, [(i, (i + s) % nc) for i in range(nc)]) for s in range(1, nc)]
+        got.append(by_origin(parts, columns, 1))
     near, far = pairings(nr)
     one = lax.ppermute(got[0], rows, near)
     two = lax.ppermute(got[1], rows, far)
-    two, one = lax.optimization_barrier((two, one))
     before, after = beside(one, two, rows)
-    whole = jnp.where(odd, jnp.concatenate(got, 1), jnp.concatenate(got[::-1], 1))
-    return jnp.concatenate([before, whole, after], 1), extra
-
-
-def spread(source, rows, at, sides, info, x3, ef, e3, eb):
-    H, Wp, C = source.shape[1:]
-    own = Wp - 4
-
-    def step(d):
-        x, row = source[d], at + d
-        for c in range(3):
-            x3[row, :, :, c * C:(c + 1) * C] = x[:, 1 + c:1 + c + own, :]
+    inner = jnp.where(odd, jnp.stack(got), jnp.stack(got[::-1]))
+    return jnp.concatenate([before[None], inner, after[None]], 0), extra
+
+
+def depth_rows(pairs, first, depth, own):
+    ends = pairs.shape[1] // depth // 2 - own
+    at = 2 * first * own, 2 * (depth * own + first * ends)
+    main = pairs[:, at[0]:at[0] + 4 * own].reshape(-1, pairs.shape[2])
+    return jnp.concatenate([main, pairs[:, at[1]:at[1] + 4 * ends].reshape(-1, pairs.shape[2])], 0)
+
+
+def from_pairs(ref, own, depth):
+    def row(d):
+        pairs, C = ref.shape[0], ref.shape[2]
+        ends = ref.shape[1] // depth // 2 - own
+        main = [ref[p, 2 * d * own:2 * (d + 1) * own, :].reshape(2, own, C) for p in range(pairs)]
+        tail = [ref[p, 2 * depth * own:, :].astype(jnp.float32)[2 * d * ends:2 * (d + 1) * ends] for p in range(pairs)]
+        return jnp.concatenate(main, 0), tail
+    return row
+
+
+def from_rows(ref, own, pairs):
+    def row(d):
+        C = ref.shape[1]
+        ends = ref.shape[0] // pairs // 4 - own
+        main = [ref[(2 * p + d) * 2 * own:(2 * p + d + 1) * 2 * own, :].reshape(2, own, C) for p in range(pairs)]
+        tail = ref[4 * pairs * own:, :].astype(jnp.float32)
+        return jnp.concatenate(main, 0), [tail[(2 * p + d) * 2 * ends:(2 * p + d + 1) * 2 * ends] for p in range(pairs)]
+    return row
+
+
+def either(odd, one, two):
+    return jax.tree.map(lambda a, b: jnp.where(odd == 1, a, b), one, two)
+
+
+def spread(source, rows, at, sides, info, x3, ef, et, eb):
+    H, own, C = x3.shape[1], x3.shape[2], x3.shape[3] // 3
+    column = lax.broadcasted_iota(jnp.int32, (own, C), 0)
+    f, none = info[4], jnp.zeros((H, C), jnp.float32)
+    ends = 2 * sides
+    for d in range(rows):
+        x, tail = source(d)
+        row = at + d
+        picks = [x[:, own - 1:own, :], x[:, 0:1, :]]
+        if sides == 1:
+            picks = [jnp.where(f == 0, picks[0], picks[1])]
+        edge = [[] for _ in range(ends + len(picks))]
+        for l in range(0, C, 128):
+            for p, part in enumerate(tail):
+                et[l // 128, 2 * p * ends:2 * (p + 1) * ends, :] = part[:, l:l + 128]
+            for e in range(ends):
+                edge[e].append(et[l // 128, pl.ds(e, H, stride=ends), :])
+            for k, pick in enumerate(picks):
+                for h in range(H):
+                    ef[k, l // 128, h * 8:h * 8 + 1, :] = pick[h, :, l:l + 128].astype(jnp.float32)
+                edge[ends + k].append(ef[k, l // 128, pl.ds(0, H, stride=8), :])
+        edge = [jnp.concatenate(e, 1) for e in edge]
+        if sides == 1:
+            e0, e1, inner = edge
+            left, right = jnp.where(f == 0, none, e1), jnp.where(f == 0, e0, none)
+            taps = [[jnp.where(f == 0, inner, e0), jnp.where(f == 0, e0, e1), jnp.where(f == 0, e1, inner)]]
+        else:
+            l0, l1, r0, r1, last, first = edge
+            left, right = l1, r0
+            taps = [[l0, l1, first], [last, r0, r1]]
         for s in range(sides):
-            low, high = x[:, 0:3, :], x[:, Wp - 3:Wp, :]
-            pick = jnp.where(info[4] == 0, high, low) if sides == 1 else (low, high)[s]
-            pick = pick.astype(jnp.float32)
-            for l in range(0, C, 128):
-                for h in range(H):
-                    ef[s, l // 128, pl.ds(h * 8, 3), :] = pick[h, :, l:l + 128]
-                for c in range(3):
-                    e3[s, 0:H, c * C + l:c * C + l + 128] = ef[s, l // 128, pl.ds(c, H, stride=8), :]
+            wide = jnp.concatenate(taps[s], 1)
             for b in range(3):
-                eb[s, b, row] = e3[s, b:b + H, :].astype(jnp.bfloat16)
-
-    for d in range(rows):
-        step(d)
+                moved = wide if b == 0 else pltpu.roll(wide, H - b, 0)
+                eb[s, b, row] = moved.astype(jnp.bfloat16)
+        for h in range(H):
+            line = x[h].astype(jnp.float32)
+            x3[row, h, :, 0:C] = jnp.where(column == 0, left[h:h + 1], pltpu.roll(line, 1, 0)).astype(jnp.bfloat16)
+            x3[row, h, :, C:2 * C] = x[h]
+            x3[row, h, :, 2 * C:] = jnp.where(column == own - 1, right[h:h + 1], pltpu.roll(line, own - 1, 0)).astype(jnp.bfloat16)
 
 
 def clear(rows, at, x3, eb):
@@ -191,17 +256,17 @@
             end * (1 - odd), jnp.where(odd == 1, end, start))
 
 
-def near_kernel(sides, xc, xn, k0, k1h, b1, k2h, b2, o_ref, keep, k1, k2, x3, ef, e3, eb, h3, raw, ends, total, sems):
+def near_kernel(sides, depth, xc, xn, k0, k1h, b1, k2h, b2, o_ref, keep, k1, k2, x3, ef, et, eb, h3, raw, ends, total, sems):
     copies = [pltpu.make_async_copy(k1h.at[a], k1.at[a], sems.at[a]) for a in range(3)]
     copies += [pltpu.make_async_copy(k2h.at[a], k2.at[a], sems.at[3 + a]) for a in range(3)]
     for copy in copies[1:3]:
         copy.start()
-    D, H, own = xc.shape[0], xc.shape[1], xc.shape[2] - 4
+    D, H, own = depth, x3.shape[1], x3.shape[2]
     info = places(D)
     odd = info[6]
-    scratch = (x3, ef, e3, eb)
-    spread(xc, D, 2 * odd, sides, info, *scratch)
-    spread(xn, 2, D * (1 - odd), sides, info, *scratch)
+    scratch = (x3, ef, et, eb)
+    spread(from_pairs(xc, own, D), D, 2 * odd, sides, info, *scratch)
+    spread(from_rows(xn, own, H // 2), 2, D * (1 - odd), sides, info, *scratch)
 
     @pl.when(info[7] > 0)
     def _():
@@ -240,13 +305,14 @@
         features(feature_sums(range(3), h3, k2, jnp.zeros(total.shape, jnp.float32)), b2, o_ref)
 
 
-def far_kernel(sides, xc, xf, keep, k1, b1, k2, b2, o_ref, x3, ef, e3, eb, h3, raw, ends, total):
-    D, H, own = xc.shape[0], xc.shape[1], xc.shape[2] - 4
+def far_kernel(sides, depth, xc, xf, keep, k1, b1, k2, b2, o_ref, x3, ef, et, eb, h3, raw, ends, total):
+    D, H, own = depth, x3.shape[1], x3.shape[2]
     info = places(D)
     odd = info[6]
-    scratch = (x3, ef, e3, eb)
-    spread(xc.at[pl.ds((D - 2) * odd, 2)], 2, 2 * (1 - odd), sides, info, *scratch)
-    spread(xf, 2, 2 * odd, sides, info, *scratch)
+    scratch = (x3, ef, et, eb)
+    tall = from_pairs(xc, own, D)
+    spread(lambda d: either(odd, tall(D - 2 + d), tall(d)), 2, 2 * (1 - odd), sides, info, *scratch)
+    spread(from_rows(xf, own, H // 2), 2, 2 * odd, sides, info, *scratch)
 
     @pl.when(info[8] > 0)
     def _():
@@ -268,15 +334,14 @@
         features(feature_sums(range(3), h3, k2, jnp.zeros(total.shape, jnp.float32)), b2, o_ref)
 
 
-def kernel_call(kernel, name, rows, sides, xc, near, operands):
-    D, H, Wp, C = xc.shape
-    own = Wp - 4
+def kernel_call(kernel, name, rows, sides, shape, near, operands):
+    D, H, own, C = shape
     weights = jax.ShapeDtypeStruct((3, 3, 3, C, C), jnp.bfloat16)
     out = [jax.ShapeDtypeStruct((2, H - 4, own, C), jnp.bfloat16)]
     scratch = [
         pltpu.VMEM((rows, H, own, 3 * C), jnp.bfloat16),
         pltpu.VMEM((sides, C // 128, H * 8, 128), jnp.float32),
-        pltpu.VMEM((sides, 2 * H, 3 * C), jnp.float32),
+        pltpu.VMEM((C // 128, 2 * sides * H, 128), jnp.float32),
         pltpu.VMEM((sides, 3, rows, H, 3 * C), jnp.bfloat16),
         pltpu.VMEM((4, H - 2, own, 3 * C), jnp.bfloat16),
         pltpu.VMEM((rows - 2, (H - 2) * own, C), jnp.float32),
@@ -290,7 +355,7 @@
         specs[3] = specs[5] = HBM
     hid = (rows - 2) * (H - 2) * own
     return pl.pallas_call(
-        functools.partial(kernel, sides),
+        functools.partial(kernel, sides, D),
         out_shape=out,
         in_specs=specs,
         out_specs=[VMEM] * len(out),
@@ -307,13 +372,15 @@
     sides = 1 if lax.axis_size("filt") == 2 else 2
 
     tall, k0 = gathered(volume, "filt", "height", kernel_one[:1])
-    near, far = exchange(tall[:2], tall[-2:], "depth")
-    out_near, keep, k1, k2 = kernel_call(near_kernel, "near", rows + 2, sides, tall, True, (tall, near, k0, kernel_one, b1, kernel_two, b2))
+    own, wide = volume.shape[2] // lax.axis_size("filt"), bias_one.shape[0]
+    shape = (rows, volume.shape[1] + 4, own, wide)
+    near, far = exchange(depth_rows(tall, 0, rows, own), depth_rows(tall, rows - 2, rows, own), "depth")
+    out_near, keep, k1, k2 = kernel_call(near_kernel, "near", rows + 2, sides, shape, True, (tall, near, k0, kernel_one, b1, kernel_two, b2))
     shard = volume.shape[3]
     def pieces(y):
         f, n = lax.axis_index("filt"), lax.axis_size("filt")
         return [lax.dynamic_slice_in_dim(y, (f + s) % n * shard, shard, 3) for s in range(n)]
-    out_far, = kernel_call(far_kernel, "far", 4, sides, tall, False, (tall, far, keep, k1, b1, k2, b2))
+    out_far, = kernel_call(far_kernel, "far", 4, sides, shape, False, (tall, far, keep, k1, b1, k2, b2))
     out = jnp.where(odd == 1, jnp.concatenate([out_near, out_far], 0), jnp.concatenate([out_far, out_near], 0))
     return by_origin(swapped(pieces(out), "filt"), "filt", 2)
 

time: 34 us -> 32.8 us (0.965)
  the two profiles are of different devices: /device:TPU:1 before, /device:TPU:18 now
where the time goes in v8:
time: 32.8 us; the launch traced here: 32.3 us
  waiting for transfers between devices  10.1 us (31%)
  starting transfers between devices  9.55 us (29%)
  Pallas kernels  8.38 us (26%)
  other arithmetic  2.49 us (8%)
  local copies, waits for them, and re-layouts  1.5 us (5%)
    pallas_call x2, Pallas kernels, kernel_call(): pl.pallas_call(functools.partial(kernel, sides, D), out_shape=out, in_spe...  8.38 us
    ppermute x1, waiting for transfers between devices, swapped(): lax.ppermute(pieces[s], axis, moves[s])  3.73 us
    ppermute x1, waiting for transfers between devices, gathered(): two = lax.ppermute(got[1], rows, far)  3.52 us
    ppermute x1, starting transfers between devices, exchange(): two = lax.ppermute(jnp.where(odd, last, first), axis, far)  2.52 us
    ppermute x2, starting transfers between devices, gathered(): lax.ppermute(sent[s - 1][r_], columns, [(i, (i + s) % nc) for i in range(...  2.09 us
    ppermute x1, starting transfers between devices, gathered(): two = lax.ppermute(got[1], rows, far)  1.92 us
    ppermute x1, starting transfers between devices, gathered(): one = lax.ppermute(got[0], rows, near)  1.64 us
    ppermute x1, waiting for transfers between devices, gathered(): one = lax.ppermute(got[0], rows, near)  1.37 us
  transfers between devices with their start and end apart: 7, of which 5 were waited for; matrix products, arithmetic and copies ran while one was open for 5% of the time, Pallas kernels for 16%

profile of v8, /device:TPU:18, one launch (start us, length us, event | category | flops | bytes accessed | tf_op | source)
XLA Modules:
  0.0 32.3 jit_solution(13728541480113648985)
XLA Ops:
  0.0 0.0 copy-start.2
  0.0 1.1 %slice_select_fusion = bf16[4,4,40,128]{3,2,1,0:T(8,128)(2,1)S(1)} fusion(bf16[4,4,64,128]{3,2,1,0:T(8,128)(2,1)} %param.5, pred[]{:T(512)S(6)} %eq.45), kind=kLoop, calls=%fused_computation.8 | loop fusion | flops 81920 | bytes 491521 | tf_op jit(solution)/shard_map/jit(_where)/select_n | solution.py:73
  1.2 1.6 %collective-permute-start = (bf16[272,128]{1,0:T(8,128)(2,1)S(1)}, bf16[272,128]{1,0:T(8,128)(2,1)S(1)}, u32[]{:S(2)}, u32[]{:S(2)}) collective-permute-start(bf16[272,128]{1,0:T(8,128)(2,1)S(1)} %get-tuple-element.29), channel_id=1, source_target_pairs={{0,1},{1,0},{2,3},{3,2},{4,5},{5,4},{6,7},{7,6},{8,9},{9,8},{10,11... | collective-permute-start | bytes 208904 | tf_op jit(solution)/shard_map/ppermute | solution.py:96
  2.8 0.5 %collective-permute-start.2 = (bf16[272,128]{1,0:T(8,128)(2,1)S(1)}, bf16[272,128]{1,0:T(8,128)(2,1)S(1)}, u32[]{:S(2)}, u32[]{:S(2)}) collective-permute-start(bf16[272,128]{1,0:T(8,128)(2,1)S(1)} %get-tuple-element.30), channel_id=1, source_target_pairs={{0,1},{1,0},{2,3},{3,2},{4,5},{5,4},{6,7},{7,6},{8,9},{9,8},{10,11... | collective-permute-start | bytes 208904 | tf_op jit(solution)/shard_map/ppermute | solution.py:96
  3.3 1.3 %slice.75.k0 = bf16[1,3,3,256,256]{4,3,2,1,0:T(8,128)(2,1)S(1)} slice(bf16[3,3,3,256,256]{4,3,2,1,0:T(8,128)(2,1)} %k1h.1), slice={[0:1], [0:3], [0:3], [0:256], [0:256]} | slice | bytes 2359296 | tf_op jit(solution)/shard_map/slice | solution.py:374
  4.7 0.0 copy-done.2
  4.7 0.0 copy-start
  4.7 0.0 copy-start.1
  4.9 1.4 %collective-permute-done = bf16[272,128]{1,0:T(8,128)(2,1)S(1)} collective-permute-done((bf16[272,128]{1,0:T(8,128)(2,1)S(1)}, bf16[272,128]{1,0:T(8,128)(2,1)S(1)}, u32[]{:S(2)}, u32[]{:S(2)}) %collective-permute-start) | collective-permute-done | bytes 69664 | tf_op jit(solution)/shard_map/ppermute | solution.py:96
  6.3 1.6 %collective-permute-start.1 = (bf16[272,256]{1,0:T(8,128)(2,1)S(1)}, bf16[272,256]{1,0:T(8,128)(2,1)S(1)}, u32[]{:S(2)}, u32[]{:S(2)}) collective-permute-start(bf16[272,256]{1,0:T(8,128)(2,1)S(1)} %maximum_select_fusion.3), channel_id=1, source_target_pairs={{0,2},{4,6},{2,0},{6,4},{1,3},{5,7},{3,1},{7,5},{8,10},{12,14},{10... | collective-permute-start | bytes 417800 | tf_op jit(solution)/shard_map/ppermute | solution.py:99
  7.9 0.0 collective-permute-done.2
  8.0 1.9 %collective-permute-start.3 = (bf16[272,256]{1,0:T(8,128)(2,1)S(1)}, bf16[272,256]{1,0:T(8,128)(2,1)S(1)}, u32[]{:S(2)}, u32[]{:S(2)}) collective-permute-start(bf16[272,256]{1,0:T(8,128)(2,1)S(1)} %maximum_select_fusion.4), channel_id=1, source_target_pairs={{2,4},{4,2},{0,0},{6,6},{3,5},{5,3},{1,1},{7,7},{10,12},{12,10},{8... | collective-permute-start | bytes 417800 | tf_op jit(solution)/shard_map/ppermute | solution.py:100
  10.0 1.4 %collective-permute-done.1 = bf16[272,256]{1,0:T(8,128)(2,1)S(1)} collective-permute-done((bf16[272,256]{1,0:T(8,128)(2,1)S(1)}, bf16[272,256]{1,0:T(8,128)(2,1)S(1)}, u32[]{:S(2)}, u32[]{:S(2)}) %collective-permute-start.1) | collective-permute-done | bytes 139296 | tf_op jit(solution)/shard_map/ppermute | solution.py:99
  11.4 3.5 %collective-permute-done.3 = bf16[272,256]{1,0:T(8,128)(2,1)S(1)} collective-permute-done((bf16[272,256]{1,0:T(8,128)(2,1)S(1)}, bf16[272,256]{1,0:T(8,128)(2,1)S(1)}, u32[]{:S(2)}, u32[]{:S(2)}) %collective-permute-start.3) | collective-permute-done | bytes 139296 | tf_op jit(solution)/shard_map/ppermute | solution.py:100
  15.0 0.1 pad_maximum_fusion.xc
  15.1 0.1 broadcast_select_fusion.1
  15.2 0.1 collective-permute-start.4
  15.3 2.5 %collective-permute-start.5 = (bf16[544,256]{1,0:T(8,128)(2,1)S(1)}, bf16[544,256]{1,0:T(8,128)(2,1)S(1)}, u32[]{:S(2)}, u32[]{:S(2)}) collective-permute-start(bf16[544,256]{1,0:T(8,128)(2,1)S(1)} %get-tuple-element.18), channel_id=1, source_target_pairs={{8,16},{16,8},{0,0},{24,24},{9,17},{17,9},{1,1},{25,25},{10,18},{1... | collective-permute-start | bytes 835592 | tf_op jit(solution)/shard_map/ppermute | solution.py:31
  17.8 0.0 collective-permute-done.4.xn
  17.8 0.0 copy-done
  17.8 0.0 copy-done.1
  17.8 5.2 %near.1 = (bf16[2,4,32,256]{3,2,1,0:T(8,128)(2,1)S(1)}, bf16[2,6,32,768]{3,2,1,0:T(8,128)(2,1)S(1)}, bf16[3,3,3,256,256]{4,3,2,1,0:T(8,128)(2,1)S(1)}, bf16[3,3,3,256,256]{4,3,2,1,0:T(8,128)(2,1)S(1)}) custom-call(bf16[4,272,256]{2,1,0:T(8,128)(2,1)S(1)} %pad_maximum_fusion.xc, bf16[544,256]{1,0:T(8,128)(2,1)S(1)} %collective-permute-done.4.xn, ...), custom_call_target="tpu_custom_call" | custom-call | flops 3623878656 | bytes 1048576 | tf_op jit(solution)/shard_map/near/pallas_call | solution.py:357
  23.0 0.1 collective-permute-done.5.xf
  23.2 3.2 %far.1 = bf16[2,4,32,256]{3,2,1,0:T(8,128)(2,1)S(1)} custom-call(bf16[4,272,256]{2,1,0:T(8,128)(2,1)S(1)} %pad_maximum_fusion.xc, bf16[544,256]{1,0:T(8,128)(2,1)S(1)} %collective-permute-done.5.xf, bf16[2,6,32,768]{3,2,1,0:T(8,128)(2,1)S(1)} %get-tuple-element.14.keep, bf16[3,3,3,256,256]{4,3,2,1,0:T(8,128)(2,1)S(1)} %get-tuple-element.15.k1, ...), custom_call_target="tpu_custom_call" | custom-call | flops 2264924160 | bytes 1048576 | tf_op jit(solution)/shard_map/far/pallas_call | solution.py:357
  26.4 0.1 constant_dynamic-slice_fusion.1
  26.5 1.3 %collective-permute-start.6 = (bf16[4,4,32,128]{3,2,1,0:T(8,128)(2,1)S(1)}, bf16[4,4,32,128]{3,2,1,0:T(8,128)(2,1)S(1)}, u32[]{:S(2)}, u32[]{:S(2)}) collective-permute-start(bf16[4,4,32,128]{3,2,1,0:T(8,128)(2,1)S(1)} %get-tuple-element.26), channel_id=1, source_target_pairs={{0,1},{1,0},{2,3},{3,2},{4,5},{5,4},{6,7},{7,6},{8,9},{9,8},{10,11... | collective-permute-start | bytes 393224 | tf_op jit(solution)/shard_map/ppermute | solution.py:57
  27.8 3.7 %collective-permute-done.6 = bf16[4,4,32,128]{3,2,1,0:T(8,128)(2,1)S(1)} collective-permute-done((bf16[4,4,32,128]{3,2,1,0:T(8,128)(2,1)S(1)}, bf16[4,4,32,128]{3,2,1,0:T(8,128)(2,1)S(1)}, u32[]{:S(2)}, u32[]{:S(2)}) %collective-permute-start.6) | collective-permute-done | bytes 131104 | tf_op jit(solution)/shard_map/ppermute | solution.py:57
  31.5 0.8 %maximum_select_fusion.2 = bf16[4,4,64,128]{3,2,1,0:T(8,128)(2,1)} fusion(bf16[4,4,32,128]{3,2,1,0:T(8,128)(2,1)S(1)} %collective-permute-done.6, bf16[4,4,32,128]{3,2,1,0:T(8,128)(2,1)S(1)} %get-tuple-element.25, pred[]{:T(512)S(6)} %eq.40), kind=kLoop, calls=%fused_computation.7 | loop fusion | flops 1179648 | bytes 524289 | tf_op jit(solution)/shard_map/jit(_where)/select_n | solution.py:48
  (20 shorter events, 0.5 us)
Async XLA Ops:
  0.0 4.7 %copy-start.2 = (bf16[4,4,64,128]{3,2,1,0:T(8,128)(2,1)S(1)}, bf16[4,4,64,128]{3,2,1,0:T(8,128)(2,1)}, u32[]{:S(2)}) copy-start(bf16[4,4,64,128]{3,2,1,0:T(8,128)(2,1)} %param.5) | copy-start | bytes 786436
  1.2 5.0 %collective-permute-start = (bf16[272,128]{1,0:T(8,128)(2,1)S(1)}, bf16[272,128]{1,0:T(8,128)(2,1)S(1)}, u32[]{:S(2)}, u32[]{:S(2)}) collective-permute-start(bf16[272,128]{1,0:T(8,128)(2,1)S(1)} %get-tuple-element.29), channel_id=1, source_target_pairs={{0,1},{1,0},{2,3},{3,2},{4,5},{5,4},{6,7},{7,6},{8,9},{9,8},{10,11... | collective-permute-start | bytes 208904 | tf_op jit(solution)/shard_map/ppermute | solution.py:96
  2.8 5.1 %collective-permute-start.2 = (bf16[272,128]{1,0:T(8,128)(2,1)S(1)}, bf16[272,128]{1,0:T(8,128)(2,1)S(1)}, u32[]{:S(2)}, u32[]{:S(2)}) collective-permute-start(bf16[272,128]{1,0:T(8,128)(2,1)S(1)} %get-tuple-element.30), channel_id=1, source_target_pairs={{0,1},{1,0},{2,3},{3,2},{4,5},{5,4},{6,7},{7,6},{8,9},{9,8},{10,11... | collective-permute-start | bytes 208904 | tf_op jit(solution)/shard_map/ppermute | solution.py:96
  4.7 13.2 %copy-start = (f32[256]{0:T(256)S(1)}, f32[256]{0:T(256)}, u32[]{:S(2)}) copy-start(f32[256]{0:T(256)} %param.7) | copy-start | bytes 3076
  4.7 13.1 %copy-start.1 = (f32[256]{0:T(256)S(1)}, f32[256]{0:T(256)}, u32[]{:S(2)}) copy-start(f32[256]{0:T(256)} %param.9) | copy-start | bytes 3076
  6.3 5.1 %collective-permute-start.1 = (bf16[272,256]{1,0:T(8,128)(2,1)S(1)}, bf16[272,256]{1,0:T(8,128)(2,1)S(1)}, u32[]{:S(2)}, u32[]{:S(2)}) collective-permute-start(bf16[272,256]{1,0:T(8,128)(2,1)S(1)} %maximum_select_fusion.3), channel_id=1, source_target_pairs={{0,2},{4,6},{2,0},{6,4},{1,3},{5,7},{3,1},{7,5},{8,10},{12,14},{10... | collective-permute-start | bytes 417800 | tf_op jit(solution)/shard_map/ppermute | solution.py:99
  8.0 6.9 %collective-permute-start.3 = (bf16[272,256]{1,0:T(8,128)(2,1)S(1)}, bf16[272,256]{1,0:T(8,128)(2,1)S(1)}, u32[]{:S(2)}, u32[]{:S(2)}) collective-permute-start(bf16[272,256]{1,0:T(8,128)(2,1)S(1)} %maximum_select_fusion.4), channel_id=1, source_target_pairs={{2,4},{4,2},{0,0},{6,6},{3,5},{5,3},{1,1},{7,7},{10,12},{12,10},{8... | collective-permute-start | bytes 417800 | tf_op jit(solution)/shard_map/ppermute | solution.py:100
  15.2 2.6 %collective-permute-start.4 = (bf16[544,256]{1,0:T(8,128)(2,1)S(1)}, bf16[544,256]{1,0:T(8,128)(2,1)S(1)}, u32[]{:S(2)}, u32[]{:S(2)}) collective-permute-start(bf16[544,256]{1,0:T(8,128)(2,1)S(1)} %get-tuple-element.17), channel_id=1, source_target_pairs={{0,8},{16,24},{8,0},{24,16},{1,9},{17,25},{9,1},{25,17},{2,10},{18... | collective-permute-start | bytes 835592 | tf_op jit(solution)/shard_map/ppermute | solution.py:30
  15.3 7.9 %collective-permute-start.5 = (bf16[544,256]{1,0:T(8,128)(2,1)S(1)}, bf16[544,256]{1,0:T(8,128)(2,1)S(1)}, u32[]{:S(2)}, u32[]{:S(2)}) collective-permute-start(bf16[544,256]{1,0:T(8,128)(2,1)S(1)} %get-tuple-element.18), channel_id=1, source_target_pairs={{8,16},{16,8},{0,0},{24,24},{9,17},{17,9},{1,1},{25,25},{10,18},{1... | collective-permute-start | bytes 835592 | tf_op jit(solution)/shard_map/ppermute | solution.py:31
  26.5 5.0 %collective-permute-start.6 = (bf16[4,4,32,128]{3,2,1,0:T(8,128)(2,1)S(1)}, bf16[4,4,32,128]{3,2,1,0:T(8,128)(2,1)S(1)}, u32[]{:S(2)}, u32[]{:S(2)}) collective-permute-start(bf16[4,4,32,128]{3,2,1,0:T(8,128)(2,1)S(1)} %get-tuple-element.26), channel_id=1, source_target_pairs={{0,1},{1,0},{2,3},{3,2},{4,5},{5,4},{6,7},{7,6},{8,9},{9,8},{10,11... | collective-permute-start | bytes 393224 | tf_op jit(solution)/shard_map/ppermute | solution.py:57

commit v9 on v8

--- a/solution.py
+++ b/solution.py
@@ -232,12 +232,12 @@
         ends[...] = acc[main:]
 
 
-def feature_sums(taps, h3, k2, acc):
-    H1, own, C = h3.shape[1], h3.shape[2], h3.shape[3] // 3
-    H0 = H1 - 2
-    for a in taps:
+def feature_sums(terms, k2, acc):
+    for pair, a in terms:
+        H1, own, C = pair.shape[1], pair.shape[2], pair.shape[3] // 3
+        H0 = H1 - 2
         for b in range(3):
-            lhs = h3[a:a + 2, b:b + H0].reshape(2 * H0 * own, 3 * C)
+            lhs = pair[:, b:b + H0].reshape(2 * H0 * own, 3 * C)
             acc += jnp.dot(lhs, k2[a, b].reshape(3 * C, C), preferred_element_type=jnp.float32)
     return acc
 
@@ -302,7 +302,7 @@
     @block
     def _():
         keep[...] = h3[pl.ds((D - 2) * odd, 2)]
-        features(feature_sums(range(3), h3, k2, jnp.zeros(total.shape, jnp.float32)), b2, o_ref)
+        features(feature_sums([(h3.at[a:a + 2], a) for a in range(3)], k2, jnp.zeros(total.shape, jnp.float32)), b2, o_ref)
 
 
 def far_kernel(sides, depth, xc, xf, keep, k1, b1, k2, b2, o_ref, x3, ef, et, eb, h3, raw, ends, total):
@@ -311,16 +311,19 @@
     odd = info[6]
     scratch = (x3, ef, et, eb)
     tall = from_pairs(xc, own, D)
-    spread(lambda d: either(odd, tall(D - 2 + d), tall(d)), 2, 2 * (1 - odd), sides, info, *scratch)
-    spread(from_rows(xf, own, H // 2), 2, 2 * odd, sides, info, *scratch)
+    first = info[0] - 1 + D * odd
+    known = 2 * (1 - odd)
+
+    @pl.when(odd >= 0)
+    def _():
+        spread(lambda d: either(odd, tall(D - 2 + d), tall(d)), 2, 2 * (1 - odd), sides, info, *scratch)
+        spread(from_rows(xf, own, H // 2), 2, 2 * odd, sides, info, *scratch)
+        total[...] = feature_sums([(keep, known)], k2, jnp.zeros(total.shape, jnp.float32))
+        h3[pl.ds(known, 2)] = keep[...]
 
     @pl.when(info[8] > 0)
     def _():
         clear(2, 2 * odd, x3, eb)
-
-    h3[pl.ds(2 * (1 - odd), 2)] = keep[...]
-
-    first = info[0] - 1 + D * odd
 
     @pl.when(odd >= 0)
     def _():
@@ -331,7 +334,7 @@
 
     @pl.when(odd >= 0)
     def _():
-        features(feature_sums(range(3), h3, k2, jnp.zeros(total.shape, jnp.float32)), b2, o_ref)
+        features(feature_sums([(h3.at[1:3], 1), (h3.at[pl.ds(2 * odd, 2)], 2 * odd)], k2, total[...]), b2, o_ref)
 
 
 def kernel_call(kernel, name, rows, sides, shape, near, operands):

time: 32.8 us -> 32.7 us (level)
  no operation moved by 1% of the time
where the time goes in v9:
time: 32.7 us; the launch traced here: 32.2 us
  waiting for transfers between devices  10.1 us (31%)
  starting transfers between devices  9.55 us (29%)
  Pallas kernels  8.22 us (25%)
  other arithmetic  2.49 us (8%)
  local copies, waits for them, and re-layouts  1.5 us (5%)
    pallas_call x2, Pallas kernels, kernel_call(): pl.pallas_call(functools.partial(kernel, sides, D), out_shape=out, in_spe...  8.22 us
    ppermute x1, waiting for transfers between devices, swapped(): lax.ppermute(pieces[s], axis, moves[s])  3.73 us
    ppermute x1, waiting for transfers between devices, gathered(): two = lax.ppermute(got[1], rows, far)  3.52 us
    ppermute x1, starting transfers between devices, exchange(): two = lax.ppermute(jnp.where(odd, last, first), axis, far)  2.52 us
    ppermute x2, starting transfers between devices, gathered(): lax.ppermute(sent[s - 1][r_], columns, [(i, (i + s) % nc) for i in range(...  2.09 us
    ppermute x1, starting transfers between devices, gathered(): two = lax.ppermute(got[1], rows, far)  1.92 us
    ppermute x1, starting transfers between devices, gathered(): one = lax.ppermute(got[0], rows, near)  1.64 us
    ppermute x1, waiting for transfers between devices, gathered(): one = lax.ppermute(got[0], rows, near)  1.37 us
  transfers between devices with their start and end apart: 7, of which 5 were waited for; matrix products, arithmetic and copies ran while one was open for 5% of the time, Pallas kernels for 16%

profile of v9, /device:TPU:18, one launch (start us, length us, event | category | flops | bytes accessed | tf_op | source)
XLA Modules:
  0.0 32.2 jit_solution(5152885543346541944)
XLA Ops:
  0.0 0.0 copy-start.2
  0.0 1.1 %slice_select_fusion = bf16[4,4,40,128]{3,2,1,0:T(8,128)(2,1)S(1)} fusion(bf16[4,4,64,128]{3,2,1,0:T(8,128)(2,1)} %param.5, pred[]{:T(512)S(6)} %eq.45), kind=kLoop, calls=%fused_computation.8 | loop fusion | flops 81920 | bytes 491521 | tf_op jit(solution)/shard_map/jit(_where)/select_n | solution.py:73
  1.2 1.6 %collective-permute-start = (bf16[272,128]{1,0:T(8,128)(2,1)S(1)}, bf16[272,128]{1,0:T(8,128)(2,1)S(1)}, u32[]{:S(2)}, u32[]{:S(2)}) collective-permute-start(bf16[272,128]{1,0:T(8,128)(2,1)S(1)} %get-tuple-element.29), channel_id=1, source_target_pairs={{0,1},{1,0},{2,3},{3,2},{4,5},{5,4},{6,7},{7,6},{8,9},{9,8},{10,11... | collective-permute-start | bytes 208904 | tf_op jit(solution)/shard_map/ppermute | solution.py:96
  2.8 0.5 %collective-permute-start.2 = (bf16[272,128]{1,0:T(8,128)(2,1)S(1)}, bf16[272,128]{1,0:T(8,128)(2,1)S(1)}, u32[]{:S(2)}, u32[]{:S(2)}) collective-permute-start(bf16[272,128]{1,0:T(8,128)(2,1)S(1)} %get-tuple-element.30), channel_id=1, source_target_pairs={{0,1},{1,0},{2,3},{3,2},{4,5},{5,4},{6,7},{7,6},{8,9},{9,8},{10,11... | collective-permute-start | bytes 208904 | tf_op jit(solution)/shard_map/ppermute | solution.py:96
  3.3 1.3 %slice.75.k0 = bf16[1,3,3,256,256]{4,3,2,1,0:T(8,128)(2,1)S(1)} slice(bf16[3,3,3,256,256]{4,3,2,1,0:T(8,128)(2,1)} %k1h.1), slice={[0:1], [0:3], [0:3], [0:256], [0:256]} | slice | bytes 2359296 | tf_op jit(solution)/shard_map/slice | solution.py:377
  4.7 0.0 copy-done.2
  4.7 0.0 copy-start
  4.7 0.0 copy-start.1
  4.9 1.4 %collective-permute-done = bf16[272,128]{1,0:T(8,128)(2,1)S(1)} collective-permute-done((bf16[272,128]{1,0:T(8,128)(2,1)S(1)}, bf16[272,128]{1,0:T(8,128)(2,1)S(1)}, u32[]{:S(2)}, u32[]{:S(2)}) %collective-permute-start) | collective-permute-done | bytes 69664 | tf_op jit(solution)/shard_map/ppermute | solution.py:96
  6.3 1.6 %collective-permute-start.1 = (bf16[272,256]{1,0:T(8,128)(2,1)S(1)}, bf16[272,256]{1,0:T(8,128)(2,1)S(1)}, u32[]{:S(2)}, u32[]{:S(2)}) collective-permute-start(bf16[272,256]{1,0:T(8,128)(2,1)S(1)} %maximum_select_fusion.3), channel_id=1, source_target_pairs={{0,2},{4,6},{2,0},{6,4},{1,3},{5,7},{3,1},{7,5},{8,10},{12,14},{10... | collective-permute-start | bytes 417800 | tf_op jit(solution)/shard_map/ppermute | solution.py:99
  7.9 0.0 collective-permute-done.2
  8.0 1.9 %collective-permute-start.3 = (bf16[272,256]{1,0:T(8,128)(2,1)S(1)}, bf16[272,256]{1,0:T(8,128)(2,1)S(1)}, u32[]{:S(2)}, u32[]{:S(2)}) collective-permute-start(bf16[272,256]{1,0:T(8,128)(2,1)S(1)} %maximum_select_fusion.4), channel_id=1, source_target_pairs={{2,4},{4,2},{0,0},{6,6},{3,5},{5,3},{1,1},{7,7},{10,12},{12,10},{8... | collective-permute-start | bytes 417800 | tf_op jit(solution)/shard_map/ppermute | solution.py:100
  10.0 1.4 %collective-permute-done.1 = bf16[272,256]{1,0:T(8,128)(2,1)S(1)} collective-permute-done((bf16[272,256]{1,0:T(8,128)(2,1)S(1)}, bf16[272,256]{1,0:T(8,128)(2,1)S(1)}, u32[]{:S(2)}, u32[]{:S(2)}) %collective-permute-start.1) | collective-permute-done | bytes 139296 | tf_op jit(solution)/shard_map/ppermute | solution.py:99
  11.4 3.5 %collective-permute-done.3 = bf16[272,256]{1,0:T(8,128)(2,1)S(1)} collective-permute-done((bf16[272,256]{1,0:T(8,128)(2,1)S(1)}, bf16[272,256]{1,0:T(8,128)(2,1)S(1)}, u32[]{:S(2)}, u32[]{:S(2)}) %collective-permute-start.3) | collective-permute-done | bytes 139296 | tf_op jit(solution)/shard_map/ppermute | solution.py:100
  15.0 0.1 pad_maximum_fusion.xc
  15.1 0.1 broadcast_select_fusion.1
  15.2 0.1 collective-permute-start.4
  15.3 2.5 %collective-permute-start.5 = (bf16[544,256]{1,0:T(8,128)(2,1)S(1)}, bf16[544,256]{1,0:T(8,128)(2,1)S(1)}, u32[]{:S(2)}, u32[]{:S(2)}) collective-permute-start(bf16[544,256]{1,0:T(8,128)(2,1)S(1)} %get-tuple-element.18), channel_id=1, source_target_pairs={{8,16},{16,8},{0,0},{24,24},{9,17},{17,9},{1,1},{25,25},{10,18},{1... | collective-permute-start | bytes 835592 | tf_op jit(solution)/shard_map/ppermute | solution.py:31
  17.8 0.0 collective-permute-done.4.xn
  17.8 0.0 copy-done
  17.8 0.0 copy-done.1
  17.8 5.2 %near.1 = (bf16[2,4,32,256]{3,2,1,0:T(8,128)(2,1)S(1)}, bf16[2,6,32,768]{3,2,1,0:T(8,128)(2,1)S(1)}, bf16[3,3,3,256,256]{4,3,2,1,0:T(8,128)(2,1)S(1)}, bf16[3,3,3,256,256]{4,3,2,1,0:T(8,128)(2,1)S(1)}) custom-call(bf16[4,272,256]{2,1,0:T(8,128)(2,1)S(1)} %pad_maximum_fusion.xc, bf16[544,256]{1,0:T(8,128)(2,1)S(1)} %collective-permute-done.4.xn, ...), custom_call_target="tpu_custom_call" | custom-call | flops 3623878656 | bytes 1048576 | tf_op jit(solution)/shard_map/near/pallas_call | solution.py:360
  23.0 0.1 collective-permute-done.5.xf
  23.2 3.0 %far.1 = bf16[2,4,32,256]{3,2,1,0:T(8,128)(2,1)S(1)} custom-call(bf16[4,272,256]{2,1,0:T(8,128)(2,1)S(1)} %pad_maximum_fusion.xc, bf16[544,256]{1,0:T(8,128)(2,1)S(1)} %collective-permute-done.5.xf, bf16[2,6,32,768]{3,2,1,0:T(8,128)(2,1)S(1)} %get-tuple-element.14.keep, bf16[3,3,3,256,256]{4,3,2,1,0:T(8,128)(2,1)S(1)} %get-tuple-element.15.k1, ...), custom_call_target="tpu_custom_call" | custom-call | flops 2264924160 | bytes 1048576 | tf_op jit(solution)/shard_map/far/pallas_call | solution.py:360
  26.3 0.1 constant_dynamic-slice_fusion.1
  26.3 1.3 %collective-permute-start.6 = (bf16[4,4,32,128]{3,2,1,0:T(8,128)(2,1)S(1)}, bf16[4,4,32,128]{3,2,1,0:T(8,128)(2,1)S(1)}, u32[]{:S(2)}, u32[]{:S(2)}) collective-permute-start(bf16[4,4,32,128]{3,2,1,0:T(8,128)(2,1)S(1)} %get-tuple-element.26), channel_id=1, source_target_pairs={{0,1},{1,0},{2,3},{3,2},{4,5},{5,4},{6,7},{7,6},{8,9},{9,8},{10,11... | collective-permute-start | bytes 393224 | tf_op jit(solution)/shard_map/ppermute | solution.py:57
  27.6 3.7 %collective-permute-done.6 = bf16[4,4,32,128]{3,2,1,0:T(8,128)(2,1)S(1)} collective-permute-done((bf16[4,4,32,128]{3,2,1,0:T(8,128)(2,1)S(1)}, bf16[4,4,32,128]{3,2,1,0:T(8,128)(2,1)S(1)}, u32[]{:S(2)}, u32[]{:S(2)}) %collective-permute-start.6) | collective-permute-done | bytes 131104 | tf_op jit(solution)/shard_map/ppermute | solution.py:57
  31.4 0.8 %maximum_select_fusion.2 = bf16[4,4,64,128]{3,2,1,0:T(8,128)(2,1)} fusion(bf16[4,4,32,128]{3,2,1,0:T(8,128)(2,1)S(1)} %collective-permute-done.6, bf16[4,4,32,128]{3,2,1,0:T(8,128)(2,1)S(1)} %get-tuple-element.25, pred[]{:T(512)S(6)} %eq.40), kind=kLoop, calls=%fused_computation.7 | loop fusion | flops 1179648 | bytes 524289 | tf_op jit(solution)/shard_map/jit(_where)/select_n | solution.py:48
  (20 shorter events, 0.5 us)
Async XLA Ops:
  0.0 4.7 %copy-start.2 = (bf16[4,4,64,128]{3,2,1,0:T(8,128)(2,1)S(1)}, bf16[4,4,64,128]{3,2,1,0:T(8,128)(2,1)}, u32[]{:S(2)}) copy-start(bf16[4,4,64,128]{3,2,1,0:T(8,128)(2,1)} %param.5) | copy-start | bytes 786436
  1.2 5.0 %collective-permute-start = (bf16[272,128]{1,0:T(8,128)(2,1)S(1)}, bf16[272,128]{1,0:T(8,128)(2,1)S(1)}, u32[]{:S(2)}, u32[]{:S(2)}) collective-permute-start(bf16[272,128]{1,0:T(8,128)(2,1)S(1)} %get-tuple-element.29), channel_id=1, source_target_pairs={{0,1},{1,0},{2,3},{3,2},{4,5},{5,4},{6,7},{7,6},{8,9},{9,8},{10,11... | collective-permute-start | bytes 208904 | tf_op jit(solution)/shard_map/ppermute | solution.py:96
  2.8 5.1 %collective-permute-start.2 = (bf16[272,128]{1,0:T(8,128)(2,1)S(1)}, bf16[272,128]{1,0:T(8,128)(2,1)S(1)}, u32[]{:S(2)}, u32[]{:S(2)}) collective-permute-start(bf16[272,128]{1,0:T(8,128)(2,1)S(1)} %get-tuple-element.30), channel_id=1, source_target_pairs={{0,1},{1,0},{2,3},{3,2},{4,5},{5,4},{6,7},{7,6},{8,9},{9,8},{10,11... | collective-permute-start | bytes 208904 | tf_op jit(solution)/shard_map/ppermute | solution.py:96
  4.7 13.2 %copy-start = (f32[256]{0:T(256)S(1)}, f32[256]{0:T(256)}, u32[]{:S(2)}) copy-start(f32[256]{0:T(256)} %param.7) | copy-start | bytes 3076
  4.7 13.1 %copy-start.1 = (f32[256]{0:T(256)S(1)}, f32[256]{0:T(256)}, u32[]{:S(2)}) copy-start(f32[256]{0:T(256)} %param.9) | copy-start | bytes 3076
  6.3 5.1 %collective-permute-start.1 = (bf16[272,256]{1,0:T(8,128)(2,1)S(1)}, bf16[272,256]{1,0:T(8,128)(2,1)S(1)}, u32[]{:S(2)}, u32[]{:S(2)}) collective-permute-start(bf16[272,256]{1,0:T(8,128)(2,1)S(1)} %maximum_select_fusion.3), channel_id=1, source_target_pairs={{0,2},{4,6},{2,0},{6,4},{1,3},{5,7},{3,1},{7,5},{8,10},{12,14},{10... | collective-permute-start | bytes 417800 | tf_op jit(solution)/shard_map/ppermute | solution.py:99
  8.0 6.9 %collective-permute-start.3 = (bf16[272,256]{1,0:T(8,128)(2,1)S(1)}, bf16[272,256]{1,0:T(8,128)(2,1)S(1)}, u32[]{:S(2)}, u32[]{:S(2)}) collective-permute-start(bf16[272,256]{1,0:T(8,128)(2,1)S(1)} %maximum_select_fusion.4), channel_id=1, source_target_pairs={{2,4},{4,2},{0,0},{6,6},{3,5},{5,3},{1,1},{7,7},{10,12},{12,10},{8... | collective-permute-start | bytes 417800 | tf_op jit(solution)/shard_map/ppermute | solution.py:100
  15.2 2.6 %collective-permute-start.4 = (bf16[544,256]{1,0:T(8,128)(2,1)S(1)}, bf16[544,256]{1,0:T(8,128)(2,1)S(1)}, u32[]{:S(2)}, u32[]{:S(2)}) collective-permute-start(bf16[544,256]{1,0:T(8,128)(2,1)S(1)} %get-tuple-element.17), channel_id=1, source_target_pairs={{0,8},{16,24},{8,0},{24,16},{1,9},{17,25},{9,1},{25,17},{2,10},{18... | collective-permute-start | bytes 835592 | tf_op jit(solution)/shard_map/ppermute | solution.py:30
  15.3 7.9 %collective-permute-start.5 = (bf16[544,256]{1,0:T(8,128)(2,1)S(1)}, bf16[544,256]{1,0:T(8,128)(2,1)S(1)}, u32[]{:S(2)}, u32[]{:S(2)}) collective-permute-start(bf16[544,256]{1,0:T(8,128)(2,1)S(1)} %get-tuple-element.18), channel_id=1, source_target_pairs={{8,16},{16,8},{0,0},{24,24},{9,17},{17,9},{1,1},{25,25},{10,18},{1... | collective-permute-start | bytes 835592 | tf_op jit(solution)/shard_map/ppermute | solution.py:31
  26.3 5.0 %collective-permute-start.6 = (bf16[4,4,32,128]{3,2,1,0:T(8,128)(2,1)S(1)}, bf16[4,4,32,128]{3,2,1,0:T(8,128)(2,1)S(1)}, u32[]{:S(2)}, u32[]{:S(2)}) collective-permute-start(bf16[4,4,32,128]{3,2,1,0:T(8,128)(2,1)S(1)} %get-tuple-element.26), channel_id=1, source_target_pairs={{0,1},{1,0},{2,3},{3,2},{4,5},{5,4},{6,7},{7,6},{8,9},{9,8},{10,11... | collective-permute-start | bytes 393224 | tf_op jit(solution)/shard_map/ppermute | solution.py:57

commit v10 on v9

--- a/solution.py
+++ b/solution.py
@@ -217,9 +217,9 @@
         h3[at, h, :, 2 * C:] = jnp.where(column == own - 1, right, pltpu.roll(row, own - 1, 0)).astype(jnp.bfloat16)
 
 
-def hidden_part(d, taps, x3, eb, k1, bias, raw, ends):
+def hidden_part(d, taps, x3, eb, k1, bias, raw, ends, outer):
     main, C = raw.shape[1:]
-    size = ends.shape[0] if d == 0 else 0
+    size = ends.shape[0] if outer else 0
     if taps[0] == 0:
         acc = jnp.zeros((main + size, C), jnp.float32)
     else:
@@ -256,7 +256,7 @@
             end * (1 - odd), jnp.where(odd == 1, end, start))
 
 
-def near_kernel(sides, depth, xc, xn, k0, k1h, b1, k2h, b2, o_ref, keep, k1, k2, x3, ef, et, eb, h3, raw, ends, total, sems):
+def near_kernel(sides, depth, xc, xn, k0, k1h, b1, k2h, b2, o_ref, keep, part_sum, k1, k2, x3, ef, et, eb, h3, raw, ends, total, sems):
     copies = [pltpu.make_async_copy(k1h.at[a], k1.at[a], sems.at[a]) for a in range(3)]
     copies += [pltpu.make_async_copy(k2h.at[a], k2.at[a], sems.at[3 + a]) for a in range(3)]
     for copy in copies[1:3]:
@@ -265,12 +265,14 @@
     info = places(D)
     odd = info[6]
     scratch = (x3, ef, et, eb)
-    spread(from_pairs(xc, own, D), D, 2 * odd, sides, info, *scratch)
-    spread(from_rows(xn, own, H // 2), 2, D * (1 - odd), sides, info, *scratch)
-
-    @pl.when(info[7] > 0)
-    def _():
-        clear(2, D * (1 - odd), x3, eb)
+    tall, near = from_pairs(xc, own, D), from_rows(xn, own, H // 2)
+
+    def lay(r):
+        def source(_):
+            if r < 2:
+                return either(odd, near(r), tall(r))
+            return either(odd, tall(r - 2), tall(r) if r < D else near(r - D))
+        spread(source, 1, r, sides, info, *scratch)
 
     first = info[0] - 1 + 2 * (1 - odd)
 
@@ -278,7 +280,7 @@
         pl.when(odd >= 0)(run)
 
     def part(d, taps):
-        hidden_part(d, taps, x3, eb, k1 if taps[0] else k0, b1, raw, ends)
+        hidden_part(d, taps, x3, eb, k1 if taps[0] else k0, b1, raw, ends, d == (0 if taps[0] else D - 1))
 
     def rows(d):
         hidden_rows(d, d, first + d, sides, info, own, H, raw, ends, h3)
@@ -293,19 +295,30 @@
         @block
         def _():
             for d in range(D):
+                if a == 0:
+                    lay(d)
                 part(d, [a])
                 if a == 2:
                     rows(d)
+            if a == 0:
+                lay(D)
+                lay(D + 1)
+
+        if a == 0:
+            @pl.when(info[7] > 0)
+            def _():
+                clear(2, D, x3, eb)
     for copy in copies[3:] + copies[:1]:
         copy.wait()
 
     @block
     def _():
         keep[...] = h3[pl.ds((D - 2) * odd, 2)]
+        part_sum[...] = feature_sums([(h3.at[pl.ds((D - 2) * odd, 2)], 2 * (1 - odd))], k2, jnp.zeros(part_sum.shape, jnp.float32))
         features(feature_sums([(h3.at[a:a + 2], a) for a in range(3)], k2, jnp.zeros(total.shape, jnp.float32)), b2, o_ref)
 
 
-def far_kernel(sides, depth, xc, xf, keep, k1, b1, k2, b2, o_ref, x3, ef, et, eb, h3, raw, ends, total):
+def far_kernel(sides, depth, xc, xf, keep, part_sum, k1, b1, k2, b2, o_ref, x3, ef, et, eb, h3, raw, ends, total):
     D, H, own = depth, x3.shape[1], x3.shape[2]
     info = places(D)
     odd = info[6]
@@ -318,7 +331,6 @@
     def _():
         spread(lambda d: either(odd, tall(D - 2 + d), tall(d)), 2, 2 * (1 - odd), sides, info, *scratch)
         spread(from_rows(xf, own, H // 2), 2, 2 * odd, sides, info, *scratch)
-        total[...] = feature_sums([(keep, known)], k2, jnp.zeros(total.shape, jnp.float32))
         h3[pl.ds(known, 2)] = keep[...]
 
     @pl.when(info[8] > 0)
@@ -328,13 +340,13 @@
     @pl.when(odd >= 0)
     def _():
         for d in range(2):
-            hidden_part(d, range(3), x3, eb, k1, b1, raw, ends)
+            hidden_part(d, range(3), x3, eb, k1, b1, raw, ends, d == 0)
         for d in range(2):
             hidden_rows(d, 2 * odd + d, first + d, sides, info, own, H, raw, ends, h3)
 
     @pl.when(odd >= 0)
     def _():
-        features(feature_sums([(h3.at[1:3], 1), (h3.at[pl.ds(2 * odd, 2)], 2 * odd)], k2, total[...]), b2, o_ref)
+        features(feature_sums([(h3.at[1:3], 1), (h3.at[pl.ds(2 * odd, 2)], 2 * odd)], k2, part_sum[...]), b2, o_ref)
 
 
 def kernel_call(kernel, name, rows, sides, shape, near, operands):
@@ -353,7 +365,7 @@
     ]
     specs = [VMEM] * len(operands)
     if near:
-        out += [jax.ShapeDtypeStruct((2, H - 2, own, 3 * C), jnp.bfloat16), weights, weights]
+        out += [jax.ShapeDtypeStruct((2, H - 2, own, 3 * C), jnp.bfloat16), jax.ShapeDtypeStruct((2 * (H - 4) * own, C), jnp.float32), weights, weights]
         scratch.append(pltpu.SemaphoreType.DMA((6,)))
         specs[3] = specs[5] = HBM
     hid = (rows - 2) * (H - 2) * own
@@ -378,12 +390,12 @@
     own, wide = volume.shape[2] // lax.axis_size("filt"), bias_one.shape[0]
     shape = (rows, volume.shape[1] + 4, own, wide)
     near, far = exchange(depth_rows(tall, 0, rows, own), depth_rows(tall, rows - 2, rows, own), "depth")
-    out_near, keep, k1, k2 = kernel_call(near_kernel, "near", rows + 2, sides, shape, True, (tall, near, k0, kernel_one, b1, kernel_two, b2))
+    out_near, keep, part_sum, k1, k2 = kernel_call(near_kernel, "near", rows + 2, sides, shape, True, (tall, near, k0, kernel_one, b1, kernel_two, b2))
     shard = volume.shape[3]
     def pieces(y):
         f, n = lax.axis_index("filt"), lax.axis_size("filt")
         return [lax.dynamic_slice_in_dim(y, (f + s) % n * shard, shard, 3) for s in range(n)]
-    out_far, = kernel_call(far_kernel, "far", 4, sides, shape, False, (tall, far, keep, k1, b1, k2, b2))
+    out_far, = kernel_call(far_kernel, "far", 4, sides, shape, False, (tall, far, keep, part_sum, k1, b1, k2, b2))
     out = jnp.where(odd == 1, jnp.concatenate([out_near, out_far], 0), jnp.concatenate([out_far, out_near], 0))
     return by_origin(swapped(pieces(out), "filt"), "filt", 2)
 

time: 32.7 us -> 32.5 us (level)
  no operation moved by 1% of the time
where the time goes in v10:
time: 32.5 us; the launch traced here: 32 us
  waiting for transfers between devices  10 us (31%)
  starting transfers between devices  9.55 us (29%)
  Pallas kernels  8.09 us (25%)
  other arithmetic  2.49 us (8%)
  local copies, waits for them, and re-layouts  1.5 us (5%)
    pallas_call x2, Pallas kernels, kernel_call(): pl.pallas_call(functools.partial(kernel, sides, D), out_shape=out, in_spe...  8.09 us
    ppermute x1, waiting for transfers between devices, swapped(): lax.ppermute(pieces[s], axis, moves[s])  3.73 us
    ppermute x1, waiting for transfers between devices, gathered(): two = lax.ppermute(got[1], rows, far)  3.52 us
    ppermute x1, starting transfers between devices, exchange(): two = lax.ppermute(jnp.where(odd, last, first), axis, far)  2.52 us
    ppermute x2, starting transfers between devices, gathered(): lax.ppermute(sent[s - 1][r_], columns, [(i, (i + s) % nc) for i in range(...  2.09 us
    ppermute x1, starting transfers between devices, gathered(): two = lax.ppermute(got[1], rows, far)  1.92 us
    ppermute x1, starting transfers between devices, gathered(): one = lax.ppermute(got[0], rows, near)  1.64 us
    ppermute x1, waiting for transfers between devices, gathered(): one = lax.ppermute(got[0], rows, near)  1.37 us
  transfers between devices with their start and end apart: 7, of which 5 were waited for; matrix products, arithmetic and copies ran while one was open for 5% of the time, Pallas kernels for 16%

profile of v10, /device:TPU:18, one launch (start us, length us, event | category | flops | bytes accessed | tf_op | source)
XLA Modules:
  0.0 32.0 jit_solution(4061348474294090829)
XLA Ops:
  0.0 0.0 copy-start.2
  0.0 1.1 %slice_select_fusion = bf16[4,4,40,128]{3,2,1,0:T(8,128)(2,1)S(1)} fusion(bf16[4,4,64,128]{3,2,1,0:T(8,128)(2,1)} %param.5, pred[]{:T(512)S(6)} %eq.45), kind=kLoop, calls=%fused_computation.8 | loop fusion | flops 81920 | bytes 491521 | tf_op jit(solution)/shard_map/jit(_where)/select_n | solution.py:73
  1.2 1.6 %collective-permute-start = (bf16[272,128]{1,0:T(8,128)(2,1)S(1)}, bf16[272,128]{1,0:T(8,128)(2,1)S(1)}, u32[]{:S(2)}, u32[]{:S(2)}) collective-permute-start(bf16[272,128]{1,0:T(8,128)(2,1)S(1)} %get-tuple-element.31), channel_id=1, source_target_pairs={{0,1},{1,0},{2,3},{3,2},{4,5},{5,4},{6,7},{7,6},{8,9},{9,8},{10,11... | collective-permute-start | bytes 208904 | tf_op jit(solution)/shard_map/ppermute | solution.py:96
  2.8 0.5 %collective-permute-start.2 = (bf16[272,128]{1,0:T(8,128)(2,1)S(1)}, bf16[272,128]{1,0:T(8,128)(2,1)S(1)}, u32[]{:S(2)}, u32[]{:S(2)}) collective-permute-start(bf16[272,128]{1,0:T(8,128)(2,1)S(1)} %get-tuple-element.32), channel_id=1, source_target_pairs={{0,1},{1,0},{2,3},{3,2},{4,5},{5,4},{6,7},{7,6},{8,9},{9,8},{10,11... | collective-permute-start | bytes 208904 | tf_op jit(solution)/shard_map/ppermute | solution.py:96
  3.3 1.3 %slice.75.k0 = bf16[1,3,3,256,256]{4,3,2,1,0:T(8,128)(2,1)S(1)} slice(bf16[3,3,3,256,256]{4,3,2,1,0:T(8,128)(2,1)} %k1h.1), slice={[0:1], [0:3], [0:3], [0:256], [0:256]} | slice | bytes 2359296 | tf_op jit(solution)/shard_map/slice | solution.py:389
  4.7 0.0 copy-done.2
  4.7 0.0 copy-start
  4.7 0.0 copy-start.1
  4.9 1.4 %collective-permute-done = bf16[272,128]{1,0:T(8,128)(2,1)S(1)} collective-permute-done((bf16[272,128]{1,0:T(8,128)(2,1)S(1)}, bf16[272,128]{1,0:T(8,128)(2,1)S(1)}, u32[]{:S(2)}, u32[]{:S(2)}) %collective-permute-start) | collective-permute-done | bytes 69664 | tf_op jit(solution)/shard_map/ppermute | solution.py:96
  6.3 1.6 %collective-permute-start.1 = (bf16[272,256]{1,0:T(8,128)(2,1)S(1)}, bf16[272,256]{1,0:T(8,128)(2,1)S(1)}, u32[]{:S(2)}, u32[]{:S(2)}) collective-permute-start(bf16[272,256]{1,0:T(8,128)(2,1)S(1)} %maximum_select_fusion.3), channel_id=1, source_target_pairs={{0,2},{4,6},{2,0},{6,4},{1,3},{5,7},{3,1},{7,5},{8,10},{12,14},{10... | collective-permute-start | bytes 417800 | tf_op jit(solution)/shard_map/ppermute | solution.py:99
  7.9 0.0 collective-permute-done.2
  8.0 1.9 %collective-permute-start.3 = (bf16[272,256]{1,0:T(8,128)(2,1)S(1)}, bf16[272,256]{1,0:T(8,128)(2,1)S(1)}, u32[]{:S(2)}, u32[]{:S(2)}) collective-permute-start(bf16[272,256]{1,0:T(8,128)(2,1)S(1)} %maximum_select_fusion.4), channel_id=1, source_target_pairs={{2,4},{4,2},{0,0},{6,6},{3,5},{5,3},{1,1},{7,7},{10,12},{12,10},{8... | collective-permute-start | bytes 417800 | tf_op jit(solution)/shard_map/ppermute | solution.py:100
  10.0 1.4 %collective-permute-done.1 = bf16[272,256]{1,0:T(8,128)(2,1)S(1)} collective-permute-done((bf16[272,256]{1,0:T(8,128)(2,1)S(1)}, bf16[272,256]{1,0:T(8,128)(2,1)S(1)}, u32[]{:S(2)}, u32[]{:S(2)}) %collective-permute-start.1) | collective-permute-done | bytes 139296 | tf_op jit(solution)/shard_map/ppermute | solution.py:99
  11.4 3.5 %collective-permute-done.3 = bf16[272,256]{1,0:T(8,128)(2,1)S(1)} collective-permute-done((bf16[272,256]{1,0:T(8,128)(2,1)S(1)}, bf16[272,256]{1,0:T(8,128)(2,1)S(1)}, u32[]{:S(2)}, u32[]{:S(2)}) %collective-permute-start.3) | collective-permute-done | bytes 139296 | tf_op jit(solution)/shard_map/ppermute | solution.py:100
  15.0 0.1 pad_maximum_fusion.xc
  15.1 0.1 broadcast_select_fusion.1
  15.2 0.1 collective-permute-start.4
  15.3 2.5 %collective-permute-start.5 = (bf16[544,256]{1,0:T(8,128)(2,1)S(1)}, bf16[544,256]{1,0:T(8,128)(2,1)S(1)}, u32[]{:S(2)}, u32[]{:S(2)}) collective-permute-start(bf16[544,256]{1,0:T(8,128)(2,1)S(1)} %get-tuple-element.20), channel_id=1, source_target_pairs={{8,16},{16,8},{0,0},{24,24},{9,17},{17,9},{1,1},{25,25},{10,18},{1... | collective-permute-start | bytes 835592 | tf_op jit(solution)/shard_map/ppermute | solution.py:31
  17.8 0.0 collective-permute-done.4.xn
  17.8 0.0 copy-done
  17.8 0.0 copy-done.1
  17.8 5.2 %near.1 = (bf16[2,4,32,256]{3,2,1,0:T(8,128)(2,1)S(1)}, bf16[2,6,32,768]{3,2,1,0:T(8,128)(2,1)S(1)}, f32[256,256]{1,0:T(8,128)S(1)}, bf16[3,3,3,256,256]{4,3,2,1...) custom-call(bf16[4,272,256]{2,1,0:T(8,128)(2,1)S(1)} %pad_maximum_fusion.xc, ...), custom_call_target="tpu_custom_call" | custom-call | flops 3623878656 | bytes 1048576 | tf_op jit(solution)/shard_map/near/pallas_call | solution.py:372
  23.1 0.1 collective-permute-done.5.xf
  23.2 2.8 %far.1 = bf16[2,4,32,256]{3,2,1,0:T(8,128)(2,1)S(1)} custom-call(bf16[4,272,256]{2,1,0:T(8,128)(2,1)S(1)} %pad_maximum_fusion.xc, bf16[544,256]{1,0:T(8,128)(2,1)S(1)} %collective-permute-done.5.xf, bf16[2,6,32,768]{3,2,1,0:T(8,128)(2,1)S(1)} %get-tuple-element.15.keep, f32[256,256]{1,0:T(8,128)S(1)} %get-tuple-element.16.part_sum, ...), custom_call_target="tpu_custom_call" | custom-call | flops 2264924160 | bytes 1048576 | tf_op jit(solution)/shard_map/far/pallas_call | solution.py:372
  26.1 0.1 constant_dynamic-slice_fusion.1
  26.1 1.3 %collective-permute-start.6 = (bf16[4,4,32,128]{3,2,1,0:T(8,128)(2,1)S(1)}, bf16[4,4,32,128]{3,2,1,0:T(8,128)(2,1)S(1)}, u32[]{:S(2)}, u32[]{:S(2)}) collective-permute-start(bf16[4,4,32,128]{3,2,1,0:T(8,128)(2,1)S(1)} %get-tuple-element.28), channel_id=1, source_target_pairs={{0,1},{1,0},{2,3},{3,2},{4,5},{5,4},{6,7},{7,6},{8,9},{9,8},{10,11... | collective-permute-start | bytes 393224 | tf_op jit(solution)/shard_map/ppermute | solution.py:57
  27.4 3.7 %collective-permute-done.6 = bf16[4,4,32,128]{3,2,1,0:T(8,128)(2,1)S(1)} collective-permute-done((bf16[4,4,32,128]{3,2,1,0:T(8,128)(2,1)S(1)}, bf16[4,4,32,128]{3,2,1,0:T(8,128)(2,1)S(1)}, u32[]{:S(2)}, u32[]{:S(2)}) %collective-permute-start.6) | collective-permute-done | bytes 131104 | tf_op jit(solution)/shard_map/ppermute | solution.py:57
  31.2 0.8 %maximum_select_fusion.2 = bf16[4,4,64,128]{3,2,1,0:T(8,128)(2,1)} fusion(bf16[4,4,32,128]{3,2,1,0:T(8,128)(2,1)S(1)} %collective-permute-done.6, bf16[4,4,32,128]{3,2,1,0:T(8,128)(2,1)S(1)} %get-tuple-element.27, pred[]{:T(512)S(6)} %eq.40), kind=kLoop, calls=%fused_computation.7 | loop fusion | flops 1179648 | bytes 524289 | tf_op jit(solution)/shard_map/jit(_where)/select_n | solution.py:48
  (20 shorter events, 0.5 us)
Async XLA Ops:
  0.0 4.7 %copy-start.2 = (bf16[4,4,64,128]{3,2,1,0:T(8,128)(2,1)S(1)}, bf16[4,4,64,128]{3,2,1,0:T(8,128)(2,1)}, u32[]{:S(2)}) copy-start(bf16[4,4,64,128]{3,2,1,0:T(8,128)(2,1)} %param.5) | copy-start | bytes 786436
  1.2 5.0 %collective-permute-start = (bf16[272,128]{1,0:T(8,128)(2,1)S(1)}, bf16[272,128]{1,0:T(8,128)(2,1)S(1)}, u32[]{:S(2)}, u32[]{:S(2)}) collective-permute-start(bf16[272,128]{1,0:T(8,128)(2,1)S(1)} %get-tuple-element.31), channel_id=1, source_target_pairs={{0,1},{1,0},{2,3},{3,2},{4,5},{5,4},{6,7},{7,6},{8,9},{9,8},{10,11... | collective-permute-start | bytes 208904 | tf_op jit(solution)/shard_map/ppermute | solution.py:96
  2.8 5.1 %collective-permute-start.2 = (bf16[272,128]{1,0:T(8,128)(2,1)S(1)}, bf16[272,128]{1,0:T(8,128)(2,1)S(1)}, u32[]{:S(2)}, u32[]{:S(2)}) collective-permute-start(bf16[272,128]{1,0:T(8,128)(2,1)S(1)} %get-tuple-element.32), channel_id=1, source_target_pairs={{0,1},{1,0},{2,3},{3,2},{4,5},{5,4},{6,7},{7,6},{8,9},{9,8},{10,11... | collective-permute-start | bytes 208904 | tf_op jit(solution)/shard_map/ppermute | solution.py:96
  4.7 13.2 %copy-start = (f32[256]{0:T(256)S(1)}, f32[256]{0:T(256)}, u32[]{:S(2)}) copy-start(f32[256]{0:T(256)} %param.7) | copy-start | bytes 3076
  4.7 13.1 %copy-start.1 = (f32[256]{0:T(256)S(1)}, f32[256]{0:T(256)}, u32[]{:S(2)}) copy-start(f32[256]{0:T(256)} %param.9) | copy-start | bytes 3076
  6.3 5.1 %collective-permute-start.1 = (bf16[272,256]{1,0:T(8,128)(2,1)S(1)}, bf16[272,256]{1,0:T(8,128)(2,1)S(1)}, u32[]{:S(2)}, u32[]{:S(2)}) collective-permute-start(bf16[272,256]{1,0:T(8,128)(2,1)S(1)} %maximum_select_fusion.3), channel_id=1, source_target_pairs={{0,2},{4,6},{2,0},{6,4},{1,3},{5,7},{3,1},{7,5},{8,10},{12,14},{10... | collective-permute-start | bytes 417800 | tf_op jit(solution)/shard_map/ppermute | solution.py:99
  8.0 6.9 %collective-permute-start.3 = (bf16[272,256]{1,0:T(8,128)(2,1)S(1)}, bf16[272,256]{1,0:T(8,128)(2,1)S(1)}, u32[]{:S(2)}, u32[]{:S(2)}) collective-permute-start(bf16[272,256]{1,0:T(8,128)(2,1)S(1)} %maximum_select_fusion.4), channel_id=1, source_target_pairs={{2,4},{4,2},{0,0},{6,6},{3,5},{5,3},{1,1},{7,7},{10,12},{12,10},{8... | collective-permute-start | bytes 417800 | tf_op jit(solution)/shard_map/ppermute | solution.py:100
  15.2 2.6 %collective-permute-start.4 = (bf16[544,256]{1,0:T(8,128)(2,1)S(1)}, bf16[544,256]{1,0:T(8,128)(2,1)S(1)}, u32[]{:S(2)}, u32[]{:S(2)}) collective-permute-start(bf16[544,256]{1,0:T(8,128)(2,1)S(1)} %get-tuple-element.19), channel_id=1, source_target_pairs={{0,8},{16,24},{8,0},{24,16},{1,9},{17,25},{9,1},{25,17},{2,10},{18... | collective-permute-start | bytes 835592 | tf_op jit(solution)/shard_map/ppermute | solution.py:30
  15.3 7.9 %collective-permute-start.5 = (bf16[544,256]{1,0:T(8,128)(2,1)S(1)}, bf16[544,256]{1,0:T(8,128)(2,1)S(1)}, u32[]{:S(2)}, u32[]{:S(2)}) collective-permute-start(bf16[544,256]{1,0:T(8,128)(2,1)S(1)} %get-tuple-element.20), channel_id=1, source_target_pairs={{8,16},{16,8},{0,0},{24,24},{9,17},{17,9},{1,1},{25,25},{10,18},{1... | collective-permute-start | bytes 835592 | tf_op jit(solution)/shard_map/ppermute | solution.py:31
  26.1 5.0 %collective-permute-start.6 = (bf16[4,4,32,128]{3,2,1,0:T(8,128)(2,1)S(1)}, bf16[4,4,32,128]{3,2,1,0:T(8,128)(2,1)S(1)}, u32[]{:S(2)}, u32[]{:S(2)}) collective-permute-start(bf16[4,4,32,128]{3,2,1,0:T(8,128)(2,1)S(1)} %get-tuple-element.28), channel_id=1, source_target_pairs={{0,1},{1,0},{2,3},{3,2},{4,5},{5,4},{6,7},{7,6},{8,9},{9,8},{10,11... | collective-permute-start | bytes 393224 | tf_op jit(solution)/shard_map/ppermute | solution.py:57

commit v11 on v10

--- a/solution.py
+++ b/solution.py
@@ -70,7 +70,7 @@
     def window(s, x):
         block = (c + s) % nc
         if nc == 2:
-            return jnp.where(block == 0, x[:, :, :own + 8], x[:, :, own - 8:])
+            return lax.dynamic_slice_in_dim(x, block * (own - 8), own + 8, 2)
         padded = jnp.pad(x, ((0, 0), (0, 0), (2, 2), (0, 0)))
         return lax.dynamic_slice_in_dim(padded, block * own, own + 4, 2)
 

time: 32.5 us -> 32.4 us (level)
  other arithmetic: 2.49 us -> 1.39 us
  local copies, waits for them, and re-layouts: 1.5 us -> 2.49 us
    select_n x2 -> x0, other arithmetic: 1.11 us -> none  [window(): return jnp.where(block == 0, x[:, :, :own + 8], x[:, :, own - 8:])]
    unnamed x6, local copies, waits for them, and re-layouts: 0.02 us -> 0.96 us
where the time goes in v11:
time: 32.4 us; the launch traced here: 31.9 us
  waiting for transfers between devices  10 us (31%)
  starting transfers between devices  9.55 us (29%)
  Pallas kernels  8.09 us (25%)
  local copies, waits for them, and re-layouts  2.49 us (8%)
  other arithmetic  1.39 us (4%)
    pallas_call x2, Pallas kernels, kernel_call(): pl.pallas_call(functools.partial(kernel, sides, D), out_shape=out, in_spe...  8.09 us
    ppermute x1, waiting for transfers between devices, swapped(): lax.ppermute(pieces[s], axis, moves[s])  3.73 us
    ppermute x1, waiting for transfers between devices, gathered(): two = lax.ppermute(got[1], rows, far)  3.52 us
    ppermute x1, starting transfers between devices, exchange(): two = lax.ppermute(jnp.where(odd, last, first), axis, far)  2.52 us
    ppermute x2, starting transfers between devices, gathered(): lax.ppermute(sent[s - 1][r_], columns, [(i, (i + s) % nc) for i in range(...  2.09 us
    ppermute x1, starting transfers between devices, gathered(): two = lax.ppermute(got[1], rows, far)  1.92 us
    ppermute x1, starting transfers between devices, gathered(): one = lax.ppermute(got[0], rows, near)  1.64 us
    ppermute x1, waiting for transfers between devices, gathered(): one = lax.ppermute(got[0], rows, near)  1.37 us
  transfers between devices with their start and end apart: 7, of which 5 were waited for; matrix products, arithmetic and copies ran while one was open for 5% of the time, Pallas kernels for 16%

profile of v11, /device:TPU:18, one launch (start us, length us, event | category | flops | bytes accessed | tf_op | source)
XLA Modules:
  0.0 31.9 jit_solution(3698122508153862395)
XLA Ops:
  0.0 0.0 copy-start
  0.0 0.9 %copy-done = bf16[4,4,64,128]{3,2,1,0:T(8,128)(2,1)S(1)} copy-done((bf16[4,4,64,128]{3,2,1,0:T(8,128)(2,1)S(1)}, bf16[4,4,64,128]{3,2,1,0:T(8,128)(2,1)}, u32[]{:S(2)}) %copy-start) | copy-done | bytes 262168
  1.1 1.6 %collective-permute-start = (bf16[272,128]{1,0:T(8,128)(2,1)S(1)}, bf16[272,128]{1,0:T(8,128)(2,1)S(1)}, u32[]{:S(2)}, u32[]{:S(2)}) collective-permute-start(bf16[272,128]{1,0:T(8,128)(2,1)S(1)} %get-tuple-element.31), channel_id=1, source_target_pairs={{0,1},{1,0},{2,3},{3,2},{4,5},{5,4},{6,7},{7,6},{8,9},{9,8},{10,11... | collective-permute-start | bytes 208904 | tf_op jit(solution)/shard_map/ppermute | solution.py:96
  2.7 0.5 %collective-permute-start.2 = (bf16[272,128]{1,0:T(8,128)(2,1)S(1)}, bf16[272,128]{1,0:T(8,128)(2,1)S(1)}, u32[]{:S(2)}, u32[]{:S(2)}) collective-permute-start(bf16[272,128]{1,0:T(8,128)(2,1)S(1)} %get-tuple-element.32), channel_id=1, source_target_pairs={{0,1},{1,0},{2,3},{3,2},{4,5},{5,4},{6,7},{7,6},{8,9},{9,8},{10,11... | collective-permute-start | bytes 208904 | tf_op jit(solution)/shard_map/ppermute | solution.py:96
  3.2 1.3 %slice.63.k0 = bf16[1,3,3,256,256]{4,3,2,1,0:T(8,128)(2,1)S(1)} slice(bf16[3,3,3,256,256]{4,3,2,1,0:T(8,128)(2,1)} %k1h.1), slice={[0:1], [0:3], [0:3], [0:256], [0:256]} | slice | bytes 2359296 | tf_op jit(solution)/shard_map/slice | solution.py:389
  4.6 0.0 copy-start.1
  4.6 0.0 copy-start.2
  4.8 1.4 %collective-permute-done = bf16[272,128]{1,0:T(8,128)(2,1)S(1)} collective-permute-done((bf16[272,128]{1,0:T(8,128)(2,1)S(1)}, bf16[272,128]{1,0:T(8,128)(2,1)S(1)}, u32[]{:S(2)}, u32[]{:S(2)}) %collective-permute-start) | collective-permute-done | bytes 69664 | tf_op jit(solution)/shard_map/ppermute | solution.py:96
  6.2 1.6 %collective-permute-start.1 = (bf16[272,256]{1,0:T(8,128)(2,1)S(1)}, bf16[272,256]{1,0:T(8,128)(2,1)S(1)}, u32[]{:S(2)}, u32[]{:S(2)}) collective-permute-start(bf16[272,256]{1,0:T(8,128)(2,1)S(1)} %maximum_select_fusion.3), channel_id=1, source_target_pairs={{0,2},{4,6},{2,0},{6,4},{1,3},{5,7},{3,1},{7,5},{8,10},{12,14},{10... | collective-permute-start | bytes 417800 | tf_op jit(solution)/shard_map/ppermute | solution.py:99
  7.8 0.0 collective-permute-done.2
  7.9 1.9 %collective-permute-start.3 = (bf16[272,256]{1,0:T(8,128)(2,1)S(1)}, bf16[272,256]{1,0:T(8,128)(2,1)S(1)}, u32[]{:S(2)}, u32[]{:S(2)}) collective-permute-start(bf16[272,256]{1,0:T(8,128)(2,1)S(1)} %maximum_select_fusion.4), channel_id=1, source_target_pairs={{2,4},{4,2},{0,0},{6,6},{3,5},{5,3},{1,1},{7,7},{10,12},{12,10},{8... | collective-permute-start | bytes 417800 | tf_op jit(solution)/shard_map/ppermute | solution.py:100
  9.9 1.4 %collective-permute-done.1 = bf16[272,256]{1,0:T(8,128)(2,1)S(1)} collective-permute-done((bf16[272,256]{1,0:T(8,128)(2,1)S(1)}, bf16[272,256]{1,0:T(8,128)(2,1)S(1)}, u32[]{:S(2)}, u32[]{:S(2)}) %collective-permute-start.1) | collective-permute-done | bytes 139296 | tf_op jit(solution)/shard_map/ppermute | solution.py:99
  11.3 3.5 %collective-permute-done.3 = bf16[272,256]{1,0:T(8,128)(2,1)S(1)} collective-permute-done((bf16[272,256]{1,0:T(8,128)(2,1)S(1)}, bf16[272,256]{1,0:T(8,128)(2,1)S(1)}, u32[]{:S(2)}, u32[]{:S(2)}) %collective-permute-start.3) | collective-permute-done | bytes 139296 | tf_op jit(solution)/shard_map/ppermute | solution.py:100
  14.8 0.1 pad_maximum_fusion.xc
  15.0 0.1 broadcast_select_fusion.1
  15.1 0.1 collective-permute-start.4
  15.2 2.5 %collective-permute-start.5 = (bf16[544,256]{1,0:T(8,128)(2,1)S(1)}, bf16[544,256]{1,0:T(8,128)(2,1)S(1)}, u32[]{:S(2)}, u32[]{:S(2)}) collective-permute-start(bf16[544,256]{1,0:T(8,128)(2,1)S(1)} %get-tuple-element.20), channel_id=1, source_target_pairs={{8,16},{16,8},{0,0},{24,24},{9,17},{17,9},{1,1},{25,25},{10,18},{1... | collective-permute-start | bytes 835592 | tf_op jit(solution)/shard_map/ppermute | solution.py:31
  17.7 0.0 collective-permute-done.4.xn
  17.7 0.0 copy-done.1
  17.7 0.0 copy-done.2
  17.7 5.2 %near.1 = (bf16[2,4,32,256]{3,2,1,0:T(8,128)(2,1)S(1)}, bf16[2,6,32,768]{3,2,1,0:T(8,128)(2,1)S(1)}, f32[256,256]{1,0:T(8,128)S(1)}, bf16[3,3,3,256,256]{4,3,2,1...) custom-call(bf16[4,272,256]{2,1,0:T(8,128)(2,1)S(1)} %pad_maximum_fusion.xc, ...), custom_call_target="tpu_custom_call" | custom-call | flops 3623878656 | bytes 1048576 | tf_op jit(solution)/shard_map/near/pallas_call | solution.py:372
  23.0 0.1 collective-permute-done.5.xf
  23.0 2.9 %far.1 = bf16[2,4,32,256]{3,2,1,0:T(8,128)(2,1)S(1)} custom-call(bf16[4,272,256]{2,1,0:T(8,128)(2,1)S(1)} %pad_maximum_fusion.xc, bf16[544,256]{1,0:T(8,128)(2,1)S(1)} %collective-permute-done.5.xf, bf16[2,6,32,768]{3,2,1,0:T(8,128)(2,1)S(1)} %get-tuple-element.15.keep, f32[256,256]{1,0:T(8,128)S(1)} %get-tuple-element.16.part_sum, ...), custom_call_target="tpu_custom_call" | custom-call | flops 2264924160 | bytes 1048576 | tf_op jit(solution)/shard_map/far/pallas_call | solution.py:372
  25.9 0.1 constant_dynamic-slice_fusion.1
  26.0 1.3 %collective-permute-start.6 = (bf16[4,4,32,128]{3,2,1,0:T(8,128)(2,1)S(1)}, bf16[4,4,32,128]{3,2,1,0:T(8,128)(2,1)S(1)}, u32[]{:S(2)}, u32[]{:S(2)}) collective-permute-start(bf16[4,4,32,128]{3,2,1,0:T(8,128)(2,1)S(1)} %get-tuple-element.28), channel_id=1, source_target_pairs={{0,1},{1,0},{2,3},{3,2},{4,5},{5,4},{6,7},{7,6},{8,9},{9,8},{10,11... | collective-permute-start | bytes 393224 | tf_op jit(solution)/shard_map/ppermute | solution.py:57
  27.3 3.7 %collective-permute-done.6 = bf16[4,4,32,128]{3,2,1,0:T(8,128)(2,1)S(1)} collective-permute-done((bf16[4,4,32,128]{3,2,1,0:T(8,128)(2,1)S(1)}, bf16[4,4,32,128]{3,2,1,0:T(8,128)(2,1)S(1)}, u32[]{:S(2)}, u32[]{:S(2)}) %collective-permute-start.6) | collective-permute-done | bytes 131104 | tf_op jit(solution)/shard_map/ppermute | solution.py:57
  31.0 0.8 %maximum_select_fusion.2 = bf16[4,4,64,128]{3,2,1,0:T(8,128)(2,1)} fusion(bf16[4,4,32,128]{3,2,1,0:T(8,128)(2,1)S(1)} %collective-permute-done.6, bf16[4,4,32,128]{3,2,1,0:T(8,128)(2,1)S(1)} %get-tuple-element.27, pred[]{:T(512)S(6)} %eq.38), kind=kLoop, calls=%fused_computation.7 | loop fusion | flops 1179648 | bytes 524289 | tf_op jit(solution)/shard_map/jit(_where)/select_n | solution.py:48
  (21 shorter events, 0.5 us)
Async XLA Ops:
  0.0 1.0 %copy-start = (bf16[4,4,64,128]{3,2,1,0:T(8,128)(2,1)S(1)}, bf16[4,4,64,128]{3,2,1,0:T(8,128)(2,1)}, u32[]{:S(2)}) copy-start(bf16[4,4,64,128]{3,2,1,0:T(8,128)(2,1)} %param.5) | copy-start | bytes 786436
  1.1 5.0 %collective-permute-start = (bf16[272,128]{1,0:T(8,128)(2,1)S(1)}, bf16[272,128]{1,0:T(8,128)(2,1)S(1)}, u32[]{:S(2)}, u32[]{:S(2)}) collective-permute-start(bf16[272,128]{1,0:T(8,128)(2,1)S(1)} %get-tuple-element.31), channel_id=1, source_target_pairs={{0,1},{1,0},{2,3},{3,2},{4,5},{5,4},{6,7},{7,6},{8,9},{9,8},{10,11... | collective-permute-start | bytes 208904 | tf_op jit(solution)/shard_map/ppermute | solution.py:96
  2.7 5.1 %collective-permute-start.2 = (bf16[272,128]{1,0:T(8,128)(2,1)S(1)}, bf16[272,128]{1,0:T(8,128)(2,1)S(1)}, u32[]{:S(2)}, u32[]{:S(2)}) collective-permute-start(bf16[272,128]{1,0:T(8,128)(2,1)S(1)} %get-tuple-element.32), channel_id=1, source_target_pairs={{0,1},{1,0},{2,3},{3,2},{4,5},{5,4},{6,7},{7,6},{8,9},{9,8},{10,11... | collective-permute-start | bytes 208904 | tf_op jit(solution)/shard_map/ppermute | solution.py:96
  4.6 13.2 %copy-start.1 = (f32[256]{0:T(256)S(1)}, f32[256]{0:T(256)}, u32[]{:S(2)}) copy-start(f32[256]{0:T(256)} %param.7) | copy-start | bytes 3076
  4.6 13.2 %copy-start.2 = (f32[256]{0:T(256)S(1)}, f32[256]{0:T(256)}, u32[]{:S(2)}) copy-start(f32[256]{0:T(256)} %param.9) | copy-start | bytes 3076
  6.2 5.1 %collective-permute-start.1 = (bf16[272,256]{1,0:T(8,128)(2,1)S(1)}, bf16[272,256]{1,0:T(8,128)(2,1)S(1)}, u32[]{:S(2)}, u32[]{:S(2)}) collective-permute-start(bf16[272,256]{1,0:T(8,128)(2,1)S(1)} %maximum_select_fusion.3), channel_id=1, source_target_pairs={{0,2},{4,6},{2,0},{6,4},{1,3},{5,7},{3,1},{7,5},{8,10},{12,14},{10... | collective-permute-start | bytes 417800 | tf_op jit(solution)/shard_map/ppermute | solution.py:99
  7.9 6.9 %collective-permute-start.3 = (bf16[272,256]{1,0:T(8,128)(2,1)S(1)}, bf16[272,256]{1,0:T(8,128)(2,1)S(1)}, u32[]{:S(2)}, u32[]{:S(2)}) collective-permute-start(bf16[272,256]{1,0:T(8,128)(2,1)S(1)} %maximum_select_fusion.4), channel_id=1, source_target_pairs={{2,4},{4,2},{0,0},{6,6},{3,5},{5,3},{1,1},{7,7},{10,12},{12,10},{8... | collective-permute-start | bytes 417800 | tf_op jit(solution)/shard_map/ppermute | solution.py:100
  15.1 2.6 %collective-permute-start.4 = (bf16[544,256]{1,0:T(8,128)(2,1)S(1)}, bf16[544,256]{1,0:T(8,128)(2,1)S(1)}, u32[]{:S(2)}, u32[]{:S(2)}) collective-permute-start(bf16[544,256]{1,0:T(8,128)(2,1)S(1)} %get-tuple-element.19), channel_id=1, source_target_pairs={{0,8},{16,24},{8,0},{24,16},{1,9},{17,25},{9,1},{25,17},{2,10},{18... | collective-permute-start | bytes 835592 | tf_op jit(solution)/shard_map/ppermute | solution.py:30
  15.2 7.9 %collective-permute-start.5 = (bf16[544,256]{1,0:T(8,128)(2,1)S(1)}, bf16[544,256]{1,0:T(8,128)(2,1)S(1)}, u32[]{:S(2)}, u32[]{:S(2)}) collective-permute-start(bf16[544,256]{1,0:T(8,128)(2,1)S(1)} %get-tuple-element.20), channel_id=1, source_target_pairs={{8,16},{16,8},{0,0},{24,24},{9,17},{17,9},{1,1},{25,25},{10,18},{1... | collective-permute-start | bytes 835592 | tf_op jit(solution)/shard_map/ppermute | solution.py:31
  26.0 5.0 %collective-permute-start.6 = (bf16[4,4,32,128]{3,2,1,0:T(8,128)(2,1)S(1)}, bf16[4,4,32,128]{3,2,1,0:T(8,128)(2,1)S(1)}, u32[]{:S(2)}, u32[]{:S(2)}) collective-permute-start(bf16[4,4,32,128]{3,2,1,0:T(8,128)(2,1)S(1)} %get-tuple-element.28), channel_id=1, source_target_pairs={{0,1},{1,0},{2,3},{3,2},{4,5},{5,4},{6,7},{7,6},{8,9},{9,8},{10,11... | collective-permute-start | bytes 393224 | tf_op jit(solution)/shard_map/ppermute | solution.py:57

commit v12 on v11

--- a/solution.py
+++ b/solution.py
@@ -397,7 +397,12 @@
         return [lax.dynamic_slice_in_dim(y, (f + s) % n * shard, shard, 3) for s in range(n)]
     out_far, = kernel_call(far_kernel, "far", 4, sides, shape, False, (tall, far, keep, part_sum, k1, b1, k2, b2))
     out = jnp.where(odd == 1, jnp.concatenate([out_near, out_far], 0), jnp.concatenate([out_far, out_near], 0))
-    return by_origin(swapped(pieces(out), "filt"), "filt", 2)
+    parts = swapped(pieces(out), "filt")
+    f, n = lax.axis_index("filt"), lax.axis_size("filt")
+    result = jnp.zeros(volume.shape, volume.dtype)
+    for s, part in enumerate(parts):
+        result = lax.dynamic_update_slice_in_dim(result, part, (f - s) % n * own, 2)
+    return result
 
 
 def solution(mesh):

time: 32.4 us -> 32.4 us (level)
  other arithmetic: 1.39 us -> 0.57 us
  local copies, waits for them, and re-layouts: 2.49 us -> 3.23 us
    select_n x5 -> x4, other arithmetic: 0.98 us -> 0.17 us  [by_origin(): jnp.where(index == 0, jnp.concatenate(parts, dim), jnp.concatenate(parts[...]
    dynamic_update_slice x0 -> x1, local copies, waits for them, and re-layouts: none -> 0.68 us  [body(): result = lax.dynamic_update_slice_in_dim(result, part, (f - s) % n * own, 2)]
    unnamed x6 -> x8, local copies, waits for them, and re-layouts: 0.96 us -> 0.97 us
where the time goes in v12:
time: 32.4 us; the launch traced here: 31.8 us
  waiting for transfers between devices  10 us (31%)
  starting transfers between devices  9.54 us (29%)
  Pallas kernels  8.09 us (25%)
  local copies, waits for them, and re-layouts  3.23 us (10%)
  other arithmetic  0.57 us (2%)
  between operations  0.33 us (1%)
    pallas_call x2, Pallas kernels, kernel_call(): pl.pallas_call(functools.partial(kernel, sides, D), out_shape=out, in_spe...  8.09 us
    ppermute x1, waiting for transfers between devices, swapped(): lax.ppermute(pieces[s], axis, moves[s])  3.73 us
    ppermute x1, waiting for transfers between devices, gathered(): two = lax.ppermute(got[1], rows, far)  3.52 us
    ppermute x1, starting transfers between devices, exchange(): two = lax.ppermute(jnp.where(odd, last, first), axis, far)  2.51 us
    ppermute x2, starting transfers between devices, gathered(): lax.ppermute(sent[s - 1][r_], columns, [(i, (i + s) % nc) for i in range(...  2.09 us
    ppermute x1, starting transfers between devices, gathered(): two = lax.ppermute(got[1], rows, far)  1.92 us
    ppermute x1, starting transfers between devices, gathered(): one = lax.ppermute(got[0], rows, near)  1.64 us
    ppermute x1, waiting for transfers between devices, gathered(): one = lax.ppermute(got[0], rows, near)  1.37 us
  transfers between devices with their start and end apart: 7, of which 5 were waited for; matrix products, arithmetic and copies ran while one was open for 5% of the time, Pallas kernels for 16%

profile of v12, /device:TPU:18, one launch (start us, length us, event | category | flops | bytes accessed | tf_op | source)
XLA Modules:
  0.0 31.8 jit_solution(756016431233784683)
XLA Ops:
  0.0 0.0 copy-start
  0.0 0.9 %copy-done = bf16[4,4,64,128]{3,2,1,0:T(8,128)(2,1)S(1)} copy-done((bf16[4,4,64,128]{3,2,1,0:T(8,128)(2,1)S(1)}, bf16[4,4,64,128]{3,2,1,0:T(8,128)(2,1)}, u32[]{:S(2)}) %copy-start) | copy-done | bytes 262168
  1.1 1.6 %collective-permute-start = (bf16[272,128]{1,0:T(8,128)(2,1)S(1)}, bf16[272,128]{1,0:T(8,128)(2,1)S(1)}, u32[]{:S(2)}, u32[]{:S(2)}) collective-permute-start(bf16[272,128]{1,0:T(8,128)(2,1)S(1)} %get-tuple-element.31), channel_id=1, source_target_pairs={{0,1},{1,0},{2,3},{3,2},{4,5},{5,4},{6,7},{7,6},{8,9},{9,8},{10,11... | collective-permute-start | bytes 208904 | tf_op jit(solution)/shard_map/ppermute | solution.py:96
  2.7 0.5 %collective-permute-start.2 = (bf16[272,128]{1,0:T(8,128)(2,1)S(1)}, bf16[272,128]{1,0:T(8,128)(2,1)S(1)}, u32[]{:S(2)}, u32[]{:S(2)}) collective-permute-start(bf16[272,128]{1,0:T(8,128)(2,1)S(1)} %get-tuple-element.32), channel_id=1, source_target_pairs={{0,1},{1,0},{2,3},{3,2},{4,5},{5,4},{6,7},{7,6},{8,9},{9,8},{10,11... | collective-permute-start | bytes 208904 | tf_op jit(solution)/shard_map/ppermute | solution.py:96
  3.2 1.3 %slice.63.k0 = bf16[1,3,3,256,256]{4,3,2,1,0:T(8,128)(2,1)S(1)} slice(bf16[3,3,3,256,256]{4,3,2,1,0:T(8,128)(2,1)} %k1h.1), slice={[0:1], [0:3], [0:3], [0:256], [0:256]} | slice | bytes 2359296 | tf_op jit(solution)/shard_map/slice | solution.py:389
  4.6 0.0 copy-start.1
  4.6 0.0 copy-start.2
  4.8 1.3 %collective-permute-done = bf16[272,128]{1,0:T(8,128)(2,1)S(1)} collective-permute-done((bf16[272,128]{1,0:T(8,128)(2,1)S(1)}, bf16[272,128]{1,0:T(8,128)(2,1)S(1)}, u32[]{:S(2)}, u32[]{:S(2)}) %collective-permute-start) | collective-permute-done | bytes 69664 | tf_op jit(solution)/shard_map/ppermute | solution.py:96
  6.2 1.6 %collective-permute-start.1 = (bf16[272,256]{1,0:T(8,128)(2,1)S(1)}, bf16[272,256]{1,0:T(8,128)(2,1)S(1)}, u32[]{:S(2)}, u32[]{:S(2)}) collective-permute-start(bf16[272,256]{1,0:T(8,128)(2,1)S(1)} %maximum_select_fusion.2), channel_id=1, source_target_pairs={{0,2},{4,6},{2,0},{6,4},{1,3},{5,7},{3,1},{7,5},{8,10},{12,14},{10... | collective-permute-start | bytes 417800 | tf_op jit(solution)/shard_map/ppermute | solution.py:99
  7.8 0.0 collective-permute-done.2
  7.9 1.9 %collective-permute-start.3 = (bf16[272,256]{1,0:T(8,128)(2,1)S(1)}, bf16[272,256]{1,0:T(8,128)(2,1)S(1)}, u32[]{:S(2)}, u32[]{:S(2)}) collective-permute-start(bf16[272,256]{1,0:T(8,128)(2,1)S(1)} %maximum_select_fusion.3), channel_id=1, source_target_pairs={{2,4},{4,2},{0,0},{6,6},{3,5},{5,3},{1,1},{7,7},{10,12},{12,10},{8... | collective-permute-start | bytes 417800 | tf_op jit(solution)/shard_map/ppermute | solution.py:100
  9.9 1.4 %collective-permute-done.1 = bf16[272,256]{1,0:T(8,128)(2,1)S(1)} collective-permute-done((bf16[272,256]{1,0:T(8,128)(2,1)S(1)}, bf16[272,256]{1,0:T(8,128)(2,1)S(1)}, u32[]{:S(2)}, u32[]{:S(2)}) %collective-permute-start.1) | collective-permute-done | bytes 139296 | tf_op jit(solution)/shard_map/ppermute | solution.py:99
  11.3 3.5 %collective-permute-done.3 = bf16[272,256]{1,0:T(8,128)(2,1)S(1)} collective-permute-done((bf16[272,256]{1,0:T(8,128)(2,1)S(1)}, bf16[272,256]{1,0:T(8,128)(2,1)S(1)}, u32[]{:S(2)}, u32[]{:S(2)}) %collective-permute-start.3) | collective-permute-done | bytes 139296 | tf_op jit(solution)/shard_map/ppermute | solution.py:100
  14.8 0.1 pad_maximum_fusion.xc
  15.0 0.1 broadcast_select_fusion.1
  15.1 0.1 collective-permute-start.4
  15.2 2.5 %collective-permute-start.5 = (bf16[544,256]{1,0:T(8,128)(2,1)S(1)}, bf16[544,256]{1,0:T(8,128)(2,1)S(1)}, u32[]{:S(2)}, u32[]{:S(2)}) collective-permute-start(bf16[544,256]{1,0:T(8,128)(2,1)S(1)} %get-tuple-element.20), channel_id=1, source_target_pairs={{8,16},{16,8},{0,0},{24,24},{9,17},{17,9},{1,1},{25,25},{10,18},{1... | collective-permute-start | bytes 835592 | tf_op jit(solution)/shard_map/ppermute | solution.py:31
  17.7 0.0 collective-permute-done.4.xn
  17.7 0.0 copy-done.1
  17.7 0.0 copy-done.2
  17.7 5.2 %near.1 = (bf16[2,4,32,256]{3,2,1,0:T(8,128)(2,1)S(1)}, bf16[2,6,32,768]{3,2,1,0:T(8,128)(2,1)S(1)}, f32[256,256]{1,0:T(8,128)S(1)}, bf16[3,3,3,256,256]{4,3,2,1...) custom-call(bf16[4,272,256]{2,1,0:T(8,128)(2,1)S(1)} %pad_maximum_fusion.xc, ...), custom_call_target="tpu_custom_call" | custom-call | flops 3623878656 | bytes 1048576 | tf_op jit(solution)/shard_map/near/pallas_call | solution.py:372
  23.0 0.1 collective-permute-done.5.xf
  23.1 2.8 %far.1 = bf16[2,4,32,256]{3,2,1,0:T(8,128)(2,1)S(1)} custom-call(bf16[4,272,256]{2,1,0:T(8,128)(2,1)S(1)} %pad_maximum_fusion.xc, bf16[544,256]{1,0:T(8,128)(2,1)S(1)} %collective-permute-done.5.xf, bf16[2,6,32,768]{3,2,1,0:T(8,128)(2,1)S(1)} %get-tuple-element.15.keep, f32[256,256]{1,0:T(8,128)S(1)} %get-tuple-element.16.part_sum, ...), custom_call_target="tpu_custom_call" | custom-call | flops 2264924160 | bytes 1048576 | tf_op jit(solution)/shard_map/far/pallas_call | solution.py:372
  26.0 0.1 constant_dynamic-slice_fusion
  26.1 0.0 copy-start.3
  26.1 1.3 %collective-permute-start.6 = (bf16[4,4,32,128]{3,2,1,0:T(8,128)(2,1)S(1)}, bf16[4,4,32,128]{3,2,1,0:T(8,128)(2,1)S(1)}, u32[]{:S(2)}, u32[]{:S(2)}) collective-permute-start(bf16[4,4,32,128]{3,2,1,0:T(8,128)(2,1)S(1)} %get-tuple-element.27), channel_id=1, source_target_pairs={{0,1},{1,0},{2,3},{3,2},{4,5},{5,4},{6,7},{7,6},{8,9},{9,8},{10,11... | collective-permute-start | bytes 393224 | tf_op jit(solution)/shard_map/ppermute | solution.py:57
  27.4 3.7 %collective-permute-done.6 = bf16[4,4,32,128]{3,2,1,0:T(8,128)(2,1)S(1)} collective-permute-done((bf16[4,4,32,128]{3,2,1,0:T(8,128)(2,1)S(1)}, bf16[4,4,32,128]{3,2,1,0:T(8,128)(2,1)S(1)}, u32[]{:S(2)}, u32[]{:S(2)}) %collective-permute-start.6) | collective-permute-done | bytes 131104 | tf_op jit(solution)/shard_map/ppermute | solution.py:57
  31.1 0.0 copy-done.3
  31.1 0.7 %constant_dynamic-update-slice_fusion = bf16[4,4,64,128]{3,2,1,0:T(8,128)(2,1)} fusion(bf16[4,4,64,128]{3,2,1,0:T(8,128)(2,1)} %copy-done.3, bf16[4,4,32,128]{3,2,1,0:T(8,128)(2,1)S(1)} %collective-permute-done.6, s32[]{:T(128)S(6)} %select_n.246), kind=kLoop, calls=%fused_computation.29 | loop fusion | bytes 262148 | tf_op jit(solution)/shard_map/dynamic_update_slice | solution.py:404
  (22 shorter events, 0.6 us)
Async XLA Ops:
  0.0 1.0 %copy-start = (bf16[4,4,64,128]{3,2,1,0:T(8,128)(2,1)S(1)}, bf16[4,4,64,128]{3,2,1,0:T(8,128)(2,1)}, u32[]{:S(2)}) copy-start(bf16[4,4,64,128]{3,2,1,0:T(8,128)(2,1)} %param.5) | copy-start | bytes 786436
  1.1 5.0 %collective-permute-start = (bf16[272,128]{1,0:T(8,128)(2,1)S(1)}, bf16[272,128]{1,0:T(8,128)(2,1)S(1)}, u32[]{:S(2)}, u32[]{:S(2)}) collective-permute-start(bf16[272,128]{1,0:T(8,128)(2,1)S(1)} %get-tuple-element.31), channel_id=1, source_target_pairs={{0,1},{1,0},{2,3},{3,2},{4,5},{5,4},{6,7},{7,6},{8,9},{9,8},{10,11... | collective-permute-start | bytes 208904 | tf_op jit(solution)/shard_map/ppermute | solution.py:96
  2.7 5.1 %collective-permute-start.2 = (bf16[272,128]{1,0:T(8,128)(2,1)S(1)}, bf16[272,128]{1,0:T(8,128)(2,1)S(1)}, u32[]{:S(2)}, u32[]{:S(2)}) collective-permute-start(bf16[272,128]{1,0:T(8,128)(2,1)S(1)} %get-tuple-element.32), channel_id=1, source_target_pairs={{0,1},{1,0},{2,3},{3,2},{4,5},{5,4},{6,7},{7,6},{8,9},{9,8},{10,11... | collective-permute-start | bytes 208904 | tf_op jit(solution)/shard_map/ppermute | solution.py:96
  4.6 13.2 %copy-start.1 = (f32[256]{0:T(256)S(1)}, f32[256]{0:T(256)}, u32[]{:S(2)}) copy-start(f32[256]{0:T(256)} %param.7) | copy-start | bytes 3076
  4.6 13.2 %copy-start.2 = (f32[256]{0:T(256)S(1)}, f32[256]{0:T(256)}, u32[]{:S(2)}) copy-start(f32[256]{0:T(256)} %param.9) | copy-start | bytes 3076
  6.2 5.1 %collective-permute-start.1 = (bf16[272,256]{1,0:T(8,128)(2,1)S(1)}, bf16[272,256]{1,0:T(8,128)(2,1)S(1)}, u32[]{:S(2)}, u32[]{:S(2)}) collective-permute-start(bf16[272,256]{1,0:T(8,128)(2,1)S(1)} %maximum_select_fusion.2), channel_id=1, source_target_pairs={{0,2},{4,6},{2,0},{6,4},{1,3},{5,7},{3,1},{7,5},{8,10},{12,14},{10... | collective-permute-start | bytes 417800 | tf_op jit(solution)/shard_map/ppermute | solution.py:99
  7.9 6.9 %collective-permute-start.3 = (bf16[272,256]{1,0:T(8,128)(2,1)S(1)}, bf16[272,256]{1,0:T(8,128)(2,1)S(1)}, u32[]{:S(2)}, u32[]{:S(2)}) collective-permute-start(bf16[272,256]{1,0:T(8,128)(2,1)S(1)} %maximum_select_fusion.3), channel_id=1, source_target_pairs={{2,4},{4,2},{0,0},{6,6},{3,5},{5,3},{1,1},{7,7},{10,12},{12,10},{8... | collective-permute-start | bytes 417800 | tf_op jit(solution)/shard_map/ppermute | solution.py:100
  15.1 2.6 %collective-permute-start.4 = (bf16[544,256]{1,0:T(8,128)(2,1)S(1)}, bf16[544,256]{1,0:T(8,128)(2,1)S(1)}, u32[]{:S(2)}, u32[]{:S(2)}) collective-permute-start(bf16[544,256]{1,0:T(8,128)(2,1)S(1)} %get-tuple-element.19), channel_id=1, source_target_pairs={{0,8},{16,24},{8,0},{24,16},{1,9},{17,25},{9,1},{25,17},{2,10},{18... | collective-permute-start | bytes 835592 | tf_op jit(solution)/shard_map/ppermute | solution.py:30
  15.2 7.9 %collective-permute-start.5 = (bf16[544,256]{1,0:T(8,128)(2,1)S(1)}, bf16[544,256]{1,0:T(8,128)(2,1)S(1)}, u32[]{:S(2)}, u32[]{:S(2)}) collective-permute-start(bf16[544,256]{1,0:T(8,128)(2,1)S(1)} %get-tuple-element.20), channel_id=1, source_target_pairs={{8,16},{16,8},{0,0},{24,24},{9,17},{17,9},{1,1},{25,25},{10,18},{1... | collective-permute-start | bytes 835592 | tf_op jit(solution)/shard_map/ppermute | solution.py:31
  26.1 5.0 %copy-start.3 = (bf16[4,4,64,128]{3,2,1,0:T(8,128)(2,1)}, bf16[4,4,64,128]{3,2,1,0:T(8,128)(2,1)S(1)}, u32[]{:S(2)}) copy-start(bf16[4,4,64,128]{3,2,1,0:T(8,128)(2,1)S(1)} %get-tuple-element.28) | copy-start | bytes 786436
  26.1 5.0 %collective-permute-start.6 = (bf16[4,4,32,128]{3,2,1,0:T(8,128)(2,1)S(1)}, bf16[4,4,32,128]{3,2,1,0:T(8,128)(2,1)S(1)}, u32[]{:S(2)}, u32[]{:S(2)}) collective-permute-start(bf16[4,4,32,128]{3,2,1,0:T(8,128)(2,1)S(1)} %get-tuple-element.27), channel_id=1, source_target_pairs={{0,1},{1,0},{2,3},{3,2},{4,5},{5,4},{6,7},{7,6},{8,9},{9,8},{10,11... | collective-permute-start | bytes 393224 | tf_op jit(solution)/shard_map/ppermute | solution.py:57
